TPU v7x, 32 devices: a whole 2x2x4 slice. The times are simulated.
32 devices in a mesh: dp: 8 (over z, y), tensor: 4 (over x, core).
Axes of the slice: x: 2, y: 2, z: 4, core: 2. Of those that a mesh axis runs over, the one named last changes fastest.
Arguments:
- states: bfloat16 [3072, 2048], P('dp'), may hold values from -6 to 6
- query_weight: bfloat16 [1, 2048, 1536], P(None, 'dp', 'tensor'), may hold values from -0.125 to 0.125
- keyvalue_matrix: bfloat16 [1, 2048, 768], P(None, 'dp'), may hold values from -0.125 to 0.125
- output_weight: bfloat16 [1, 2048, 1536], P(None, 'dp', 'tensor'), may hold values from -0.625 to 0.625
- gate_weight: bfloat16 [1, 2048, 4864], P(None, 'dp', 'tensor'), may hold values from -0.125 to 0.125
- up_weight: bfloat16 [1, 2048, 4864], P(None, 'dp', 'tensor'), may hold values from -0.125 to 0.125
- down_weight: bfloat16 [1, 2048, 4864], P(None, 'dp', 'tensor'), may hold values from -0.078125 to 0.078125
- norm_gains: bfloat16 [1, 2048, 2], P(None, 'dp'), may hold values from 0.099609375 to 1.8984375
- query_gain: float32 [1, 64], replicated, may hold values from 0.7 to 1.8
- key_gain: float32 [1, 64], replicated, may hold values from 0.7 to 1.8
- slot_sequence: int32 [24], replicated, may hold values from 0 to 1, as said below
- slot_offset: int32 [24], replicated, may hold values from 0 to 1408, as said below
- out_grad: bfloat16 [3072, 2048], P('dp'), may hold values from -6 to 6
Outputs:
- result: bfloat16 [3072, 2048], P('dp')
- states_grad: float32 [3072, 2048], P('dp')
- grad_query: float32 [1, 2048, 1536], P(None, 'dp', 'tensor')
- grad_keyvalue: float32 [1, 2048, 768], P(None, 'dp')
- grad_output: float32 [1, 2048, 1536], P(None, 'dp', 'tensor')
- grad_gate: float32 [1, 2048, 4864], P(None, 'dp', 'tensor')
- grad_up: float32 [1, 2048, 4864], P(None, 'dp', 'tensor')
- grad_down: float32 [1, 2048, 4864], P(None, 'dp', 'tensor')
- grad_norms: float32 [1, 2048, 2], P(None, 'dp')
- grad_querygain: float32 [1, 64], replicated
- grad_keygain: float32 [1, 64], replicated
Inputs may be any that keep to these rules, and one draw needn't show every extreme that they name: Slot s (on index s // 3 of dp) holds 128 tokens of sequence slot_sequence[s]; every sequence has 8 to 32 blocks, and one has exactly 12, no fewer than any other. `slot_offset`: the blocks of one sequence have the offsets 0, 128, 256, ... each once.
All inputs are finite; a program needn't handle non-finite values.
Results may differ from a plain program's by a relative error of at most 0.015.
The roundings to bfloat16 on the way count: a program that leaves them out, or rounds other values in their place, can miss the bound.
Values may be sent and summed in bfloat16 or wider, within the bound.
A program may use at most 192 MiB of HBM per device.

v0:
```python
import jax
import jax.numpy as jnp
from jax import lax
from jax.sharding import PartitionSpec as P

QUERY_HEADS = 24
KEYVALUE_HEADS = 6
HEAD_WIDTH = 64
LAYER_COUNT = 1
STRETCH = 128


EPSILON = 1e-06
NEGATIVE = -1e30
PRECISE = lax.Precision.HIGHEST


def normed(vector, gain_vector):
    return (
        vector
        * lax.rsqrt(jnp.mean(vector * vector, axis=-1, keepdims=True) + EPSILON)
        * gain_vector
    )


def angles(positions, head_size):
    frequency = 10000.0 ** (-jnp.arange(head_size // 2, dtype=jnp.float32) * 2.0 / head_size)
    phase_angle = positions.astype(jnp.float32)[:, None] * frequency[None, :]
    return (jnp.cos(phase_angle)[:, None, :], jnp.sin(phase_angle)[:, None, :])


def rotated(vector, cosines, sines):
    half_width = vector.shape[-1] // 2
    front = vector[..., :half_width]
    behind = vector[..., half_width:]
    return jnp.concatenate(
        [front * cosines - behind * sines, behind * cosines + front * sines], axis=-1
    )


def product(left_side, right_side):
    return jnp.dot(left_side, right_side, preferred_element_type=jnp.float32)


def by_rows(left_side, right_side):
    return lax.dot_general(
        left_side, right_side, (((0,), (0,)), ((), ())), preferred_element_type=jnp.float32
    )


def by_cols(left_side, right_side):
    return lax.dot_general(
        left_side, right_side, (((1,), (1,)), ((), ())), preferred_element_type=jnp.float32
    )


def local(
    states,
    query_weight,
    keyvalue_matrix,
    output_weight,
    gate_weight,
    up_weight,
    down_weight,
    norm_gains,
    query_gain,
    key_gain,
    slot_sequence,
    slot_offset,
    out_grad,
):
    token_rows = states.shape[0]
    dp_ranks = lax.axis_size("dp")
    tensor_ranks = lax.axis_size("tensor")
    heads_here = QUERY_HEADS // tensor_ranks
    head_width = heads_here * HEAD_WIDTH
    sharing_count = QUERY_HEADS // KEYVALUE_HEADS
    score_scale = HEAD_WIDTH ** (-0.5)
    slot_count = slot_sequence.shape[0]
    seq_all = jnp.repeat(slot_sequence, STRETCH)
    pos_all = jnp.repeat(slot_offset, STRETCH) + jnp.tile(
        jnp.arange(STRETCH, dtype=jnp.int32), slot_count
    )
    row_start = lax.axis_index("dp") * token_rows
    seq_here = lax.dynamic_slice_in_dim(seq_all, row_start, token_rows)
    pos_here = lax.dynamic_slice_in_dim(pos_all, row_start, token_rows)
    cosines, sines = angles(pos_here, HEAD_WIDTH)
    wanted = (
        lax.axis_index("tensor") * heads_here + jnp.arange(heads_here, dtype=jnp.int32)
    ) // sharing_count
    keyvalue_index = jnp.arange(KEYVALUE_HEADS, dtype=jnp.int32)
    select = (wanted[:, None] == keyvalue_index[None, :]).astype(jnp.float32)
    send_width = heads_here * HEAD_WIDTH

    def query_side(query_lin, gain_vector):
        return rotated(
            normed(query_lin.reshape(token_rows, heads_here, HEAD_WIDTH), gain_vector),
            cosines,
            sines,
        )

    def key_side(keyvalue_linear, gain_vector):
        key_head_rows = keyvalue_linear[:, : KEYVALUE_HEADS * HEAD_WIDTH].reshape(
            token_rows, KEYVALUE_HEADS, HEAD_WIDTH
        )
        value_head_rows = keyvalue_linear[:, KEYVALUE_HEADS * HEAD_WIDTH :].reshape(
            token_rows, KEYVALUE_HEADS, HEAD_WIDTH
        )
        key_head_rows = rotated(normed(key_head_rows, gain_vector), cosines, sines)
        spread_keys = jnp.einsum("tjd,ij->tid", key_head_rows, select, precision=PRECISE)
        spread_values = jnp.einsum("tjd,ij->tid", value_head_rows, select, precision=PRECISE)
        return jnp.concatenate(
            [
                spread_keys.reshape(token_rows, send_width),
                spread_values.reshape(token_rows, send_width),
            ],
            axis=1,
        )

    def key_block(piece, block_index):
        block = lax.dynamic_slice_in_dim(piece, block_index * token_rows, token_rows, 0)
        block_start = block_index * token_rows
        seq_keys = lax.dynamic_slice_in_dim(seq_all, block_start, token_rows)
        pos_keys = lax.dynamic_slice_in_dim(pos_all, block_start, token_rows)
        visible = (seq_keys[None, :] == seq_here[:, None]) & (
            pos_keys[None, :] <= pos_here[:, None]
        )
        key_head_rows = block[:, :send_width].reshape(token_rows, heads_here, HEAD_WIDTH)
        value_head_rows = block[:, send_width:].reshape(token_rows, heads_here, HEAD_WIDTH)
        return (key_head_rows, value_head_rows, visible, block_start)

    def narrowed(grads_heads):
        return grads_heads.reshape(token_rows, send_width)

    def branch_total(partial_value):
        return lax.psum(partial_value, "tensor")

    def input_total(partial_value):
        return lax.psum(partial_value, "tensor")

    hidden_state = states.astype(jnp.float32)
    layer_index = 0
    gathered = (
        lax.all_gather(query_weight[layer_index], "dp", axis=0, tiled=True),
        lax.all_gather(keyvalue_matrix[layer_index], "dp", axis=0, tiled=True),
        lax.all_gather(output_weight[layer_index], "dp", axis=0, tiled=True),
        lax.all_gather(gate_weight[layer_index], "dp", axis=0, tiled=True),
        lax.all_gather(up_weight[layer_index], "dp", axis=0, tiled=True),
        lax.all_gather(down_weight[layer_index], "dp", axis=0, tiled=True),
        lax.all_gather(norm_gains[layer_index], "dp", axis=0, tiled=True),
    )
    w_query, w_keyvalue, w_output, w_gate, w_up, w_down, norm_scale = gathered
    norm_scale = norm_scale.astype(jnp.float32)
    query_g = query_gain[layer_index]
    key_g = key_gain[layer_index]
    attn_in = normed(hidden_state, norm_scale[:, 0]).astype(jnp.bfloat16)
    query_lin = product(attn_in, w_query)
    queries = query_side(query_lin, query_g).astype(jnp.bfloat16)
    keyvalue_linear = product(attn_in, w_keyvalue)
    keyvalue_send = key_side(keyvalue_linear, key_g).astype(jnp.bfloat16)

    def forward_fold(running, piece, piece_start, queries=queries):

        def forward_fold_step(running, block_index):
            key_head_rows, value_head_rows, visible, block_start = key_block(piece, block_index)

            def forward_attend_block(running):
                top_score, weight_sum, weighted = running
                scores = (
                    jnp.einsum(
                        "qhd,khd->hqk", queries, key_head_rows, preferred_element_type=jnp.float32
                    )
                    * score_scale
                )
                scores = jnp.where(visible[None], scores, NEGATIVE)
                new_top = jnp.maximum(top_score, jnp.max(scores, axis=-1))
                weights = jnp.where(visible[None], jnp.exp(scores - new_top[:, :, None]), 0.0)
                factor = jnp.exp(top_score - new_top)
                weight_sum = weight_sum * factor + jnp.sum(weights, axis=-1)
                weighted = weighted * factor.T[:, :, None] + jnp.einsum(
                    "hqk,khd->qhd", weights, value_head_rows.astype(jnp.float32)
                )
                return (new_top, weight_sum, weighted)

            return (
                lax.cond(
                    jnp.any(visible), forward_attend_block, lambda state_in: state_in, running
                ),
                None,
            )

        running, _ = lax.scan(
            forward_fold_step, running, jnp.arange(piece.shape[0] // token_rows, dtype=jnp.int32)
        )
        return running

    initial = (
        jnp.full((heads_here, token_rows), NEGATIVE, jnp.float32),
        jnp.zeros((heads_here, token_rows), jnp.float32),
        jnp.zeros((token_rows, heads_here, HEAD_WIDTH), jnp.float32),
    )
    top_score, weight_sum, weighted = forward_fold(
        initial, lax.all_gather(keyvalue_send, "dp", axis=0, tiled=True), jnp.int32(0)
    )
    attended = weighted / weight_sum.T[:, :, None]
    log_total = top_score + jnp.log(weight_sum)
    attn_out = attended.reshape(token_rows, head_width).astype(jnp.bfloat16)
    middle = hidden_state + branch_total(by_cols(attn_out, w_output))
    ffn_in = normed(middle, norm_scale[:, 1]).astype(jnp.bfloat16)
    gate_pre = product(ffn_in, w_gate)
    up_pre = product(ffn_in, w_up)
    mixed = (jax.nn.silu(gate_pre) * up_pre).astype(jnp.bfloat16)
    kept_weights = None
    saved = [
        (
            kept_weights,
            hidden_state,
            attn_in,
            query_lin,
            queries,
            keyvalue_linear,
            keyvalue_send,
            attended,
            log_total,
            attn_out,
            middle,
            ffn_in,
            gate_pre,
            up_pre,
            mixed,
        )
    ]
    hidden_state = middle + branch_total(by_cols(mixed, w_down))
    result = hidden_state.astype(jnp.bfloat16)
    residual_grad = out_grad.astype(jnp.float32)
    grad_lists = [[] for slot_index in range(7)]
    querygain_list = []
    keygain_list = []
    for layer_index in reversed(range(LAYER_COUNT)):
        (
            kept_weights,
            layer_input,
            attn_in,
            query_lin,
            queries,
            keyvalue_linear,
            keyvalue_send,
            attended,
            log_total,
            attn_out,
            middle,
            ffn_in,
            gate_pre,
            up_pre,
            mixed,
        ) = saved[layer_index]
        gathered = (
            lax.all_gather(query_weight[layer_index], "dp", axis=0, tiled=True),
            lax.all_gather(keyvalue_matrix[layer_index], "dp", axis=0, tiled=True),
            lax.all_gather(output_weight[layer_index], "dp", axis=0, tiled=True),
            lax.all_gather(gate_weight[layer_index], "dp", axis=0, tiled=True),
            lax.all_gather(up_weight[layer_index], "dp", axis=0, tiled=True),
            lax.all_gather(down_weight[layer_index], "dp", axis=0, tiled=True),
            lax.all_gather(norm_gains[layer_index], "dp", axis=0, tiled=True),
        )
        w_query, w_keyvalue, w_output, w_gate, w_up, w_down, norm_scale = gathered
        norm_scale = norm_scale.astype(jnp.float32)
        query_g = query_gain[layer_index]
        key_g = key_gain[layer_index]
        down_grad = residual_grad.astype(jnp.bfloat16)
        d_mixed = product(down_grad, w_down)
        d_wdown = by_rows(down_grad, mixed)
        sigmoid_gate = jax.nn.sigmoid(gate_pre)
        d_gate = (d_mixed * up_pre * sigmoid_gate * (1.0 + gate_pre * (1.0 - sigmoid_gate))).astype(
            jnp.bfloat16
        )
        d_up = (d_mixed * gate_pre * sigmoid_gate).astype(jnp.bfloat16)
        d_wgate = by_rows(ffn_in, d_gate)
        d_wup = by_rows(ffn_in, d_up)
        d_ffn_in = input_total(by_cols(d_gate, w_gate) + by_cols(d_up, w_up))
        _, norm_pull = jax.vjp(normed, middle, norm_scale[:, 1])
        d_middle_norm, d_gain_ffn = norm_pull(d_ffn_in)
        grad_middle = residual_grad + d_middle_norm
        output_grad = grad_middle.astype(jnp.bfloat16)
        d_wout = by_rows(output_grad, attn_out)
        d_heads = (
            product(output_grad, w_output)
            .astype(jnp.bfloat16)
            .reshape(token_rows, heads_here, HEAD_WIDTH)
        )
        delta = jnp.sum(d_heads.astype(jnp.float32) * attended, axis=-1).T

        def backward_fold(
            running,
            piece,
            piece_start,
            queries=queries,
            log_total=log_total,
            d_heads=d_heads,
            delta=delta,
        ):

            def backward_fold_step(running, block_index):
                key_head_rows, value_head_rows, visible, block_start = key_block(piece, block_index)

                def backward_attend_block(running):
                    d_query, d_keyvalue = running
                    scores = (
                        jnp.einsum(
                            "qhd,khd->hqk",
                            queries,
                            key_head_rows,
                            preferred_element_type=jnp.float32,
                        )
                        * score_scale
                    )
                    weights = jnp.where(visible[None], jnp.exp(scores - log_total[:, :, None]), 0.0)
                    d_weights = jnp.einsum(
                        "qhd,khd->hqk", d_heads, value_head_rows, preferred_element_type=jnp.float32
                    )
                    d_scores = (weights * (d_weights - delta[:, :, None])).astype(jnp.bfloat16)
                    d_query = (
                        d_query
                        + jnp.einsum(
                            "hqk,khd->qhd",
                            d_scores,
                            key_head_rows,
                            preferred_element_type=jnp.float32,
                        )
                        * score_scale
                    )
                    d_keys = (
                        jnp.einsum(
                            "hqk,qhd->khd", d_scores, queries, preferred_element_type=jnp.float32
                        )
                        * score_scale
                    )
                    d_values = jnp.einsum("hqk,qhd->khd", weights, d_heads.astype(jnp.float32))
                    before_add = lax.dynamic_slice_in_dim(d_keyvalue, block_start, token_rows, 0)
                    after_add = before_add + jnp.concatenate(
                        [narrowed(d_keys), narrowed(d_values)], axis=1
                    )
                    return (
                        d_query,
                        lax.dynamic_update_slice_in_dim(d_keyvalue, after_add, block_start, 0),
                    )

                return (
                    lax.cond(
                        jnp.any(visible), backward_attend_block, lambda state_in: state_in, running
                    ),
                    None,
                )

            running, _ = lax.scan(
                backward_fold_step,
                running,
                jnp.arange(piece.shape[0] // token_rows, dtype=jnp.int32),
            )
            return running

        initial = (
            jnp.zeros((token_rows, heads_here, HEAD_WIDTH), jnp.float32),
            jnp.zeros((token_rows * dp_ranks, 2 * send_width), jnp.float32),
        )
        d_query, d_keyvalue = backward_fold(
            initial, lax.all_gather(keyvalue_send, "dp", axis=0, tiled=True), jnp.int32(0)
        )
        d_keyvalue_here = lax.psum_scatter(d_keyvalue, "dp", scatter_dimension=0, tiled=True)
        _, query_pull = jax.vjp(query_side, query_lin, query_g)
        d_query_lin, d_querygain = query_pull(d_query)
        _, key_pull = jax.vjp(key_side, keyvalue_linear, key_g)
        d_keyvalue_lin, d_keygain = key_pull(d_keyvalue_here)
        d_query_lin = d_query_lin.astype(jnp.bfloat16)
        d_keyvalue_lin = d_keyvalue_lin.astype(jnp.bfloat16)
        d_wquery = by_rows(attn_in, d_query_lin)
        d_wkeyvalue = by_rows(attn_in, d_keyvalue_lin)
        d_attn_in = input_total(by_cols(d_query_lin, w_query) + by_cols(d_keyvalue_lin, w_keyvalue))
        _, norm_pull = jax.vjp(normed, layer_input, norm_scale[:, 0])
        d_input_norm, d_gain_attn = norm_pull(d_attn_in)
        residual_grad = grad_middle + d_input_norm
        d_gains = jnp.stack([d_gain_attn, d_gain_ffn], axis=1)
        d_wkeyvalue = lax.psum(d_wkeyvalue, "tensor")
        shares = list(
            (
                lax.psum_scatter(d_wquery, "dp", scatter_dimension=0, tiled=True),
                lax.psum_scatter(d_wkeyvalue, "dp", scatter_dimension=0, tiled=True),
                lax.psum_scatter(d_wout, "dp", scatter_dimension=0, tiled=True),
                lax.psum_scatter(d_wgate, "dp", scatter_dimension=0, tiled=True),
                lax.psum_scatter(d_wup, "dp", scatter_dimension=0, tiled=True),
                lax.psum_scatter(d_wdown, "dp", scatter_dimension=0, tiled=True),
                lax.psum_scatter(d_gains, "dp", scatter_dimension=0, tiled=True),
            )
        )
        for slot_index in range(7):
            grad_lists[slot_index].append(shares[slot_index])
        querygain_list.append(d_querygain)
        keygain_list.append(d_keygain)
    stacked = [jnp.stack(entries[::-1], axis=0) for entries in grad_lists]
    querygain_sum, keygain_sum = lax.psum(
        (jnp.stack(querygain_list[::-1], axis=0), jnp.stack(keygain_list[::-1], axis=0)),
        ("dp", "tensor"),
    )
    return (
        result,
        residual_grad,
        stacked[0],
        stacked[1],
        stacked[2],
        stacked[3],
        stacked[4],
        stacked[5],
        stacked[6],
        querygain_sum,
        keygain_sum,
    )


def solution(mesh):
    return jax.shard_map(
        local,
        mesh=mesh,
        in_specs=(
            P("dp", None),
            P(None, "dp", "tensor"),
            P(None, "dp", None),
            P(None, "dp", "tensor"),
            P(None, "dp", "tensor"),
            P(None, "dp", "tensor"),
            P(None, "dp", "tensor"),
            P(None, "dp", None),
            P(),
            P(),
            P(),
            P(),
            P("dp", None),
        ),
        out_specs=(
            P("dp", None),
            P("dp", None),
            P(None, "dp", "tensor"),
            P(None, "dp", None),
            P(None, "dp", "tensor"),
            P(None, "dp", "tensor"),
            P(None, "dp", "tensor"),
            P(None, "dp", "tensor"),
            P(None, "dp", None),
            P(),
            P(),
        ),
        check_vma=False,
    )
```

profile of v0, /device:TPU:0, one launch (start us, length us, event | category | flops | bytes accessed | tf_op | source)
XLA Modules:
  0.0 2026.4 jit_solution(17399523420014513180)
XLA Ops:
  8.7 22.5 %all-gather = bf16[1,2048,2]{1,2,0:T(2,128)(2,1)S(1)} all-gather(bf16[1,256,2]{1,2,0:T(2,128)(2,1)} %param.28), channel_id=2, replica_groups=mesh['dp'=8,'tensor'=4] {'dp'}, dimensions={1}, use_global_device_ids=true | all-gather | bytes 9216 | tf_op jit(solution)/shard_map/all_gather | solution.py:150
  35.6 21.2 %all-gather.19.cloned.1.call-done = bf16[1,2048,384]{2,1,0:T(8,128)(2,1)} async-done(((bf16[1,256,384]{2,1,0:T(8,128)(2,1)}), bf16[1,2048,384]{2,1,0:T(8,128)(2,1)}) %all-gather.19.cloned.1.call-update) | async-done | bytes 1572880 | tf_op jit(solution)/shard_map/all_gather | solution.py:144
  59.9 58.4 %all-gather.17.cloned.1.call-done = bf16[1,2048,768]{2,1,0:T(8,128)(2,1)} async-done(((bf16[1,256,768]{2,1,0:T(8,128)(2,1)}), bf16[1,2048,768]{2,1,0:T(8,128)(2,1)}) %all-gather.17.cloned.1.call-update) | async-done | bytes 3145744 | tf_op jit(solution)/shard_map/all_gather | solution.py:145
  130.6 77.0 %all-gather.15.cloned.1.call-done = bf16[3072,768]{0,1:T(8,128)(2,1)} async-done(((bf16[384,768]{0,1:T(8,128)(2,1)}), bf16[3072,768]{0,1:T(8,128)(2,1)}) %all-gather.15.cloned.1.call-update) | async-done | bytes 4718608 | tf_op jit(solution)/shard_map/all_gather | solution.py:203
  207.7 68.9 %while.26 = (s32[]{:T(128)}, f32[6,384]{1,0:T(8,128)S(1)}, f32[6,384]{1,0:T(8,128)S(1)}, f32[384,6,64]{0,2,1:T(8,128)S(1)}, s32[8]{0:T(128)S(1)}, /*index=5*/s32...) while((s32[]{:T(128)}, f32[6,384]{1,0:T(8,128)S(1)}, ...), condition=%wide.region_9.10_spmd, body=%wide.region_3.9_spmd.sunk | while | flops 238000896 | bytes 14610785 | solution.py:192
  283.7 53.1 %all-gather.27.cloned.1.call-done = bf16[1,2048,1216]{1,2,0:T(8,128)(2,1)} async-done(((bf16[1,256,1216]{1,2,0:T(8,128)(2,1)}), bf16[1,2048,1216]{1,2,0:T(8,128)(2,1)}) %all-gather.27.cloned.1.call-update) | async-done | bytes 4980752 | tf_op jit(solution)/shard_map/all_gather | solution.py:149
  343.3 62.9 %all-reduce.12.cloned.1.call-done = f32[384,2048]{1,0:T(8,128)} async-done(((f32[384,2048]{1,0:T(8,128)}), f32[384,2048]{1,0:T(8,128)}) %all-reduce.12.cloned.1.call-update) | async-done | bytes 3145744 | tf_op jit(solution)/shard_map/psum | solution.py:136
  410.7 81.8 %all-gather.25.cloned.1.call-done = bf16[1,2048,1216]{1,2,0:T(8,128)(2,1)} async-done(((bf16[1,256,1216]{1,2,0:T(8,128)(2,1)}), bf16[1,2048,1216]{1,2,0:T(8,128)(2,1)}) %all-gather.25.cloned.1.call-update) | async-done | bytes 4980752 | tf_op jit(solution)/shard_map/all_gather | solution.py:148
  499.0 77.8 %all-gather.23.cloned.1.call-done = bf16[1,2048,1216]{1,2,0:T(8,128)(2,1)} async-done(((bf16[1,256,1216]{1,2,0:T(8,128)(2,1)}), bf16[1,2048,1216]{1,2,0:T(8,128)(2,1)}) %all-gather.23.cloned.1.call-update) | async-done | bytes 4980752 | tf_op jit(solution)/shard_map/all_gather | solution.py:147
  592.9 66.1 %all-reduce.14.cloned.1.call-done = f32[384,2048]{1,0:T(8,128)} async-done(((f32[384,2048]{1,0:T(8,128)}), f32[384,2048]{1,0:T(8,128)}) %all-reduce.14.cloned.1.call-update) | async-done | bytes 3145744 | tf_op jit(solution)/shard_map/psum | solution.py:139
  672.9 172.2 %while.27 = (s32[]{:T(128)}, f32[384,6,64]{0,2,1:T(8,128)}, f32[3072,768]{0,1:T(8,128)}, s32[8]{0:T(128)S(1)}, s32[3072]{0:T(1024)}, /*index=5*/s32[384]{0:T(512...) while((s32[]{:T(128)}, f32[384,6,64]{0,2,1:T(8,128)}, ...), condition=%wide.region_20.21_spmd, body=%wide.region_16.20_spmd.sunk | while | flops 575815680 | bytes 27909536 | solution.py:355
  742.0 17.6 conditional.5
  763.7 17.5 conditional.5
  785.3 17.6 conditional.5
  807.0 17.5 conditional.5
  846.9 160.9 %reduce-scatter.11.cloned.1.call-done = f32[384,768]{0,1:T(8,128)} async-done(((f32[3072,768]{0,1:T(8,128)}), f32[384,768]{0,1:T(8,128)}) %reduce-scatter.11.cloned.1.call-update) | async-done | bytes 1179664 | tf_op jit(solution)/shard_map/reduce_scatter | solution.py:369
  1031.5 103.9 %reduce-scatter.23.cloned.1.call-done = f32[256,768]{1,0:T(8,128)} async-done(((f32[2048,768]{1,0:T(8,128)}), f32[256,768]{1,0:T(8,128)}) %reduce-scatter.23.cloned.1.call-update) | async-done | bytes 786448 | tf_op jit(solution)/shard_map/reduce_scatter | solution.py:387
  1135.7 134.0 %all-reduce.16.cloned.1.call-done = (f32[384,2048]{1,0:T(8,128)}, f32[384,2048]{1,0:T(8,128)}, f32[256,768]{1,0:T(8,128)}) async-done(((f32[384,2048]{1,0:T(8,128)}, f32[384,2048]{1,0:T(8,128)}, f32[256,768]{1,0:T(8,128)}), (f32[384,2048]{1,0:T(8,128)}, f32[384,2048]{1,0:T(8,128)}, f32[256,768]{1,0:T(8,128)})) %all-reduce.16.cloned.1.call-update) | async-done | bytes 7077904 | tf_op jit(solution)/shard_map/psum | solution.py:136
  1303.0 39.7 %all-reduce.6 = (f32[1,64]{1,0:T(1,128)}, f32[1,64]{1,0:T(1,128)}) all-reduce(f32[1,64]{1,0:T(1,128)S(1)} %bitcast.225, f32[1,64]{1,0:T(1,128)S(1)} %bitcast.224), channel_id=1, replica_groups=mesh['dp'=8,'tensor'=4] {'dp','tensor'}, use_global_device_ids=true, to_apply=%region_37.38 | all-reduce | flops 128 | bytes 1024 | tf_op jit(solution)/shard_map/psum | solution.py:400
  1352.0 63.8 %reduce-scatter.15.cloned.1.call-done = f32[256,384]{1,0:T(8,128)} async-done(((f32[2048,384]{1,0:T(8,128)}), f32[256,384]{1,0:T(8,128)}) %reduce-scatter.15.cloned.1.call-update) | async-done | bytes 393232 | tf_op jit(solution)/shard_map/reduce_scatter | solution.py:388
  1415.8 174.8 %reduce-scatter.21.cloned.1.call-done = f32[256,1216]{0,1:T(8,128)} async-done(((f32[2048,1216]{0,1:T(8,128)}), f32[256,1216]{0,1:T(8,128)}) %reduce-scatter.21.cloned.1.call-update) | async-done | bytes 1245200 | tf_op jit(solution)/shard_map/reduce_scatter | solution.py:391
  1590.6 174.8 %reduce-scatter.17.cloned.1.call-done = f32[256,1216]{0,1:T(8,128)} async-done(((f32[2048,1216]{0,1:T(8,128)}), f32[256,1216]{0,1:T(8,128)}) %reduce-scatter.17.cloned.1.call-update) | async-done | bytes 1245200 | tf_op jit(solution)/shard_map/reduce_scatter | solution.py:389
  1765.4 174.8 %reduce-scatter.19.cloned.1.call-done = f32[256,1216]{0,1:T(8,128)} async-done(((f32[2048,1216]{0,1:T(8,128)}), f32[256,1216]{0,1:T(8,128)}) %reduce-scatter.19.cloned.1.call-update) | async-done | bytes 1245200 | tf_op jit(solution)/shard_map/reduce_scatter | solution.py:390
  1940.2 78.0 %reduce-scatter.13.cloned.1.call-done = f32[256,384]{1,0:T(8,128)} async-done(((f32[2048,384]{1,0:T(8,128)}), f32[256,384]{1,0:T(8,128)}) %reduce-scatter.13.cloned.1.call-update) | async-done | bytes 393232 | tf_op jit(solution)/shard_map/reduce_scatter | solution.py:386
  (419 shorter events, 468.0 us)
Async XLA Ops:
  7.2 49.6 %all-gather.19.cloned.1.call-start = ((), (), s32[]{:S(2)}) async-start(), calls=%async_computation.18 | async-start | bytes 1769472 | tf_op jit(solution)/shard_map/all_gather | solution.py:144
  7.9 110.3 %all-gather.17.cloned.1.call-start = ((), (), s32[]{:S(2)}) async-start(), calls=%async_computation.17 | async-start | bytes 3538944 | tf_op jit(solution)/shard_map/all_gather | solution.py:145
  8.7 198.9 %all-gather.15.cloned.1.call-start = ((), (), s32[]{:S(2)}) async-start(), calls=%async_computation.8 | async-start | bytes 5308416 | tf_op jit(solution)/shard_map/all_gather | solution.py:203
  127.8 148.9 %all-gather.21.cloned.1.call-start = ((), (), s32[]{:S(2)}) async-start(), calls=%async_computation.19 | async-start | bytes 1769472 | tf_op jit(solution)/shard_map/all_gather | solution.py:146
  128.4 208.4 %all-gather.27.cloned.1.call-start = ((), (), s32[]{:S(2)}) async-start(), calls=%async_computation.22 | async-start | bytes 5603328 | tf_op jit(solution)/shard_map/all_gather | solution.py:149
  129.0 277.3 %all-reduce.12.cloned.1.call-start = ((), (), s32[]{:S(2)}) async-start(), calls=%async_computation.9 | async-start | bytes 6291456 | tf_op jit(solution)/shard_map/psum | solution.py:136
  281.7 210.8 %all-gather.25.cloned.1.call-start = ((), (), s32[]{:S(2)}) async-start(), calls=%async_computation.21 | async-start | bytes 5603328 | tf_op jit(solution)/shard_map/all_gather | solution.py:148
  282.4 294.3 %all-gather.23.cloned.1.call-start = ((), (), s32[]{:S(2)}) async-start(), calls=%async_computation.20 | async-start | bytes 5603328 | tf_op jit(solution)/shard_map/all_gather | solution.py:147
  283.2 375.8 %all-reduce.14.cloned.1.call-start = ((), (), s32[]{:S(2)}) async-start(), calls=%async_computation.10 | async-start | bytes 6291456 | tf_op jit(solution)/shard_map/psum | solution.py:139
  410.7 166.1 %copy-start.9 = (bf16[384,2048]{1,0:T(8,128)(2,1)}, bf16[384,2048]{1,0:T(8,128)(2,1)S(1)}, u32[]{:S(2)}) copy-start(bf16[384,2048]{1,0:T(8,128)(2,1)S(1)} %multiply_convert_fusion) | copy-start | bytes 4718596
  592.2 415.6 %reduce-scatter.11.cloned.1.call-start = ((), (), s32[]{:S(2)}) async-start(), calls=%async_computation.11 | async-start | bytes 10616832 | tf_op jit(solution)/shard_map/reduce_scatter | solution.py:369
  845.2 164.0 %copy-start.45 = (s32[6]{0:T(128)S(1)}, s32[6]{0:T(128)}, u32[]{:S(2)}) copy-start(s32[6]{0:T(128)} %copy-done.44) | copy-start | bytes 76
  845.2 290.2 %reduce-scatter.23.cloned.1.call-start = ((), (), s32[]{:S(2)}) async-start(), calls=%async_computation.23 | async-start | bytes 7077888 | tf_op jit(solution)/shard_map/reduce_scatter | solution.py:387
  846.9 164.0 %copy-start.34 = (f32[384,32]{0,1:T(8,128)S(1)}, f32[384,32]{0,1:T(8,128)}, u32[]{:S(2)}) copy-start(f32[384,32]{0,1:T(8,128)} %copy-done.33) | copy-start | bytes 147460
  846.9 164.0 %copy-start.36 = (f32[384,32]{0,1:T(8,128)S(1)}, f32[384,32]{0,1:T(8,128)}, u32[]{:S(2)}) copy-start(f32[384,32]{0,1:T(8,128)} %copy-done.35) | copy-start | bytes 147460
  1018.1 251.6 %all-reduce.16.cloned.1.call-start = ((), (), s32[]{:S(2)}) async-start(), calls=%async_computation.25 | async-start | bytes 14155776 | tf_op jit(solution)/shard_map/psum | solution.py:136
  1135.4 215.1 %reduce-scatter.25.cloned.1.call-start = ((), (), s32[]{:S(2)}) async-start(), calls=%async_computation.24 | async-start | bytes 1179648
  1274.0 141.8 %reduce-scatter.15.cloned.1.call-start = ((), (), s32[]{:S(2)}) async-start(), calls=%async_computation.13 | async-start | bytes 3538944 | tf_op jit(solution)/shard_map/reduce_scatter | solution.py:388
  1278.8 311.8 %reduce-scatter.21.cloned.1.call-start = ((), (), s32[]{:S(2)}) async-start(), calls=%async_computation.16 | async-start | bytes 11206656 | tf_op jit(solution)/shard_map/reduce_scatter | solution.py:391
  1285.6 479.8 %reduce-scatter.17.cloned.1.call-start = ((), (), s32[]{:S(2)}) async-start(), calls=%async_computation.14 | async-start | bytes 11206656 | tf_op jit(solution)/shard_map/reduce_scatter | solution.py:389
  1293.5 646.7 %reduce-scatter.19.cloned.1.call-start = ((), (), s32[]{:S(2)}) async-start(), calls=%async_computation.15 | async-start | bytes 11206656 | tf_op jit(solution)/shard_map/reduce_scatter | solution.py:390
  1300.0 718.3 %reduce-scatter.13.cloned.1.call-start = ((), (), s32[]{:S(2)}) async-start(), calls=%async_computation.12 | async-start | bytes 3538944 | tf_op jit(solution)/shard_map/reduce_scatter | solution.py:386
  1348.0 670.3 %copy-start.32 = (f32[256,768]{1,0:T(8,128)S(1)}, f32[256,768]{1,0:T(8,128)}, u32[]{:S(2)}) copy-start(f32[256,768]{1,0:T(8,128)} %get-tuple-element.389) | copy-start | bytes 2359300
  1348.0 671.2 %copy-start.1 = (s32[24]{0:T(128)S(1)}, s32[24]{0:T(128)}, u32[]{:S(2)}) copy-start(s32[24]{0:T(128)} %param.31) | copy-start | bytes 292
  (45 other events, 1059.0 us)
Sparse Core Ops, SparseCore 0:
  10.2 46.5 all-gather.18
  59.0 59.2 all-gather.16
  127.9 79.6 all-gather.14
  209.7 42.6 all-gather.20
  254.3 82.4 all-gather.26
  339.6 66.5 all-reduce.11
  408.3 84.1 all-gather.24
  494.5 82.2 all-gather.22
  592.3 66.5 all-reduce.13
  845.3 162.4 reduce-scatter.10
  1018.3 117.0 reduce-scatter.22
  1137.8 131.8 all-reduce.15
  1274.2 63.8 reduce-scatter.24
  1342.4 73.3 reduce-scatter.14
  1420.3 170.2 reduce-scatter.20
  1595.2 170.2 reduce-scatter.16
  1770.0 170.2 reduce-scatter.18
  1944.7 73.5 reduce-scatter.12
where the time goes:
time: 2040 us; the launch traced here: 2030 us
  waiting for transfers between devices  1570 us (77%)
  matrix products  159 us (8%)
  local copies, waits for them, and re-layouts  136 us (7%)
  other arithmetic  63.2 us (3%)
  blocking collectives  62.2 us (3%)
  loops' own time  21 us (1%)
    psum x2, waiting for transfers between devices, branch_total(): return lax.psum(partial_value, 'tensor')  197 us
    reduce_scatter x1, waiting for transfers between devices, local(): lax.psum_scatter(d_wgate, 'dp', scatter_dimension=0, tiled=True)  175 us
    reduce_scatter x1, waiting for transfers between devices, local(): lax.psum_scatter(d_wdown, 'dp', scatter_dimension=0, tiled=True)  175 us
    reduce_scatter x1, waiting for transfers between devices, local(): lax.psum_scatter(d_wup, 'dp', scatter_dimension=0, tiled=True)  175 us
    reduce_scatter x1, waiting for transfers between devices, local(): lax.psum_scatter(d_keyvalue, 'dp', scatter_dimension=0, tiled=True)  161 us
    reduce_scatter x1, waiting for transfers between devices, local(): lax.psum_scatter(d_wkeyvalue, 'dp', scatter_dimension=0, tiled=True)  104 us
    all_gather x1, waiting for transfers between devices, local(): lax.all_gather(up_weight[layer_index], 'dp', axis=0, tiled=True)  81.8 us
    reduce_scatter x1, waiting for transfers between devices, local(): lax.psum_scatter(d_wquery, 'dp', scatter_dimension=0, tiled=True)  78 us
  transfers between devices with their start and end apart: 18, of which 16 were waited for; matrix products, arithmetic and copies ran while one was open for 7% of the time, Pallas kernels for 0%

commit v1 on v0

v1 whole, which is shorter than its diff:
```python
import functools

import jax
import jax.numpy as jnp
from jax import lax
from jax.experimental import pallas as pl
from jax.experimental.pallas import tpu as pltpu
from jax.sharding import PartitionSpec as P

QUERY_HEADS = 24
KEYVALUE_HEADS = 6
HEAD_WIDTH = 64
STRETCH = 128
EPSILON = 1e-06
PLANES = 4
PAIRS = 3
LOG2E = 1.4426950408889634
BF16 = jnp.bfloat16
F32 = jnp.float32


def product(left_side, right_side):
    return jnp.dot(left_side, right_side, preferred_element_type=F32)


def by_rows(left_side, right_side):
    return lax.dot_general(
        left_side, right_side, (((0,), (0,)), ((), ())), preferred_element_type=F32
    )


def by_cols(left_side, right_side):
    return lax.dot_general(
        left_side, right_side, (((1,), (1,)), ((), ())), preferred_element_type=F32
    )


def normed(vector, gain_vector):
    return (
        vector
        * lax.rsqrt(jnp.mean(vector * vector, axis=-1, keepdims=True) + EPSILON)
        * gain_vector
    )


def angles(positions, head_size):
    frequency = 10000.0 ** (-jnp.arange(head_size // 2, dtype=F32) * 2.0 / head_size)
    phase_angle = positions.astype(F32)[:, None] * frequency[None, :]
    return (jnp.cos(phase_angle)[:, None, :], jnp.sin(phase_angle)[:, None, :])


def rotated(vector, cosines, sines):
    half_width = vector.shape[-1] // 2
    front = vector[..., :half_width]
    behind = vector[..., half_width:]
    return jnp.concatenate(
        [front * cosines - behind * sines, behind * cosines + front * sines], axis=-1
    )


def visible_mask(shape, key_axis):
    keys = lax.broadcasted_iota(jnp.int32, shape, key_axis)
    queries = lax.rem(lax.broadcasted_iota(jnp.int32, shape, 1 - key_axis), STRETCH)
    return keys <= queries


def attend_kernel(count_ref, slots_ref, parity_ref, q_ref, kv_ref, out_ref, acc_ref):
    odd = parity_ref[0] == 1
    ones = jnp.ones((STRETCH, HEAD_WIDTH), BF16)

    def add_block(block, slot, last):
        tile = kv_ref[slot]
        keys = [tile[:, :64], tile[:, 64:128]]
        values = [
            jnp.concatenate([tile[:, 128:192], ones], axis=1),
            jnp.concatenate([tile[:, 192:256], ones], axis=1),
        ]
        middle_key = jnp.where(odd, keys[1], keys[0])
        middle_value = jnp.where(odd, values[1], values[0])
        for pair, key, value in (
            (0, keys[0], values[0]),
            (1, middle_key, middle_value),
            (2, keys[1], values[1]),
        ):
            scores = by_cols(q_ref[block, pair], key)
            weights = jnp.exp2(scores * (LOG2E * HEAD_WIDTH**-0.5))
            if last:
                weights = jnp.where(visible_mask(weights.shape, 1), weights, 0.0)
            acc_ref[pair] += product(weights.astype(BF16), value)

    def one_block(block, carry):
        acc_ref[...] = jnp.zeros_like(acc_ref)
        count = count_ref[block]

        def step(index, inner):
            add_block(block, slots_ref[block, index], False)
            return inner

        lax.fori_loop(0, count - 1, step, 0)
        add_block(block, slots_ref[block, count - 1], True)
        for pair in range(PAIRS):
            total = acc_ref[pair]
            denominator = total[:, HEAD_WIDTH:]
            out_ref[block, pair] = jnp.concatenate(
                [total[:, :HEAD_WIDTH] / denominator, jnp.log2(denominator)], axis=1
            )
        return carry

    lax.fori_loop(0, q_ref.shape[0], one_block, 0)


def attend(counts, slots, parity, queries, keyvalues):
    blocks = queries.shape[0]
    smem = pl.BlockSpec(memory_space=pltpu.SMEM)
    vmem = pl.BlockSpec(memory_space=pltpu.VMEM)
    return pl.pallas_call(
        attend_kernel,
        out_shape=jax.ShapeDtypeStruct((blocks, PAIRS, 2 * STRETCH, 128), F32),
        in_specs=[smem, smem, smem, vmem, vmem],
        out_specs=vmem,
        scratch_shapes=[pltpu.VMEM((PAIRS, 2 * STRETCH, 128), F32)],
        compiler_params=pltpu.CompilerParams(vmem_limit_bytes=40 << 20),
        cost_estimate=pl.CostEstimate(
            flops=4 * 20 * PAIRS * 256 * 128 * 64 * 4, bytes_accessed=8 << 20, transcendentals=0
        ),
        name="attend",
    )(counts, slots, parity, queries, keyvalues)


def attend_back_kernel(
    count_ref, slots_ref, parity_ref, q_ref, do_ref, log_ref, delta_ref, kv_ref, dq_ref, dkv_ref
):
    odd = parity_ref[0] == 1
    scale = HEAD_WIDTH**-0.5
    dq_ref[...] = jnp.zeros_like(dq_ref)
    dkv_ref[...] = jnp.zeros_like(dkv_ref)

    def add_block(block, slot, last):
        tile = kv_ref[slot]
        keys = [tile[:, :64], tile[:, 64:128]]
        values = [tile[:, 128:192], tile[:, 192:256]]
        middle_key = jnp.where(odd, keys[1], keys[0])
        middle_value = jnp.where(odd, values[1], values[0])
        d_keys, d_values = [], []
        for pair, key, value in (
            (0, keys[0], values[0]),
            (1, middle_key, middle_value),
            (2, keys[1], values[1]),
        ):
            query, d_out = q_ref[block, pair], do_ref[block, pair]
            scores = by_cols(key, query)
            weights = jnp.exp2(scores * (LOG2E * scale) - log_ref[block, pair])
            if last:
                weights = jnp.where(visible_mask(weights.shape, 0), weights, 0.0)
            d_weights = by_cols(value, d_out)
            d_scores = (weights * (d_weights - delta_ref[block, pair])).astype(BF16)
            d_values.append(product(weights.astype(BF16), d_out))
            d_keys.append(product(d_scores, query))
            dq_ref[block, pair] += by_rows(d_scores, key) * scale
        zero = jnp.zeros((STRETCH, HEAD_WIDTH), F32)
        parts = [
            (d_keys[0] + jnp.where(odd, zero, d_keys[1])) * scale,
            (d_keys[2] + jnp.where(odd, d_keys[1], zero)) * scale,
            d_values[0] + jnp.where(odd, zero, d_values[1]),
            d_values[2] + jnp.where(odd, d_values[1], zero),
        ]
        dkv_ref[slot] += jnp.concatenate(parts, axis=1)

    def one_block(block, carry):
        count = count_ref[block]

        def step(index, inner):
            add_block(block, slots_ref[block, index], False)
            return inner

        lax.fori_loop(0, count - 1, step, 0)
        add_block(block, slots_ref[block, count - 1], True)
        return carry

    lax.fori_loop(0, q_ref.shape[0], one_block, 0)


def attend_back(counts, slots, parity, queries, d_out, logs, delta, keyvalues):
    blocks = queries.shape[0]
    smem = pl.BlockSpec(memory_space=pltpu.SMEM)
    vmem = pl.BlockSpec(memory_space=pltpu.VMEM)
    return pl.pallas_call(
        attend_back_kernel,
        out_shape=(
            jax.ShapeDtypeStruct((blocks, PAIRS, 2 * STRETCH, HEAD_WIDTH), F32),
            jax.ShapeDtypeStruct(keyvalues.shape, F32),
        ),
        in_specs=[smem] * 3 + [vmem] * 5,
        out_specs=(vmem, vmem),
        compiler_params=pltpu.CompilerParams(vmem_limit_bytes=56 << 20),
        cost_estimate=pl.CostEstimate(
            flops=10 * 20 * PAIRS * 256 * 128 * 64 * 4, bytes_accessed=8 << 20, transcendentals=0
        ),
        name="attend_back",
    )(counts, slots, parity, queries, d_out, logs, delta, keyvalues)


def local(
    states,
    query_weight,
    keyvalue_matrix,
    output_weight,
    gate_weight,
    up_weight,
    down_weight,
    norm_gains,
    query_gain,
    key_gain,
    slot_sequence,
    slot_offset,
    out_grad,
):
    token_rows, width = states.shape
    dp_ranks = lax.axis_size("dp")
    tensor_ranks = lax.axis_size("tensor")
    lines = dp_ranks // PLANES
    rank, part = lax.axis_index("dp"), lax.axis_index("tensor")
    plane, line = rank // lines, rank % lines
    quarter = token_rows // tensor_ranks
    heads_here = QUERY_HEADS // tensor_ranks
    head_width = heads_here * HEAD_WIDTH
    sharing_count = QUERY_HEADS // KEYVALUE_HEADS
    blocks_here = token_rows // STRETCH
    slot_count = slot_sequence.shape[0]
    hidden = gate_weight.shape[2]
    slice_width = hidden // PLANES
    weight_rows = width // dp_ranks

    def send(value, kz=0, ky=0, kx=0, kc=0):
        move_rank, move_part = kz * lines + ky, kx * 2 + kc
        pairs = [
            (r * tensor_ranks + p, (r ^ move_rank) * tensor_ranks + (p ^ move_part))
            for r in range(dp_ranks)
            for p in range(tensor_ranks)
        ]
        return lax.ppermute(value, ("dp", "tensor"), pairs)

    def gather_planes(value):
        near = send(value, kz=1)
        far = send(value, kz=2)
        return [value, near, far, send(far, kz=1)]

    def gather_dp(value):
        whole = jnp.zeros((dp_ranks, *value.shape), value.dtype)
        for kz, piece in enumerate(gather_planes(value)):
            for ky in range(lines):
                got = send(piece, ky=ky) if ky else piece
                whole = lax.dynamic_update_index_in_dim(whole, got, rank ^ (kz * lines + ky), 0)
        return whole

    def rounded(value):
        return value.astype(BF16)

    def scatter_dp(whole):
        def piece(move):
            return lax.dynamic_index_in_dim(whole, rank ^ move, 0, keepdims=False)

        parts = []
        for kz in range(PLANES):
            total = piece(kz * lines).astype(F32)
            for ky in range(1, lines):
                total = total + send(rounded(piece(kz * lines + ky)), ky=ky).astype(F32)
            parts.append(total)
        return scatter_planes(parts)

    def scatter_planes(parts):
        near = parts[0] + send(rounded(parts[1]), kz=1).astype(F32)
        far = parts[2] + send(rounded(parts[3]), kz=1).astype(F32)
        return near + send(rounded(far), kz=2).astype(F32)

    def scatter_tensor(blocks):
        got = send(rounded(jnp.concatenate([blocks[1], blocks[3]], axis=0)), kc=1).astype(F32)
        rows = blocks[0].shape[0]
        here = blocks[0] + got[:rows]
        there = blocks[2] + got[rows:]
        return here + send(rounded(there), kx=1).astype(F32)

    def gather_tensor(block):
        both = jnp.concatenate([block, send(block, kx=1)], axis=0)
        return jnp.concatenate([both, send(both, kc=1)], axis=0)

    def in_order(blocks):
        whole = jnp.zeros_like(blocks)
        for index, move in enumerate((0, 2, 1, 3)):
            whole = lax.dynamic_update_slice_in_dim(
                whole,
                blocks[index * quarter : (index + 1) * quarter],
                (part ^ move) * quarter,
                0,
            )
        return whole

    def quarters(value):
        return [
            lax.dynamic_slice_in_dim(value, (part ^ move) * quarter, quarter, 0)
            for move in range(tensor_ranks)
        ]

    sequence_here = lax.dynamic_slice_in_dim(slot_sequence, rank * blocks_here, blocks_here)
    offset_here = lax.dynamic_slice_in_dim(slot_offset, rank * blocks_here, blocks_here)
    counts = offset_here // STRETCH + 1
    places = jnp.arange(slot_count, dtype=jnp.int32)
    same = (slot_sequence[None, None, :] == sequence_here[:, None, None]) & (
        slot_offset[None, None, :] == places[None, :, None] * STRETCH
    )
    slots = jnp.sum(jnp.where(same, places[None, None, :], 0), axis=2).astype(jnp.int32)
    parity = jnp.reshape(part % 2, (1,)).astype(jnp.int32)
    positions = (offset_here[:, None] + jnp.arange(STRETCH, dtype=jnp.int32)[None, :]).reshape(-1)
    cosines, sines = angles(positions, HEAD_WIDTH)

    first_key = (part * heads_here) // sharing_count * HEAD_WIDTH
    value_start = KEYVALUE_HEADS * HEAD_WIDTH
    kv_columns = [
        lax.dynamic_slice_in_dim(keyvalue_matrix[0], first_key, 2 * HEAD_WIDTH, 1),
        lax.dynamic_slice_in_dim(keyvalue_matrix[0], value_start + first_key, 2 * HEAD_WIDTH, 1),
    ]
    gains = gather_dp(norm_gains[0].T).transpose(1, 0, 2).reshape(2, width).astype(F32)
    w_attend = gather_dp(jnp.concatenate([query_weight[0], *kv_columns], axis=1)).reshape(width, -1)
    w_output = gather_dp(output_weight[0]).reshape(width, head_width)

    def sliced(weight):
        return weight[0].reshape(weight_rows, PLANES, slice_width).transpose(1, 0, 2)

    pad_first = -2 * slice_width % 128
    pad_second = -slice_width % 128
    packed = jnp.concatenate(
        [
            sliced(gate_weight),
            sliced(up_weight),
            jnp.zeros((PLANES, weight_rows, pad_first), BF16),
            sliced(down_weight),
            jnp.zeros((PLANES, weight_rows, pad_second), BF16),
        ],
        axis=2,
    )
    w_hidden = jnp.zeros((dp_ranks, weight_rows, packed.shape[2]), BF16)
    for kz in range(PLANES):
        piece = lax.dynamic_index_in_dim(packed, plane ^ kz, 0, keepdims=False)
        piece = send(piece, kz=kz) if kz else piece
        for ky in range(lines):
            got = send(piece, ky=ky) if ky else piece
            w_hidden = lax.dynamic_update_index_in_dim(w_hidden, got, rank ^ (kz * lines + ky), 0)
    w_hidden = w_hidden.reshape(width, -1)
    down_start = 2 * slice_width + pad_first
    w_gate_up = w_hidden[:, : 2 * slice_width]
    w_down = w_hidden[:, down_start : down_start + slice_width]

    def gather_group(block):
        return [gather_tensor(piece) for piece in gather_planes(block)]

    def quarter_of(value):
        return lax.dynamic_slice_in_dim(value, part * quarter, quarter, 0)

    query_g, key_g = query_gain[0], key_gain[0]
    attn_in = rounded(normed(states.astype(F32), gains[0]))
    lin = product(attn_in, w_attend)
    query_lin, keyvalue_lin = lin[:, :head_width], lin[:, head_width:]

    def query_side(linear, gain_vector):
        return rotated(
            normed(linear.reshape(token_rows, heads_here, HEAD_WIDTH), gain_vector), cosines, sines
        )

    def key_side(linear, gain_vector):
        keys = linear[:, : 2 * HEAD_WIDTH].reshape(token_rows, 2, HEAD_WIDTH)
        keys = rotated(normed(keys, gain_vector), cosines, sines)
        return jnp.concatenate(
            [keys.reshape(token_rows, 2 * HEAD_WIDTH), linear[:, 2 * HEAD_WIDTH :]], axis=1
        )

    def to_pairs(value):
        return (
            value.reshape(blocks_here, STRETCH, PAIRS, 2, -1)
            .transpose(0, 2, 3, 1, 4)
            .reshape(blocks_here, PAIRS, 2 * STRETCH, -1)
        )

    def from_pairs(value):
        return (
            value.reshape(blocks_here, PAIRS, 2, STRETCH, -1)
            .transpose(0, 3, 1, 2, 4)
            .reshape(token_rows, heads_here, -1)
        )

    queries = to_pairs(rounded(query_side(query_lin, query_g)))
    keyvalues = gather_dp(rounded(key_side(keyvalue_lin, key_g)))
    keyvalues = keyvalues.reshape(slot_count, STRETCH, 4 * HEAD_WIDTH)
    attended = attend(counts, slots, parity, queries, keyvalues)
    attn_out = rounded(from_pairs(attended[..., :HEAD_WIDTH]).reshape(token_rows, head_width))
    logs = attended[..., HEAD_WIDTH]

    branch = scatter_tensor(quarters(by_cols(attn_out, w_output)))
    states_quarter = quarter_of(states).astype(F32)
    middle = states_quarter + branch
    ffn_in = rounded(normed(middle, gains[1]))

    down_grads = gather_group(quarter_of(out_grad))
    ffn_ins = gather_group(ffn_in)
    mixed_chunks, d_chunks, back_parts, out_parts = [], [], [], []
    for down_grad, ffn_chunk in zip(down_grads, ffn_ins):
        gate_up = product(ffn_chunk, w_gate_up)
        gate_pre, up_pre = gate_up[:, :slice_width], gate_up[:, slice_width:]
        sigmoid_gate = jax.nn.sigmoid(gate_pre)
        mixed = rounded(gate_pre * sigmoid_gate * up_pre)
        d_mixed = product(down_grad, w_down)
        d_gate = d_mixed * up_pre * sigmoid_gate * (1.0 + gate_pre * (1.0 - sigmoid_gate))
        d_up = d_mixed * gate_pre * sigmoid_gate
        d_gate_up = jnp.concatenate([rounded(d_gate), rounded(d_up)], axis=1)
        mixed_chunks.append(mixed)
        d_chunks.append(d_gate_up)

        def reduced(value):
            blocks = value.reshape(4, quarter, width)
            return scatter_tensor([blocks[0], blocks[2], blocks[1], blocks[3]])

        back_parts.append(reduced(by_cols(d_gate_up, w_gate_up)))
        out_parts.append(reduced(by_cols(mixed, w_down)))
    d_ffn_in = scatter_planes(back_parts)

    def norm_back(vector, gain_vector, grad):
        inverse = lax.rsqrt(jnp.mean(vector * vector, axis=-1, keepdims=True) + EPSILON)
        unit = vector * inverse
        scaled = grad * gain_vector
        back = inverse * (scaled - unit * jnp.mean(scaled * unit, axis=-1, keepdims=True))
        return back, jnp.sum(grad * unit, axis=0)

    d_middle, d_gain_ffn = norm_back(middle, gains[1], d_ffn_in)
    grad_middle = quarter_of(out_grad).astype(F32) + d_middle
    output_grad = in_order(gather_tensor(rounded(grad_middle)))

    d_wout = by_rows(output_grad, attn_out)
    d_heads = rounded(product(output_grad, w_output)).reshape(token_rows, heads_here, HEAD_WIDTH)
    d_pairs = to_pairs(d_heads)
    delta = jnp.sum(d_pairs.astype(F32) * attended[..., :HEAD_WIDTH], axis=-1)
    d_query, d_keyvalue = attend_back(
        counts,
        slots,
        parity,
        queries,
        d_pairs,
        logs[:, :, None, :],
        delta[:, :, None, :],
        keyvalues,
    )
    d_keyvalue_here = scatter_dp(d_keyvalue.reshape(dp_ranks, token_rows, 4 * HEAD_WIDTH))
    _, query_pull = jax.vjp(query_side, query_lin, query_g)
    d_query_lin, d_querygain = query_pull(from_pairs(d_query))
    _, key_pull = jax.vjp(key_side, keyvalue_lin, key_g)
    d_keyvalue_lin, d_keygain = key_pull(d_keyvalue_here)
    d_lin = jnp.concatenate([rounded(d_query_lin), rounded(d_keyvalue_lin)], axis=1)
    d_attn_in = scatter_tensor(quarters(by_cols(d_lin, w_attend)))
    d_states, d_gain_attn = norm_back(states_quarter, gains[0], d_attn_in)
    states_grad = in_order(gather_tensor(rounded(grad_middle + d_states))).astype(F32)

    d_wattend = scatter_dp(by_rows(attn_in, d_lin).reshape(dp_ranks, weight_rows, -1))
    d_wout = scatter_dp(d_wout.reshape(dp_ranks, weight_rows, -1))
    ffn_all = jnp.concatenate(ffn_ins, axis=0)
    down_all = jnp.concatenate(down_grads, axis=0)
    grads_hidden = jnp.concatenate(
        [
            by_rows(ffn_all, jnp.concatenate(d_chunks, axis=0)),
            by_rows(down_all, jnp.concatenate(mixed_chunks, axis=0)),
        ],
        axis=1,
    ).reshape(dp_ranks, weight_rows, 3 * slice_width)
    collected = jnp.zeros((PLANES, weight_rows, 3 * slice_width), F32)
    for kz in range(PLANES):
        total = lax.dynamic_index_in_dim(grads_hidden, rank ^ (kz * lines), 0, keepdims=False)
        for ky in range(1, lines):
            piece = lax.dynamic_index_in_dim(
                grads_hidden, rank ^ (kz * lines + ky), 0, keepdims=False
            )
            total = total + send(rounded(piece), ky=ky).astype(F32)
        if kz:
            total = send(rounded(total), kz=kz).astype(F32)
        collected = lax.dynamic_update_index_in_dim(collected, total, plane ^ kz, 0)

    def unsliced(index):
        piece = collected[:, :, index * slice_width : (index + 1) * slice_width]
        return piece.transpose(1, 0, 2).reshape(1, weight_rows, hidden)

    kv_grad = d_wattend[:, head_width:]
    spread = jnp.zeros((weight_rows, 2 * value_start), F32)
    spread = lax.dynamic_update_slice_in_dim(spread, kv_grad[:, : 2 * HEAD_WIDTH], first_key, 1)
    spread = lax.dynamic_update_slice_in_dim(
        spread, kv_grad[:, 2 * HEAD_WIDTH :], value_start + first_key, 1
    )
    d_wkeyvalue = lax.psum(spread, "tensor")

    result_quarter = rounded(middle + scatter_planes(out_parts))
    result = in_order(gather_tensor(result_quarter))

    small = jnp.concatenate([d_gain_attn, d_gain_ffn, d_querygain, d_keygain])
    small = lax.psum(small, ("dp", "tensor"))
    d_gains = lax.dynamic_slice_in_dim(
        small[: 2 * width].reshape(2, width), rank * weight_rows, weight_rows, 1
    ).T
    return (
        result,
        states_grad,
        d_wattend[None, :, :head_width],
        d_wkeyvalue[None],
        d_wout[None],
        unsliced(0),
        unsliced(1),
        unsliced(2),
        d_gains[None],
        small[2 * width : 2 * width + HEAD_WIDTH][None],
        small[2 * width + HEAD_WIDTH :][None],
    )


def solution(mesh):
    return jax.shard_map(
        local,
        mesh=mesh,
        in_specs=(
            P("dp", None),
            P(None, "dp", "tensor"),
            P(None, "dp", None),
            P(None, "dp", "tensor"),
            P(None, "dp", "tensor"),
            P(None, "dp", "tensor"),
            P(None, "dp", "tensor"),
            P(None, "dp", None),
            P(),
            P(),
            P(),
            P(),
            P("dp", None),
        ),
        out_specs=(
            P("dp", None),
            P("dp", None),
            P(None, "dp", "tensor"),
            P(None, "dp", None),
            P(None, "dp", "tensor"),
            P(None, "dp", "tensor"),
            P(None, "dp", "tensor"),
            P(None, "dp", "tensor"),
            P(None, "dp", None),
            P(),
            P(),
        ),
        check_vma=False,
    )
```

time: 2040 us -> 869 us (0.43)
  waiting for transfers between devices: 1570 us -> 333 us
  starting transfers between devices: 1.65 us -> 132 us
  matrix products: 159 us -> 85.1 us
  Pallas kernels: 0 us -> 39.6 us
  blocking collectives: 62.2 us -> 37.1 us
  loops' own time: 21 us -> 0 us
    reduce_scatter x7 -> x0, waiting for transfers between devices: 931 us -> none  [the longest x1 175 us: local(): lax.psum_scatter(d_wgate, 'dp', scatter_dimension=0, tiled=True)]
    all_gather x7 -> x0, waiting for transfers between devices: 369 us -> none  [the longest x1 81.8 us: local(): lax.all_gather(up_weight[layer_index], 'dp', axis=0, tiled=True)]
    ppermute x0 -> x117, waiting for transfers between devices: none -> 332 us  [send(): return lax.ppermute(value, ('dp', 'tensor'), pairs)]
    psum x3 -> x1, waiting for transfers between devices: 263 us -> 0.01 us  [local(): d_wkeyvalue = lax.psum(spread, 'tensor')]
    ppermute x0 -> x117, starting transfers between devices: none -> 132 us  [send(): return lax.ppermute(value, ('dp', 'tensor'), pairs)]
    dot_general x66 -> x10, matrix products: 106 us -> 30.3 us  [product(): return jnp.dot(left_side, right_side, preferred_element_type=F32)]
    pallas_call x0 -> x2, Pallas kernels: none -> 39.6 us  [the longest x1 26.8 us: attend_back(): pl.pallas_call(attend_back_kernel, out_shape=(jax.ShapeDtypeStruct((block...]
    unnamed x105 -> x266, local copies, waits for them, and re-layouts: 12.4 us -> 46.6 us
  transfers between devices with their start and end apart: 18 -> 118, of which waited for: 16 -> 53; matrix products, arithmetic and copies ran while one was open for 7% -> 34% of each run, Pallas kernels for 0% -> 5%
where the time goes in v1:
time: 869 us; the launch traced here: 856 us
  waiting for transfers between devices  333 us (38%)
  local copies, waits for them, and re-layouts  154 us (18%)
  starting transfers between devices  132 us (15%)
  matrix products  85.1 us (10%)
  other arithmetic  58.1 us (7%)
  Pallas kernels  39.6 us (5%)
  blocking collectives  37.1 us (4%)
  between operations  16.9 us (2%)
    ppermute x117, waiting for transfers between devices, send(): return lax.ppermute(value, ('dp', 'tensor'), pairs)  332 us
    ppermute x117, starting transfers between devices, send(): return lax.ppermute(value, ('dp', 'tensor'), pairs)  132 us
    unnamed x266, local copies, waits for them, and re-layouts  46.6 us
    psum x1, blocking collectives, local(): small = lax.psum(small, ('dp', 'tensor'))  37.1 us
    dot_general x10, matrix products, by_cols(): lax.dot_general(left_side, right_side, (((1,), (1,)), ((), ())), preferre...  31.1 us
    dot_general x10, matrix products, product(): return jnp.dot(left_side, right_side, preferred_element_type=F32)  30.3 us
    pallas_call x1, Pallas kernels, attend_back(): pl.pallas_call(attend_back_kernel, out_shape=(jax.ShapeDtypeStruct((block...  26.8 us
    dot_general x4, matrix products, by_rows(): lax.dot_general(left_side, right_side, (((0,), (0,)), ((), ())), preferre...  23.7 us
  transfers between devices with their start and end apart: 118, of which 53 were waited for; matrix products, arithmetic and copies ran while one was open for 34% of the time, Pallas kernels for 5%

profile of v1, /device:TPU:0, one launch (start us, length us, event | category | flops | bytes accessed | tf_op | source)
XLA Modules:
  0.0 856.2 jit_solution(1846649725244007606)
XLA Ops:
  83.8 8.8 %collective-permute-done.26 = bf16[256,384]{1,0:T(8,128)(2,1)S(1)} collective-permute-done((bf16[256,384]{1,0:T(8,128)(2,1)}, bf16[256,384]{1,0:T(8,128)(2,1)S(1)}, u32[]{:S(2)}, u32[]{:S(2)}) %collective-permute-start.26) | collective-permute-done | bytes 196640 | tf_op jit(solution)/shard_map/ppermute | solution.py:241
  95.3 9.3 %collective-permute-done.32 = bf16[256,1024]{1,0:T(8,128)(2,1)S(1)} collective-permute-done((bf16[256,1024]{1,0:T(8,128)(2,1)S(1)}, bf16[256,1024]{1,0:T(8,128)(2,1)S(1)}, u32[]{:S(2)}, u32[]{:S(2)}) %collective-permute-start.32) | collective-permute-done | bytes 524320 | tf_op jit(solution)/shard_map/ppermute | solution.py:241
  179.5 14.6 %collective-permute-start.17 = (bf16[384,256]{1,0:T(8,128)(2,1)S(1)}, bf16[384,256]{1,0:T(8,128)(2,1)S(1)}, u32[]{:S(2)}, u32[]{:S(2)}) collective-permute-start(bf16[384,256]{1,0:T(8,128)(2,1)S(1)} %pad_maximum_fusion.18), channel_id=1, source_target_pairs={{0,16},{1,17},{2,18},{3,19},{4,20},{5,21},{6,22},{7,23},{8,24},{9,... | collective-permute-start | bytes 589832 | tf_op jit(solution)/shard_map/ppermute | solution.py:241
  226.7 12.8 %attend.1 = f32[3,3,256,128]{3,2,1,0:T(8,128)S(1)} custom-call(s32[3]{0:T(128)S(1)} %get-tuple-element.37.count_ref, s32[3,24]{1,0:T(4,128)S(1)} %select_reduce_fusion.slots_ref, s32[1]{0:T(128)} %bitcast.parity_ref, bf16[3,3,256,64]{3,2,1,0:T(8,128)(2,1)S(1)} %bitcast.334, bf16[24,128,256]{2,1,0:T(8,128)(2,1)S(1)} %bitcast.332), custom_call_target="tpu_custom_call" | custom-call | flops 2013265920 | bytes 8388608 | tf_op jit(solution)/shard_map/attend/pallas_call | solution.py:116
  270.5 12.7 %collective-permute-done.47 = bf16[96,2048]{1,0:T(8,128)(2,1)S(1)} collective-permute-done((bf16[96,2048]{1,0:T(8,128)(2,1)S(1)}, bf16[96,2048]{1,0:T(8,128)(2,1)S(1)}, u32[]{:S(2)}, u32[]{:S(2)}) %collective-permute-start.47) | collective-permute-done | bytes 393248 | tf_op jit(solution)/shard_map/ppermute | solution.py:241
  303.7 7.3 collective-permute-done.53
  366.8 16.1 %fusion.3 = f32[2048,608]{0,1:T(8,128)} fusion(bf16[1536,2048]{1,0:T(8,128)(2,1)S(1)} %constant_dynamic-update-slice_fusion.4, bf16[384,304]{0,1:T(8,128)(2,1)S(1)} %get-tuple-element.84, bf16[384,304]{0,1:T(8,128)(2,1)S(1)} %get-tuple-element.83, bf16[384,304]{0,1:T(8,128)(2,1)S(1)} %get-tuple-element.86, bf16[384,304]{0,1:T(8,128)(2,1)S(1)} %get-tuple-element.85, ...), kind=kOutput, calls=%fused_computation.6 | convolution fusion | flops 3840147456 | bytes 13139968 | tf_op jit(solution)/shard_map/dot_general | solution.py:27
  402.7 12.9 %constant_dynamic-slice_fusion.1 = (bf16[1,256,912]{1,0,2:T(2,128)(2,1)S(1)}, bf16[1,256,912]{1,0,2:T(2,128)(2,1)S(1)}, bf16[1,256,912]{1,0,2:T(2,128)(2,1)S(1)}, bf16[1,256,912]{1,0,2:T(2,128)(2,1)S(1)}) fusion(f32[8,256,912]{1,0,2:T(8,128)} %bitcast.337, s32[]{:T(128)S(6)} %select_n.196, s32[]{:T(128)S(6)} %select_n.194, s32[]{:T(128)S(6)} %select_n.192, ...), kind=kLoop, calls=%fused_computation.412 | loop fusion | bytes 3735568 | tf_op jit(solution)/shard_map/jit(dynamic_index_in_dim)/dynamic_slice | solution.py:475
  440.3 7.5 collective-permute-done.111
  449.0 8.8 %collective-permute-done.113 = bf16[256,912]{0,1:T(8,128)(2,1)S(1)} collective-permute-done((bf16[256,912]{0,1:T(8,128)(2,1)S(1)}, bf16[256,912]{0,1:T(8,128)(2,1)S(1)}, u32[]{:S(2)}, u32[]{:S(2)}) %collective-permute-start.113) | collective-permute-done | bytes 466976 | tf_op jit(solution)/shard_map/ppermute | solution.py:241
  459.0 8.8 %collective-permute-done.115 = bf16[256,912]{0,1:T(8,128)(2,1)S(1)} collective-permute-done((bf16[256,912]{0,1:T(8,128)(2,1)S(1)}, bf16[256,912]{0,1:T(8,128)(2,1)S(1)}, u32[]{:S(2)}, u32[]{:S(2)}) %collective-permute-start.115) | collective-permute-done | bytes 466976 | tf_op jit(solution)/shard_map/ppermute | solution.py:241
  468.7 8.3 collective-permute-done.110
  480.6 23.4 %collective-permute-done.45 = bf16[96,2048]{1,0:T(8,128)(2,1)S(1)} collective-permute-done((bf16[96,2048]{1,0:T(8,128)(2,1)S(1)}, bf16[96,2048]{1,0:T(8,128)(2,1)S(1)}, u32[]{:S(2)}, u32[]{:S(2)}) %collective-permute-start.45) | collective-permute-done | bytes 393248 | tf_op jit(solution)/shard_map/ppermute | solution.py:241
  507.8 17.1 %collective-permute-done.112 = bf16[256,912]{0,1:T(8,128)(2,1)S(1)} collective-permute-done((bf16[256,912]{0,1:T(8,128)(2,1)S(1)}, bf16[256,912]{0,1:T(8,128)(2,1)S(1)}, u32[]{:S(2)}, u32[]{:S(2)}) %collective-permute-start.112) | collective-permute-done | bytes 466976 | tf_op jit(solution)/shard_map/ppermute | solution.py:241
  526.7 11.0 %collective-permute-done.116 = bf16[256,912]{0,1:T(8,128)(2,1)S(1)} collective-permute-done((bf16[256,912]{0,1:T(8,128)(2,1)S(1)}, bf16[256,912]{0,1:T(8,128)(2,1)S(1)}, u32[]{:S(2)}, u32[]{:S(2)}) %collective-permute-start.116) | collective-permute-done | bytes 466976 | tf_op jit(solution)/shard_map/ppermute | solution.py:241
  540.0 14.6 %collective-permute-done.56 = bf16[96,2048]{1,0:T(8,128)(2,1)S(1)} collective-permute-done((bf16[96,2048]{1,0:T(8,128)(2,1)S(1)}, bf16[96,2048]{1,0:T(8,128)(2,1)S(1)}, u32[]{:S(2)}, u32[]{:S(2)}) %collective-permute-start.56) | collective-permute-done | bytes 393248 | tf_op jit(solution)/shard_map/ppermute | solution.py:241
  554.6 13.0 %collective-permute-start.81 = (bf16[96,2048]{1,0:T(8,128)(2,1)S(1)}, bf16[96,2048]{1,0:T(8,128)(2,1)S(1)}, u32[]{:S(2)}, u32[]{:S(2)}) collective-permute-start(bf16[96,2048]{1,0:T(8,128)(2,1)S(1)} %fusion.94), channel_id=1, source_target_pairs={{0,8},{1,9},{2,10},{3,11},{4,12},{5,13},{6,14},{7,15},{8,0},{9,1},... | collective-permute-start | bytes 1179656 | tf_op jit(solution)/shard_map/ppermute | solution.py:241
  567.9 9.8 %collective-permute-done.81 = bf16[96,2048]{1,0:T(8,128)(2,1)S(1)} collective-permute-done((bf16[96,2048]{1,0:T(8,128)(2,1)S(1)}, bf16[96,2048]{1,0:T(8,128)(2,1)S(1)}, u32[]{:S(2)}, u32[]{:S(2)}) %collective-permute-start.81) | collective-permute-done | bytes 393248 | tf_op jit(solution)/shard_map/ppermute | solution.py:241
  580.0 14.5 %collective-permute-done.57 = bf16[96,2048]{1,0:T(8,128)(2,1)S(1)} collective-permute-done((bf16[96,2048]{1,0:T(8,128)(2,1)S(1)}, bf16[96,2048]{1,0:T(8,128)(2,1)S(1)}, u32[]{:S(2)}, u32[]{:S(2)}) %collective-permute-start.57) | collective-permute-done | bytes 393248 | tf_op jit(solution)/shard_map/ppermute | solution.py:241
  597.7 25.3 %collective-permute-done.82 = bf16[96,2048]{1,0:T(8,128)(2,1)S(1)} collective-permute-done((bf16[96,2048]{1,0:T(8,128)(2,1)S(1)}, bf16[96,2048]{1,0:T(8,128)(2,1)S(1)}, u32[]{:S(2)}, u32[]{:S(2)}) %collective-permute-start.82) | collective-permute-done | bytes 393248 | tf_op jit(solution)/shard_map/ppermute | solution.py:241
  629.8 8.0 collective-permute-done.83
  665.4 26.8 %attend_back.1 = (f32[3,3,256,64]{3,2,1,0:T(8,128)}, f32[24,128,256]{2,1,0:T(8,128)}) custom-call(s32[3]{0:T(128)} %copy-done.3, s32[3,24]{1,0:T(4,128)} %copy-done.2, s32[1]{0:T(128)} %bitcast.parity_ref, bf16[3,3,256,64]{3,2,1,0:T(8,128)(2,1)} %bitcast.335, bf16[3,3,256,64]{3,2,1,0:T(8,128)(2,1)} %bitcast.359, f32[3,3,1,256]{3,2,1,0:T(1,128)} %bitcast.401, ...), custom_call_target="tpu_custom_call" | custom-call | flops 5033164800 | bytes 8388608 | tf_op jit(solution)/shard_map/attend_back/pallas_call | solution.py:187
  789.2 8.6 %collective-permute-done.102 = bf16[256,640]{1,0:T(8,128)(2,1)S(1)} collective-permute-done((bf16[256,640]{1,0:T(8,128)(2,1)S(1)}, bf16[256,640]{1,0:T(8,128)(2,1)S(1)}, u32[]{:S(2)}, u32[]{:S(2)}) %collective-permute-start.102) | collective-permute-done | bytes 327712 | tf_op jit(solution)/shard_map/ppermute | solution.py:241
  804.6 37.1 %psum.15 = f32[4224]{0:T(1024)S(1)} all-reduce(f32[4224]{0:T(1024)S(1)} %concatenate.217), channel_id=1, replica_groups=mesh['dp'=8,'tensor'=4] {'dp','tensor'}, use_global_device_ids=true, to_apply=%region_16.17 | all-reduce | flops 4224 | bytes 33792 | tf_op jit(solution)/shard_map/psum | solution.py:499
  (732 shorter events, 502.4 us)
Async XLA Ops:
  7.2 839.9 %all-reduce.8.cloned.1.call-start = ((), (), s32[]{:S(2)}) async-start(), calls=%async_computation | async-start | bytes 1572864 | tf_op jit(solution)/shard_map/psum | solution.py:493
  14.5 57.8 %collective-permute-start.24 = (bf16[256,384]{1,0:T(8,128)(2,1)}, bf16[256,384]{1,0:T(8,128)(2,1)}, u32[]{:S(2)}, u32[]{:S(2)}) collective-permute-start(bf16[256,384]{1,0:T(8,128)(2,1)} %bitcast.392), channel_id=1, source_target_pairs={{0,16},{1,17},{2,18},{3,19},{4,20},{5,21},{6,22},{7,23},{8,24},{9,... | collective-permute-start | bytes 589832 | tf_op jit(solution)/shard_map/ppermute | solution.py:241
  14.8 48.3 %collective-permute-start.22 = (bf16[256,384]{1,0:T(8,128)(2,1)}, bf16[256,384]{1,0:T(8,128)(2,1)}, u32[]{:S(2)}, u32[]{:S(2)}) collective-permute-start(bf16[256,384]{1,0:T(8,128)(2,1)} %bitcast.393), channel_id=1, source_target_pairs={{0,8},{1,9},{2,10},{3,11},{4,12},{5,13},{6,14},{7,15},{8,0},{9,1},... | collective-permute-start | bytes 589832 | tf_op jit(solution)/shard_map/ppermute | solution.py:241
  60.4 48.9 %collective-permute-start.10 = (bf16[256,640]{1,0:T(8,128)(2,1)}, bf16[256,640]{1,0:T(8,128)(2,1)S(1)}, u32[]{:S(2)}, u32[]{:S(2)}) collective-permute-start(bf16[256,640]{1,0:T(8,128)(2,1)} %pad_maximum_fusion.15), channel_id=1, source_target_pairs={{0,16},{1,17},{2,18},{3,19},{4,20},{5,21},{6,22},{7,23},{8,24},{9,... | collective-permute-start | bytes 983048 | tf_op jit(solution)/shard_map/ppermute | solution.py:241
  63.1 64.2 %collective-permute-start.71 = (bf16[96,2048]{1,0:T(8,128)(2,1)S(1)}, bf16[96,2048]{1,0:T(8,128)(2,1)S(1)}, u32[]{:S(2)}, u32[]{:S(2)}) collective-permute-start(bf16[96,2048]{1,0:T(8,128)(2,1)S(1)} %get-tuple-element.26), channel_id=1, source_target_pairs={{0,16},{1,17},{2,18},{3,19},{4,20},{5,21},{6,22},{7,23},{8,24},{9,... | collective-permute-start | bytes 1179656 | tf_op jit(solution)/shard_map/ppermute | solution.py:241
  67.8 50.6 %collective-permute-start.65 = (bf16[96,2048]{1,0:T(8,128)(2,1)S(1)}, bf16[96,2048]{1,0:T(8,128)(2,1)S(1)}, u32[]{:S(2)}, u32[]{:S(2)}) collective-permute-start(bf16[96,2048]{1,0:T(8,128)(2,1)S(1)} %get-tuple-element.26), channel_id=1, source_target_pairs={{0,8},{1,9},{2,10},{3,11},{4,12},{5,13},{6,14},{7,15},{8,0},{9,1},... | collective-permute-start | bytes 1179656 | tf_op jit(solution)/shard_map/ppermute | solution.py:241
  127.3 81.9 %collective-permute-start.62 = (bf16[192,2048]{1,0:T(8,128)(2,1)}, bf16[192,2048]{1,0:T(8,128)(2,1)}, u32[]{:S(2)}, u32[]{:S(2)}) collective-permute-start(bf16[192,2048]{1,0:T(8,128)(2,1)} %pad_maximum_fusion.7), channel_id=1, source_target_pairs={{0,1},{1,0},{2,3},{3,2},{4,5},{5,4},{6,7},{7,6},{8,9},{9,8},{10,11... | collective-permute-start | bytes 2359304 | tf_op jit(solution)/shard_map/ppermute | solution.py:241
  161.9 88.5 %collective-permute-start.73 = (bf16[192,2048]{1,0:T(8,128)(2,1)}, bf16[192,2048]{1,0:T(8,128)(2,1)}, u32[]{:S(2)}, u32[]{:S(2)}) collective-permute-start(bf16[192,2048]{1,0:T(8,128)(2,1)} %pad_maximum_fusion.9), channel_id=1, source_target_pairs={{0,1},{1,0},{2,3},{3,2},{4,5},{5,4},{6,7},{7,6},{8,9},{9,8},{10,11... | collective-permute-start | bytes 2359304 | tf_op jit(solution)/shard_map/ppermute | solution.py:241
  165.6 79.7 %collective-permute-start.67 = (bf16[192,2048]{1,0:T(8,128)(2,1)}, bf16[192,2048]{1,0:T(8,128)(2,1)}, u32[]{:S(2)}, u32[]{:S(2)}) collective-permute-start(bf16[192,2048]{1,0:T(8,128)(2,1)} %pad_maximum_fusion.8), channel_id=1, source_target_pairs={{0,1},{1,0},{2,3},{3,2},{4,5},{5,4},{6,7},{7,6},{8,9},{9,8},{10,11... | collective-permute-start | bytes 2359304 | tf_op jit(solution)/shard_map/ppermute | solution.py:241
  207.3 60.5 %collective-permute-start.78 = (bf16[192,2048]{1,0:T(8,128)(2,1)}, bf16[192,2048]{1,0:T(8,128)(2,1)}, u32[]{:S(2)}, u32[]{:S(2)}) collective-permute-start(bf16[192,2048]{1,0:T(8,128)(2,1)} %pad_maximum_fusion.10), channel_id=1, source_target_pairs={{0,1},{1,0},{2,3},{3,2},{4,5},{5,4},{6,7},{7,6},{8,9},{9,8},{10,11... | collective-permute-start | bytes 2359304 | tf_op jit(solution)/shard_map/ppermute | solution.py:241
  321.5 97.5 %collective-permute-start.63 = (bf16[192,2048]{1,0:T(8,128)(2,1)}, bf16[192,2048]{1,0:T(8,128)(2,1)}, u32[]{:S(2)}, u32[]{:S(2)}) collective-permute-start(bf16[192,2048]{1,0:T(8,128)(2,1)} %concatenate.237), channel_id=1, source_target_pairs={{0,1},{1,0},{2,3},{3,2},{4,5},{5,4},{6,7},{7,6},{8,9},{9,8},{10,11... | collective-permute-start | bytes 2359304 | tf_op jit(solution)/shard_map/ppermute | solution.py:241
  325.7 97.0 %collective-permute-start.39 = (bf16[192,2048]{1,0:T(8,128)(2,1)}, bf16[192,2048]{1,0:T(8,128)(2,1)}, u32[]{:S(2)}, u32[]{:S(2)}) collective-permute-start(bf16[192,2048]{1,0:T(8,128)(2,1)} %concatenate.241), channel_id=1, source_target_pairs={{0,1},{1,0},{2,3},{3,2},{4,5},{5,4},{6,7},{7,6},{8,9},{9,8},{10,11... | collective-permute-start | bytes 2359304 | tf_op jit(solution)/shard_map/ppermute | solution.py:241
  336.2 94.2 %collective-permute-start.68 = (bf16[192,2048]{1,0:T(8,128)(2,1)S(1)}, bf16[192,2048]{1,0:T(8,128)(2,1)}, u32[]{:S(2)}, u32[]{:S(2)}) collective-permute-start(bf16[192,2048]{1,0:T(8,128)(2,1)S(1)} %concatenate.236), channel_id=1, source_target_pairs={{0,1},{1,0},{2,3},{3,2},{4,5},{5,4},{6,7},{7,6},{8,9},{9,8},{10,11... | collective-permute-start | bytes 2359304 | tf_op jit(solution)/shard_map/ppermute | solution.py:241
  347.7 84.2 %collective-permute-start.74 = (bf16[192,2048]{1,0:T(8,128)(2,1)}, bf16[192,2048]{1,0:T(8,128)(2,1)}, u32[]{:S(2)}, u32[]{:S(2)}) collective-permute-start(bf16[192,2048]{1,0:T(8,128)(2,1)} %concatenate.235), channel_id=1, source_target_pairs={{0,1},{1,0},{2,3},{3,2},{4,5},{5,4},{6,7},{7,6},{8,9},{9,8},{10,11... | collective-permute-start | bytes 2359304 | tf_op jit(solution)/shard_map/ppermute | solution.py:241
  356.4 77.6 %collective-permute-start.44 = (bf16[192,2048]{1,0:T(8,128)(2,1)}, bf16[192,2048]{1,0:T(8,128)(2,1)}, u32[]{:S(2)}, u32[]{:S(2)}) collective-permute-start(bf16[192,2048]{1,0:T(8,128)(2,1)} %concatenate.240), channel_id=1, source_target_pairs={{0,1},{1,0},{2,3},{3,2},{4,5},{5,4},{6,7},{7,6},{8,9},{9,8},{10,11... | collective-permute-start | bytes 2359304 | tf_op jit(solution)/shard_map/ppermute | solution.py:241
  422.7 173.6 %collective-permute-start.64 = (bf16[96,2048]{1,0:T(8,128)(2,1)}, bf16[96,2048]{1,0:T(8,128)(2,1)}, u32[]{:S(2)}, u32[]{:S(2)}) collective-permute-start(bf16[96,2048]{1,0:T(8,128)(2,1)} %fusion.102), channel_id=1, source_target_pairs={{0,2},{1,3},{2,0},{3,1},{4,6},{5,7},{6,4},{7,5},{8,10},{9,11},{10,... | collective-permute-start | bytes 1179656 | tf_op jit(solution)/shard_map/ppermute | solution.py:241
  430.3 49.3 %collective-permute-start.79 = (bf16[192,2048]{1,0:T(8,128)(2,1)}, bf16[192,2048]{1,0:T(8,128)(2,1)S(1)}, u32[]{:S(2)}, u32[]{:S(2)}) collective-permute-start(bf16[192,2048]{1,0:T(8,128)(2,1)} %concatenate.234), channel_id=1, source_target_pairs={{0,1},{1,0},{2,3},{3,2},{4,5},{5,4},{6,7},{7,6},{8,9},{9,8},{10,11... | collective-permute-start | bytes 2359304 | tf_op jit(solution)/shard_map/ppermute | solution.py:241
  431.9 73.9 %collective-permute-start.55 = (bf16[192,2048]{1,0:T(8,128)(2,1)}, bf16[192,2048]{1,0:T(8,128)(2,1)S(1)}, u32[]{:S(2)}, u32[]{:S(2)}) collective-permute-start(bf16[192,2048]{1,0:T(8,128)(2,1)} %concatenate.238), channel_id=1, source_target_pairs={{0,1},{1,0},{2,3},{3,2},{4,5},{5,4},{6,7},{7,6},{8,9},{9,8},{10,11... | collective-permute-start | bytes 2359304 | tf_op jit(solution)/shard_map/ppermute | solution.py:241
  476.9 149.6 %collective-permute-start.40 = (bf16[96,2048]{1,0:T(8,128)(2,1)S(1)}, bf16[96,2048]{1,0:T(8,128)(2,1)S(1)}, u32[]{:S(2)}, u32[]{:S(2)}) collective-permute-start(bf16[96,2048]{1,0:T(8,128)(2,1)S(1)} %copy-done.80), channel_id=1, source_target_pairs={{0,2},{1,3},{2,0},{3,1},{4,6},{5,7},{6,4},{7,5},{8,10},{9,11},{10,... | collective-permute-start | bytes 1179656 | tf_op jit(solution)/shard_map/ppermute | solution.py:241
  478.0 89.7 %collective-permute-start.75 = (bf16[96,2048]{1,0:T(8,128)(2,1)S(1)}, bf16[96,2048]{1,0:T(8,128)(2,1)S(1)}, u32[]{:S(2)}, u32[]{:S(2)}) collective-permute-start(bf16[96,2048]{1,0:T(8,128)(2,1)S(1)} %fusion.95), channel_id=1, source_target_pairs={{0,2},{1,3},{2,0},{3,1},{4,6},{5,7},{6,4},{7,5},{8,10},{9,11},{10,... | collective-permute-start | bytes 1179656 | tf_op jit(solution)/shard_map/ppermute | solution.py:241
  642.9 74.1 %collective-permute-start.60 = (bf16[192,2048]{1,0:T(8,128)(2,1)}, bf16[192,2048]{1,0:T(8,128)(2,1)}, u32[]{:S(2)}, u32[]{:S(2)}) collective-permute-start(bf16[192,2048]{1,0:T(8,128)(2,1)} %pad_maximum_fusion.6), channel_id=1, source_target_pairs={{0,1},{1,0},{2,3},{3,2},{4,5},{5,4},{6,7},{7,6},{8,9},{9,8},{10,11... | collective-permute-start | bytes 2359304 | tf_op jit(solution)/shard_map/ppermute | solution.py:241
  662.4 74.6 %collective-permute-start.107 = (bf16[256,384]{1,0:T(8,128)(2,1)}, bf16[256,384]{1,0:T(8,128)(2,1)}, u32[]{:S(2)}, u32[]{:S(2)}) collective-permute-start(bf16[256,384]{1,0:T(8,128)(2,1)} %get-tuple-element.57), channel_id=1, source_target_pairs={{0,4},{1,5},{2,6},{3,7},{4,0},{5,1},{6,2},{7,3},{8,12},{9,13},{10,... | collective-permute-start | bytes 589832 | tf_op jit(solution)/shard_map/ppermute | solution.py:241
  663.3 92.4 %collective-permute-start.106 = (bf16[256,384]{1,0:T(8,128)(2,1)}, bf16[256,384]{1,0:T(8,128)(2,1)}, u32[]{:S(2)}, u32[]{:S(2)}) collective-permute-start(bf16[256,384]{1,0:T(8,128)(2,1)} %get-tuple-element.58), channel_id=1, source_target_pairs={{0,4},{1,5},{2,6},{3,7},{4,0},{5,1},{6,2},{7,3},{8,12},{9,13},{10,... | collective-permute-start | bytes 589832 | tf_op jit(solution)/shard_map/ppermute | solution.py:241
  664.4 72.7 %collective-permute-start.104 = (bf16[256,384]{1,0:T(8,128)(2,1)}, bf16[256,384]{1,0:T(8,128)(2,1)}, u32[]{:S(2)}, u32[]{:S(2)}) collective-permute-start(bf16[256,384]{1,0:T(8,128)(2,1)} %get-tuple-element.59), channel_id=1, source_target_pairs={{0,4},{1,5},{2,6},{3,7},{4,0},{5,1},{6,2},{7,3},{8,12},{9,13},{10,... | collective-permute-start | bytes 589832 | tf_op jit(solution)/shard_map/ppermute | solution.py:241
  (209 other events, 3690.3 us)
Sparse Core Ops, SparseCore 0:
  802.7 31.5 all-reduce.7

commit v2 on v1

--- a/solution.py
+++ b/solution.py
@@ -200,6 +200,346 @@
     )(counts, slots, parity, queries, d_out, logs, delta, keyvalues)
 
 
+class Place:
+    def __init__(self, lines):
+        rank, part = lax.axis_index("dp"), lax.axis_index("tensor")
+        self.lines = lines
+        self.z, self.y = rank // lines, lax.rem(rank, lines)
+        self.x, self.c = part // 2, lax.rem(part, 2)
+        self.quarter = self.c * 2 + self.x
+
+    def plane(self, move):
+        if move == 0:
+            return self.z
+        if move == 1:
+            return self.z + 1 - 2 * lax.rem(self.z, 2)
+        if move == 2:
+            return self.z + 2 - 4 * (self.z // 2)
+        return 3 - self.z
+
+    def to(self, kz=0, ky=0, kx=0, kc=0):
+        y = 1 - self.y if ky else self.y
+        x = 1 - self.x if kx else self.x
+        c = 1 - self.c if kc else self.c
+        return (self.plane(kz) * self.lines + y, x * 2 + c)
+
+
+class Links:
+    def __init__(self, place, send_sems, recv_sems):
+        self.place, self.send_sems, self.recv_sems = place, send_sems, recv_sems
+        self.started = []
+
+    def greet(self, moves):
+        barrier = pltpu.get_barrier_semaphore()
+        for move in moves:
+            pl.semaphore_signal(
+                barrier, inc=1, device_id=self.place.to(**move), device_id_type=pl.DeviceIdType.MESH
+            )
+        pl.semaphore_wait(barrier, len(moves))
+
+    def send(self, source, target, **move):
+        number = len(self.started)
+        copy = pltpu.make_async_remote_copy(
+            src_ref=source,
+            dst_ref=target,
+            send_sem=self.send_sems.at[number],
+            recv_sem=self.recv_sems.at[number],
+            device_id=self.place.to(**move),
+            device_id_type=pl.DeviceIdType.MESH,
+        )
+        copy.start()
+        self.started.append(copy)
+        return copy
+
+    def finish(self):
+        for copy in self.started:
+            copy.wait_send()
+
+
+def rows_at(index, size):
+    return pl.ds(pl.multiple_of(index * size, size), size)
+
+
+MIDDLE_COPIES = 50
+
+
+def middle_kernel(
+    lines,
+    slice_width,
+    attn_ref,
+    states_ref,
+    grad_ref,
+    gain_ref,
+    w_output_any,
+    w_hidden_any,
+    down_any,
+    middle_ref,
+    back_ref,
+    gain_out_ref,
+    d_heads_ref,
+    output_grad_ref,
+    mixed_ref,
+    collected_ref,
+    w_output_ref,
+    w_hidden_ref,
+    down_ref,
+    ffn_ref,
+    d_hidden_ref,
+    partial_ref,
+    core_out,
+    core_in,
+    x_out,
+    x_in,
+    sums_ref,
+    z_out,
+    z_in,
+    y_out,
+    y_in,
+    blocks_ref,
+    g_out,
+    local_sems,
+    send_sems,
+    recv_sems,
+):
+    here = Place(lines)
+    links = Links(here, send_sems, recv_sems)
+    quarter, width = middle_ref.shape
+    half = 2 * quarter
+    token_rows = 4 * quarter
+    hidden = slice_width
+
+    loads = [
+        pltpu.make_async_copy(w_output_any, w_output_ref, local_sems.at[0]),
+        pltpu.make_async_copy(w_hidden_any, w_hidden_ref, local_sems.at[1]),
+        pltpu.make_async_copy(down_any, down_ref, local_sems.at[2]),
+    ]
+    for load in loads:
+        load.start()
+    links.greet([dict(kc=1), dict(kx=1), dict(ky=1), dict(kz=1), dict(kz=2), dict(kz=3)])
+    mine = rows_at(here.quarter, quarter)
+    my_half, other_half = rows_at(here.c, half), rows_at(1 - here.c, half)
+
+    loads[0].wait()
+    cut = 4
+    piece = width // cut
+    core_copies = []
+    for part in range(cut):
+        columns = slice(part * piece, (part + 1) * piece)
+        weight = w_output_ref[columns, :]
+        core_out[4, :, columns] = by_cols(attn_ref[other_half, :], weight).astype(BF16)
+        core_copies.append(
+            links.send(core_out.at[4, :, columns], core_in.at[4, :, columns], kc=1)
+        )
+        partial_ref[0, :half, columns] = by_cols(attn_ref[my_half, :], weight)
+    x_copies = []
+    x_mine, x_other = rows_at(here.x, quarter), rows_at(1 - here.x, quarter)
+    for part in range(cut):
+        columns = slice(part * piece, (part + 1) * piece)
+        core_copies[part].wait_recv()
+        x_out[4, :, columns] = (
+            partial_ref[0, x_other, columns] + core_in[4, x_other, columns].astype(F32)
+        ).astype(BF16)
+        x_copies.append(links.send(x_out.at[4, :, columns], x_in.at[4, :, columns], kx=1))
+        middle_ref[:, columns] = (
+            states_ref[mine, columns].astype(F32)
+            + partial_ref[0, x_mine, columns]
+            + core_in[4, x_mine, columns].astype(F32)
+        )
+    for part in range(cut):
+        columns = slice(part * piece, (part + 1) * piece)
+        x_copies[part].wait_recv()
+        middle_ref[:, columns] += x_in[4, :, columns].astype(F32)
+    middle = middle_ref[...]
+    inverse = lax.rsqrt(jnp.mean(middle * middle, axis=-1, keepdims=True) + EPSILON)
+    ffn_ref[here.z, mine, :] = (middle * inverse * gain_ref[...]).astype(BF16)
+
+    def block_of(move):
+        return ffn_ref.at[here.plane(move), mine]
+
+    far = links.send(block_of(0), block_of(0), kz=2)
+    near = links.send(block_of(0), block_of(0), kz=1)
+    across = {0: links.send(block_of(0), block_of(0), kx=1)}
+    near.wait_recv()
+    across[1] = links.send(block_of(1), block_of(1), kx=1)
+    far.wait_recv()
+    corner = links.send(block_of(2), block_of(2), kz=1)
+    across[2] = links.send(block_of(2), block_of(2), kx=1)
+    cores = {}
+
+    def spread(move):
+        across[move].wait_recv()
+        both = ffn_ref.at[here.plane(move), my_half]
+        cores[move] = links.send(both, both, kc=1)
+
+    spread(0)
+    loads[1].wait()
+    loads[2].wait()
+    core_copies, x_copies = [], []
+
+    def add_cores(move):
+        core_copies[move].wait_recv()
+        total_rows = rows_at(here.c * 2 + 1 - here.x, quarter)
+        x_out[move] = (
+            partial_ref[move % 2, total_rows, :] + core_in[move, x_other, :].astype(F32)
+        ).astype(BF16)
+        x_copies.append(links.send(x_out.at[move], x_in.at[move], kx=1))
+        sums_ref[move] = partial_ref[move % 2, mine, :] + core_in[move, x_mine, :].astype(F32)
+
+    def add_x(move):
+        x_copies[move].wait_recv()
+        sums_ref[move] += x_in[move].astype(F32)
+
+    order = (0, 1, 2, 3)
+    for index, move in enumerate(order):
+        if move < 3:
+            if move == 2:
+                corner.wait_recv()
+                across[3] = links.send(block_of(3), block_of(3), kx=1)
+        cores[move].wait_recv()
+        plane = here.plane(move)
+        chunk = ffn_ref[plane]
+        gate_pre = by_cols(w_hidden_ref[:hidden, :], chunk)
+        up_pre = by_cols(w_hidden_ref[hidden : 2 * hidden, :], chunk)
+        sigmoid_gate = 1.0 / (1.0 + jnp.exp(-gate_pre))
+        silu = gate_pre * sigmoid_gate
+        columns = pl.ds(pl.multiple_of(plane * token_rows, token_rows), token_rows)
+        mixed_ref[:, columns] = (silu * up_pre).astype(BF16)
+        d_mixed = by_cols(w_hidden_ref[2 * hidden :, :], down_ref[plane])
+        d_hidden_ref[:hidden, columns] = (
+            d_mixed * up_pre * sigmoid_gate * (1.0 + gate_pre * (1.0 - sigmoid_gate))
+        ).astype(BF16)
+        d_hidden_ref[hidden:, columns] = (d_mixed * silu).astype(BF16)
+        partial_ref[move % 2] = by_rows(d_hidden_ref[:, columns], w_hidden_ref[: 2 * hidden, :])
+        core_out[move] = partial_ref[move % 2, other_half, :].astype(BF16)
+        core_copies.append(links.send(core_out.at[move], core_in.at[move], kc=1))
+        if index > 0:
+            add_cores(order[index - 1])
+        if move + 1 < 4:
+            spread(move + 1)
+    add_cores(3)
+
+    weight_rows = width // (4 * lines)
+
+    def gradient(move, line):
+        rank = here.plane(move) * lines + line
+        columns = pl.ds(pl.multiple_of(rank * weight_rows, weight_rows), weight_rows)
+        first = jnp.zeros((2 * hidden, weight_rows), F32)
+        second = jnp.zeros((hidden, weight_rows), F32)
+        for plane in range(4):
+            tokens = slice(plane * token_rows, (plane + 1) * token_rows)
+            first += product(d_hidden_ref[:, tokens], ffn_ref[plane, :, columns])
+            second += product(mixed_ref[:, tokens], down_ref[plane, :, columns])
+        return first, second
+
+    y_copies = {}
+    for move in (3, 2, 1, 0):
+        first, second = gradient(move, 1 - here.y)
+        y_out[move, : 2 * hidden] = first.astype(BF16)
+        y_out[move, 2 * hidden :] = second.astype(BF16)
+        y_copies[move] = links.send(y_out.at[move], y_in.at[move], ky=1)
+
+    add_x(0)
+    add_x(1)
+    z_out[0] = sums_ref[1].astype(BF16)
+    z_copies = [links.send(z_out.at[0], z_in.at[0], kz=1)]
+    add_x(2)
+    add_x(3)
+    z_out[1] = sums_ref[3].astype(BF16)
+    z_copies.append(links.send(z_out.at[1], z_in.at[1], kz=1))
+    first, second = gradient(3, here.y)
+    blocks_ref[0, : 2 * hidden] = first
+    blocks_ref[0, 2 * hidden :] = second
+    z_copies[1].wait_recv()
+    z_out[2] = (sums_ref[2] + z_in[1].astype(F32)).astype(BF16)
+    z_copies.append(links.send(z_out.at[2], z_in.at[2], kz=2))
+    for slot, move in enumerate((2, 1, 0)):
+        first, second = gradient(move, here.y)
+        blocks_ref[slot + 1, : 2 * hidden] = first
+        blocks_ref[slot + 1, 2 * hidden :] = second
+    z_copies[0].wait_recv()
+    z_copies[2].wait_recv()
+    d_normed = sums_ref[0] + z_in[0].astype(F32) + z_in[2].astype(F32)
+    middle = middle_ref[...]
+    inverse = lax.rsqrt(jnp.mean(middle * middle, axis=-1, keepdims=True) + EPSILON)
+    unit = middle * inverse
+    gain_out_ref[...] = jnp.sum(d_normed * unit, axis=0, keepdims=True)
+    scaled = d_normed * gain_ref[...]
+    back = inverse * (scaled - unit * jnp.mean(scaled * unit, axis=-1, keepdims=True))
+    grad_middle = grad_ref[mine, :].astype(F32) + back
+    back_ref[...] = grad_middle
+    output_grad_ref[mine, :] = grad_middle.astype(BF16)
+    block = output_grad_ref.at[mine]
+    links.send(block, block, kx=1).wait_recv()
+    both = output_grad_ref.at[my_half]
+    core = links.send(both, both, kc=1)
+
+    g_copies = []
+    for slot, move in enumerate((3, 2, 1, 0)):
+        y_copies[move].wait_recv()
+        total = blocks_ref[slot] + y_in[move].astype(F32)
+        if move:
+            g_out[slot] = total.astype(BF16)
+            g_copies.append(links.send(g_out.at[slot], collected_ref.at[here.z], kz=move))
+        else:
+            collected_ref[here.z] = total.astype(BF16)
+    core.wait_recv()
+    d_heads_ref[...] = product(output_grad_ref[...], w_output_ref[...]).astype(BF16)
+    for copy in g_copies:
+        copy.wait_recv()
+    links.finish()
+
+
+def middle(lines, slice_width, attn_out, states, out_grad, gain, w_output, w_hidden, down_grads):
+    token_rows, width = states.shape
+    quarter = token_rows // 4
+    half = 2 * quarter
+    hidden = slice_width
+    weight_rows = width // (4 * lines)
+    vmem = pl.BlockSpec(memory_space=pltpu.VMEM)
+    hbm = pl.BlockSpec(memory_space=pl.ANY)
+    shape = jax.ShapeDtypeStruct
+    return pl.pallas_call(
+        functools.partial(middle_kernel, lines, slice_width),
+        out_shape=(
+            shape((quarter, width), F32),
+            shape((quarter, width), F32),
+            shape((1, width), F32),
+            shape(attn_out.shape, BF16),
+            shape((token_rows, width), BF16),
+            shape((hidden, 4 * token_rows), BF16),
+            shape((4, 3 * hidden, weight_rows), BF16),
+        ),
+        in_specs=[vmem] * 4 + [hbm] * 3,
+        out_specs=(vmem,) * 7,
+        scratch_shapes=[
+            pltpu.VMEM(w_output.shape, BF16),
+            pltpu.VMEM(w_hidden.shape, BF16),
+            pltpu.VMEM(down_grads.shape, BF16),
+            pltpu.VMEM((4, token_rows, width), BF16),
+            pltpu.VMEM((2 * hidden, 4 * token_rows), BF16),
+            pltpu.VMEM((2, token_rows, width), F32),
+            pltpu.VMEM((5, half, width), BF16),
+            pltpu.VMEM((5, half, width), BF16),
+            pltpu.VMEM((5, quarter, width), BF16),
+            pltpu.VMEM((5, quarter, width), BF16),
+            pltpu.VMEM((4, quarter, width), F32),
+            pltpu.VMEM((3, quarter, width), BF16),
+            pltpu.VMEM((3, quarter, width), BF16),
+            pltpu.VMEM((4, 3 * hidden, weight_rows), BF16),
+            pltpu.VMEM((4, 3 * hidden, weight_rows), BF16),
+            pltpu.VMEM((4, 3 * hidden, weight_rows), F32),
+            pltpu.VMEM((3, 3 * hidden, weight_rows), BF16),
+            pltpu.SemaphoreType.DMA((3,)),
+            pltpu.SemaphoreType.DMA((MIDDLE_COPIES,)),
+            pltpu.SemaphoreType.DMA((MIDDLE_COPIES,)),
+        ],
+        compiler_params=pltpu.CompilerParams(
+            collective_id=0, has_side_effects=True, vmem_limit_bytes=62 << 20
+        ),
+        name="middle",
+    )(attn_out, states, out_grad, gain, w_output, w_hidden, down_grads)
+
+
 def local(
     states,
     query_weight,
@@ -230,6 +570,7 @@
     hidden = gate_weight.shape[2]
     slice_width = hidden // PLANES
     weight_rows = width // dp_ranks
+    kernels = lines == 2 and weight_rows % 128 == 0 and tensor_ranks == 4
 
     def send(value, kz=0, ky=0, kx=0, kc=0):
         move_rank, move_part = kz * lines + ky, kx * 2 + kc
@@ -284,20 +625,21 @@
         both = jnp.concatenate([block, send(block, kx=1)], axis=0)
         return jnp.concatenate([both, send(both, kc=1)], axis=0)
 
+    def first_row(move):
+        other = part ^ move
+        return (other % 2 * 2 + other // 2) * quarter
+
     def in_order(blocks):
         whole = jnp.zeros_like(blocks)
         for index, move in enumerate((0, 2, 1, 3)):
             whole = lax.dynamic_update_slice_in_dim(
-                whole,
-                blocks[index * quarter : (index + 1) * quarter],
-                (part ^ move) * quarter,
-                0,
+                whole, blocks[index * quarter : (index + 1) * quarter], first_row(move), 0
             )
         return whole
 
     def quarters(value):
         return [
-            lax.dynamic_slice_in_dim(value, (part ^ move) * quarter, quarter, 0)
+            lax.dynamic_slice_in_dim(value, first_row(move), quarter, 0)
             for move in range(tensor_ranks)
         ]
 
@@ -323,38 +665,50 @@
     w_attend = gather_dp(jnp.concatenate([query_weight[0], *kv_columns], axis=1)).reshape(width, -1)
     w_output = gather_dp(output_weight[0]).reshape(width, head_width)
 
+    def turned(weight):
+        pieces = weight[0].reshape(weight_rows, PLANES, slice_width)
+        return pieces.transpose(1, 2, 0)
+
     def sliced(weight):
         return weight[0].reshape(weight_rows, PLANES, slice_width).transpose(1, 0, 2)
 
     pad_first = -2 * slice_width % 128
     pad_second = -slice_width % 128
-    packed = jnp.concatenate(
-        [
-            sliced(gate_weight),
-            sliced(up_weight),
-            jnp.zeros((PLANES, weight_rows, pad_first), BF16),
-            sliced(down_weight),
-            jnp.zeros((PLANES, weight_rows, pad_second), BF16),
-        ],
-        axis=2,
-    )
-    w_hidden = jnp.zeros((dp_ranks, weight_rows, packed.shape[2]), BF16)
+    if kernels:
+        packed = jnp.concatenate(
+            [turned(gate_weight), turned(up_weight), turned(down_weight)], axis=1
+        )
+    else:
+        packed = jnp.concatenate(
+            [
+                sliced(gate_weight),
+                sliced(up_weight),
+                jnp.zeros((PLANES, weight_rows, pad_first), BF16),
+                sliced(down_weight),
+                jnp.zeros((PLANES, weight_rows, pad_second), BF16),
+            ],
+            axis=2,
+        )
+    w_hidden = jnp.zeros((dp_ranks, *packed.shape[1:]), BF16)
     for kz in range(PLANES):
         piece = lax.dynamic_index_in_dim(packed, plane ^ kz, 0, keepdims=False)
         piece = send(piece, kz=kz) if kz else piece
         for ky in range(lines):
             got = send(piece, ky=ky) if ky else piece
             w_hidden = lax.dynamic_update_index_in_dim(w_hidden, got, rank ^ (kz * lines + ky), 0)
-    w_hidden = w_hidden.reshape(width, -1)
-    down_start = 2 * slice_width + pad_first
-    w_gate_up = w_hidden[:, : 2 * slice_width]
-    w_down = w_hidden[:, down_start : down_start + slice_width]
+    if kernels:
+        w_hidden = w_hidden.transpose(1, 0, 2).reshape(3 * slice_width, width)
+    else:
+        w_hidden = w_hidden.reshape(width, -1)
+        down_start = 2 * slice_width + pad_first
+        w_gate_up = w_hidden[:, : 2 * slice_width]
+        w_down = w_hidden[:, down_start : down_start + slice_width]
 
     def gather_group(block):
         return [gather_tensor(piece) for piece in gather_planes(block)]
 
     def quarter_of(value):
-        return lax.dynamic_slice_in_dim(value, part * quarter, quarter, 0)
+        return lax.dynamic_slice_in_dim(value, first_row(0), quarter, 0)
 
     query_g, key_g = query_gain[0], key_gain[0]
     attn_in = rounded(normed(states.astype(F32), gains[0]))
@@ -394,34 +748,6 @@
     attn_out = rounded(from_pairs(attended[..., :HEAD_WIDTH]).reshape(token_rows, head_width))
     logs = attended[..., HEAD_WIDTH]
 
-    branch = scatter_tensor(quarters(by_cols(attn_out, w_output)))
-    states_quarter = quarter_of(states).astype(F32)
-    middle = states_quarter + branch
-    ffn_in = rounded(normed(middle, gains[1]))
-
-    down_grads = gather_group(quarter_of(out_grad))
-    ffn_ins = gather_group(ffn_in)
-    mixed_chunks, d_chunks, back_parts, out_parts = [], [], [], []
-    for down_grad, ffn_chunk in zip(down_grads, ffn_ins):
-        gate_up = product(ffn_chunk, w_gate_up)
-        gate_pre, up_pre = gate_up[:, :slice_width], gate_up[:, slice_width:]
-        sigmoid_gate = jax.nn.sigmoid(gate_pre)
-        mixed = rounded(gate_pre * sigmoid_gate * up_pre)
-        d_mixed = product(down_grad, w_down)
-        d_gate = d_mixed * up_pre * sigmoid_gate * (1.0 + gate_pre * (1.0 - sigmoid_gate))
-        d_up = d_mixed * gate_pre * sigmoid_gate
-        d_gate_up = jnp.concatenate([rounded(d_gate), rounded(d_up)], axis=1)
-        mixed_chunks.append(mixed)
-        d_chunks.append(d_gate_up)
-
-        def reduced(value):
-            blocks = value.reshape(4, quarter, width)
-            return scatter_tensor([blocks[0], blocks[2], blocks[1], blocks[3]])
-
-        back_parts.append(reduced(by_cols(d_gate_up, w_gate_up)))
-        out_parts.append(reduced(by_cols(mixed, w_down)))
-    d_ffn_in = scatter_planes(back_parts)
-
     def norm_back(vector, gain_vector, grad):
         inverse = lax.rsqrt(jnp.mean(vector * vector, axis=-1, keepdims=True) + EPSILON)
         unit = vector * inverse
@@ -429,13 +755,62 @@
         back = inverse * (scaled - unit * jnp.mean(scaled * unit, axis=-1, keepdims=True))
         return back, jnp.sum(grad * unit, axis=0)
 
-    d_middle, d_gain_ffn = norm_back(middle, gains[1], d_ffn_in)
-    grad_middle = quarter_of(out_grad).astype(F32) + d_middle
-    output_grad = in_order(gather_tensor(rounded(grad_middle)))
-
-    d_wout = by_rows(output_grad, attn_out)
-    d_heads = rounded(product(output_grad, w_output)).reshape(token_rows, heads_here, HEAD_WIDTH)
-    d_pairs = to_pairs(d_heads)
+
+    def planes_in_order(chunks):
+        whole = jnp.zeros((PLANES, *chunks[0].shape), chunks[0].dtype)
+        for kz, chunk in enumerate(chunks):
+            whole = lax.dynamic_update_index_in_dim(whole, chunk, plane ^ kz, 0)
+        return whole
+
+    states_quarter = quarter_of(states).astype(F32)
+    down_grads = gather_group(quarter_of(out_grad))
+    if kernels:
+        down_all = planes_in_order([in_order(chunk) for chunk in down_grads])
+        middle_rows, grad_middle, d_gain_ffn, d_heads, output_grad, mixed, collected = middle(
+            lines, slice_width, attn_out, states, out_grad, gains[1:], w_output, w_hidden, down_all
+        )
+        d_gain_ffn = d_gain_ffn[0]
+        d_wout = by_rows(output_grad, attn_out)
+        out_parts = []
+        for kz in range(PLANES):
+            chunk = lax.dynamic_slice_in_dim(
+                mixed, (plane ^ kz) * token_rows, token_rows, 1
+            )
+            out_parts.append(scatter_tensor(quarters(by_rows(chunk, w_hidden[2 * slice_width :]))))
+    else:
+        branch = scatter_tensor(quarters(by_cols(attn_out, w_output)))
+        middle_rows = states_quarter + branch
+        ffn_in = rounded(normed(middle_rows, gains[1]))
+
+        ffn_ins = gather_group(ffn_in)
+        mixed_chunks, d_chunks, back_parts, out_parts = [], [], [], []
+        for down_grad, ffn_chunk in zip(down_grads, ffn_ins):
+            gate_up = product(ffn_chunk, w_gate_up)
+            gate_pre, up_pre = gate_up[:, :slice_width], gate_up[:, slice_width:]
+            sigmoid_gate = jax.nn.sigmoid(gate_pre)
+            mixed = rounded(gate_pre * sigmoid_gate * up_pre)
+            d_mixed = product(down_grad, w_down)
+            d_gate = d_mixed * up_pre * sigmoid_gate * (1.0 + gate_pre * (1.0 - sigmoid_gate))
+            d_up = d_mixed * gate_pre * sigmoid_gate
+            d_gate_up = jnp.concatenate([rounded(d_gate), rounded(d_up)], axis=1)
+            mixed_chunks.append(mixed)
+            d_chunks.append(d_gate_up)
+
+            def reduced(value):
+                blocks = value.reshape(4, quarter, width)
+                return scatter_tensor([blocks[0], blocks[2], blocks[1], blocks[3]])
+
+            back_parts.append(reduced(by_cols(d_gate_up, w_gate_up)))
+            out_parts.append(reduced(by_cols(mixed, w_down)))
+        d_ffn_in = scatter_planes(back_parts)
+
+        d_middle, d_gain_ffn = norm_back(middle_rows, gains[1], d_ffn_in)
+        grad_middle = quarter_of(out_grad).astype(F32) + d_middle
+        output_grad = in_order(gather_tensor(rounded(grad_middle)))
+        d_wout = by_rows(output_grad, attn_out)
+        d_heads = rounded(product(output_grad, w_output))
+
+    d_pairs = to_pairs(d_heads.reshape(token_rows, heads_here, HEAD_WIDTH))
     delta = jnp.sum(d_pairs.astype(F32) * attended[..., :HEAD_WIDTH], axis=-1)
     d_query, d_keyvalue = attend_back(
         counts,
@@ -459,30 +834,35 @@
 
     d_wattend = scatter_dp(by_rows(attn_in, d_lin).reshape(dp_ranks, weight_rows, -1))
     d_wout = scatter_dp(d_wout.reshape(dp_ranks, weight_rows, -1))
-    ffn_all = jnp.concatenate(ffn_ins, axis=0)
-    down_all = jnp.concatenate(down_grads, axis=0)
-    grads_hidden = jnp.concatenate(
-        [
-            by_rows(ffn_all, jnp.concatenate(d_chunks, axis=0)),
-            by_rows(down_all, jnp.concatenate(mixed_chunks, axis=0)),
-        ],
-        axis=1,
-    ).reshape(dp_ranks, weight_rows, 3 * slice_width)
-    collected = jnp.zeros((PLANES, weight_rows, 3 * slice_width), F32)
-    for kz in range(PLANES):
-        total = lax.dynamic_index_in_dim(grads_hidden, rank ^ (kz * lines), 0, keepdims=False)
-        for ky in range(1, lines):
-            piece = lax.dynamic_index_in_dim(
-                grads_hidden, rank ^ (kz * lines + ky), 0, keepdims=False
-            )
-            total = total + send(rounded(piece), ky=ky).astype(F32)
-        if kz:
-            total = send(rounded(total), kz=kz).astype(F32)
-        collected = lax.dynamic_update_index_in_dim(collected, total, plane ^ kz, 0)
+    if not kernels:
+        ffn_all = jnp.concatenate(ffn_ins, axis=0)
+        down_all = jnp.concatenate(down_grads, axis=0)
+        grads_hidden = jnp.concatenate(
+            [
+                by_rows(ffn_all, jnp.concatenate(d_chunks, axis=0)),
+                by_rows(down_all, jnp.concatenate(mixed_chunks, axis=0)),
+            ],
+            axis=1,
+        ).reshape(dp_ranks, weight_rows, 3 * slice_width)
+        collected = jnp.zeros((PLANES, weight_rows, 3 * slice_width), F32)
+        for kz in range(PLANES):
+            total = lax.dynamic_index_in_dim(grads_hidden, rank ^ (kz * lines), 0, keepdims=False)
+            for ky in range(1, lines):
+                piece = lax.dynamic_index_in_dim(
+                    grads_hidden, rank ^ (kz * lines + ky), 0, keepdims=False
+                )
+                total = total + send(rounded(piece), ky=ky).astype(F32)
+            if kz:
+                total = send(rounded(total), kz=kz).astype(F32)
+            collected = lax.dynamic_update_index_in_dim(collected, total, plane ^ kz, 0)
 
     def unsliced(index):
-        piece = collected[:, :, index * slice_width : (index + 1) * slice_width]
-        return piece.transpose(1, 0, 2).reshape(1, weight_rows, hidden)
+        columns = slice(index * slice_width, (index + 1) * slice_width)
+        if kernels:
+            piece = collected[:, columns].transpose(2, 0, 1).astype(F32)
+        else:
+            piece = collected[:, :, columns].transpose(1, 0, 2)
+        return piece.reshape(1, weight_rows, hidden)
 
     kv_grad = d_wattend[:, head_width:]
     spread = jnp.zeros((weight_rows, 2 * value_start), F32)
@@ -492,7 +872,7 @@
     )
     d_wkeyvalue = lax.psum(spread, "tensor")
 
-    result_quarter = rounded(middle + scatter_planes(out_parts))
+    result_quarter = rounded(middle_rows + scatter_planes(out_parts))
     result = in_order(gather_tensor(result_quarter))
 
     small = jnp.concatenate([d_gain_attn, d_gain_ffn, d_querygain, d_keygain])

time: 869 us -> 880 us (1.013)
  Pallas kernels: 39.6 us -> 206 us
  waiting for transfers between devices: 333 us -> 177 us
  local copies, waits for them, and re-layouts: 154 us -> 290 us
  matrix products: 85.1 us -> 14.6 us
  starting transfers between devices: 132 us -> 86.3 us
  other arithmetic: 58.1 us -> 36.2 us
    pallas_call x0 -> x1, Pallas kernels: none -> 167 us  [middle(): pl.pallas_call(functools.partial(middle_kernel, lines, slice_width), out_...]
    ppermute x117 -> x84, waiting for transfers between devices: 332 us -> 177 us  [send(): return lax.ppermute(value, ('dp', 'tensor'), pairs)]
    dynamic_update_slice x8, local copies, waits for them, and re-layouts: 12.9 us -> 166 us  [local(): lax.dynamic_update_index_in_dim(w_hidden, got, rank ^ kz * lines + ky, 0)]
    ppermute x117 -> x84, starting transfers between devices: 132 us -> 86.3 us  [send(): return lax.ppermute(value, ('dp', 'tensor'), pairs)]
    dot_general x10 -> x1, matrix products: 31.1 us -> 3.29 us  [by_cols(): lax.dot_general(left_side, right_side, (((1,), (1,)), ((), ())), preferre...]
    dot_general x10 -> x1, matrix products: 30.3 us -> 3.17 us  [product(): return jnp.dot(left_side, right_side, preferred_element_type=F32)]
    unnamed x266 -> x150, local copies, waits for them, and re-layouts: 46.6 us -> 22.3 us
    broadcast_in_dim x2 -> x21, local copies, waits for them, and re-layouts: 2.9 us -> 20.1 us  [the longest x7 11.5 us: local(): lax.dynamic_update_index_in_dim(w_hidden, got, rank ^ kz * lines + ky, 0)]
  transfers between devices with their start and end apart: 118 -> 85, of which waited for: 53 -> 28; matrix products, arithmetic and copies ran while one was open for 34% -> 37% of each run, Pallas kernels for 5% -> 2%
where the time goes in v2:
time: 880 us; the launch traced here: 864 us
  local copies, waits for them, and re-layouts  290 us (33%)
  Pallas kernels  206 us (23%)
  waiting for transfers between devices  177 us (20%)
  starting transfers between devices  86.3 us (10%)
  blocking collectives  37 us (4%)
  other arithmetic  36.2 us (4%)
  between operations  16.3 us (2%)
  matrix products  14.6 us (2%)
    ppermute x84, waiting for transfers between devices, send(): return lax.ppermute(value, ('dp', 'tensor'), pairs)  177 us
    pallas_call x1, Pallas kernels, middle(): pl.pallas_call(functools.partial(middle_kernel, lines, slice_width), out_...  167 us
    dynamic_update_slice x8, local copies, waits for them, and re-layouts, local(): lax.dynamic_update_index_in_dim(w_hidden, got, rank ^ kz * lines + ky, 0)  166 us
    ppermute x84, starting transfers between devices, send(): return lax.ppermute(value, ('dp', 'tensor'), pairs)  86.3 us
    psum x1, blocking collectives, local(): small = lax.psum(small, ('dp', 'tensor'))  37 us
    pallas_call x1, Pallas kernels, attend_back(): pl.pallas_call(attend_back_kernel, out_shape=(jax.ShapeDtypeStruct((block...  26.6 us
    unnamed x150, local copies, waits for them, and re-layouts  22.3 us
    dynamic_update_slice x22, local copies, waits for them, and re-layouts, in_order(): lax.dynamic_update_slice_in_dim(whole, blocks[index * quarter:(index + 1)...  22.1 us
  transfers between devices with their start and end apart: 85, of which 28 were waited for; matrix products, arithmetic and copies ran while one was open for 37% of the time, Pallas kernels for 2%

profile of v2, /device:TPU:0, one launch (start us, length us, event | category | flops | bytes accessed | tf_op | source)
XLA Modules:
  0.0 863.9 jit_solution(16356465868497858927)
XLA Ops:
  35.2 20.8 %dynamic_update_slice.264 = bf16[8,912,256]{2,0,1:T(8,128)(2,1)} dynamic-update-slice(bf16[8,912,256]{2,0,1:T(8,128)(2,1)} %broadcast_in_dim.272, bf16[1,912,256]{2,0,1:T(2,128)(2,1)} %copy.92, s32[]{:T(128)S(6)} %select_n.366, s32[]{:T(128)} %constant.490.clone.1, s32[]{:T(128)} %constant.490.clone.1) | dynamic-update-slice | bytes 933892 | tf_op jit(solution)/shard_map/jit(dynamic_update_index_in_dim)/dynamic_update_slice | solution.py:698
  70.3 10.6 %collective-permute-done.22 = bf16[256,384]{1,0:T(8,128)(2,1)} collective-permute-done((bf16[256,384]{1,0:T(8,128)(2,1)S(1)}, bf16[256,384]{1,0:T(8,128)(2,1)}, u32[]{:S(2)}, u32[]{:S(2)}) %collective-permute-start.22) | collective-permute-done | bytes 196640 | tf_op jit(solution)/shard_map/ppermute | solution.py:582
  84.2 8.1 collective-permute-done.8
  119.1 18.7 %collective-permute-done.26 = bf16[256,384]{1,0:T(8,128)(2,1)S(1)} collective-permute-done((bf16[256,384]{1,0:T(8,128)(2,1)S(1)}, bf16[256,384]{1,0:T(8,128)(2,1)S(1)}, u32[]{:S(2)}, u32[]{:S(2)}) %collective-permute-start.26) | collective-permute-done | bytes 196640 | tf_op jit(solution)/shard_map/ppermute | solution.py:582
  147.3 20.8 %dynamic_update_slice.265 = bf16[8,912,256]{2,0,1:T(8,128)(2,1)} dynamic-update-slice(bf16[8,912,256]{2,0,1:T(8,128)(2,1)} %dynamic_update_slice.264, bf16[1,912,256]{2,0,1:T(2,128)(2,1)} %copy.93, s32[]{:T(128)S(6)} %select_n.367, s32[]{:T(128)} %constant.490.clone.1, s32[]{:T(128)} %constant.490.clone.1) | dynamic-update-slice | bytes 933892 | tf_op jit(solution)/shard_map/jit(dynamic_update_index_in_dim)/dynamic_update_slice | solution.py:698
  168.1 20.8 %dynamic_update_slice.266 = bf16[8,912,256]{2,0,1:T(8,128)(2,1)} dynamic-update-slice(bf16[8,912,256]{2,0,1:T(8,128)(2,1)} %dynamic_update_slice.265, bf16[1,912,256]{2,0,1:T(2,128)(2,1)} %copy.94, s32[]{:T(128)S(6)} %select_n.368, s32[]{:T(128)} %constant.490.clone.1, s32[]{:T(128)} %constant.490.clone.1) | dynamic-update-slice | bytes 933892 | tf_op jit(solution)/shard_map/jit(dynamic_update_index_in_dim)/dynamic_update_slice | solution.py:698
  218.3 6.1 collective-permute-done.32
  226.0 8.4 collective-permute-done.34
  236.6 20.8 %dynamic_update_slice.267 = bf16[8,912,256]{2,0,1:T(8,128)(2,1)} dynamic-update-slice(bf16[8,912,256]{2,0,1:T(8,128)(2,1)} %dynamic_update_slice.266, bf16[1,912,256]{2,0,1:T(2,128)(2,1)} %copy.95, s32[]{:T(128)S(6)} %select_n.369, s32[]{:T(128)} %constant.490.clone.1, s32[]{:T(128)} %constant.490.clone.1) | dynamic-update-slice | bytes 933892 | tf_op jit(solution)/shard_map/jit(dynamic_update_index_in_dim)/dynamic_update_slice | solution.py:698
  257.4 20.8 %dynamic_update_slice.268 = bf16[8,912,256]{2,0,1:T(8,128)(2,1)} dynamic-update-slice(bf16[8,912,256]{2,0,1:T(8,128)(2,1)} %dynamic_update_slice.267, bf16[1,912,256]{2,0,1:T(2,128)(2,1)} %copy.96, s32[]{:T(128)S(6)} %select_n.370, s32[]{:T(128)} %constant.490.clone.1, s32[]{:T(128)} %constant.490.clone.1) | dynamic-update-slice | bytes 933892 | tf_op jit(solution)/shard_map/jit(dynamic_update_index_in_dim)/dynamic_update_slice | solution.py:698
  278.2 20.8 %dynamic_update_slice.269 = bf16[8,912,256]{2,0,1:T(8,128)(2,1)} dynamic-update-slice(bf16[8,912,256]{2,0,1:T(8,128)(2,1)} %dynamic_update_slice.268, bf16[1,912,256]{2,0,1:T(2,128)(2,1)} %copy.97, s32[]{:T(128)S(6)} %select_n.371, s32[]{:T(128)} %constant.490.clone.1, s32[]{:T(128)} %constant.490.clone.1) | dynamic-update-slice | bytes 933892 | tf_op jit(solution)/shard_map/jit(dynamic_update_index_in_dim)/dynamic_update_slice | solution.py:698
  299.0 20.9 %dynamic_update_slice.270 = bf16[8,912,256]{2,0,1:T(8,128)(2,1)} dynamic-update-slice(bf16[8,912,256]{2,0,1:T(8,128)(2,1)} %dynamic_update_slice.269, bf16[1,912,256]{2,0,1:T(2,128)(2,1)} %copy.98, s32[]{:T(128)S(6)} %select_n.372, s32[]{:T(128)} %constant.490.clone.1, s32[]{:T(128)} %constant.490.clone.1) | dynamic-update-slice | bytes 933892 | tf_op jit(solution)/shard_map/jit(dynamic_update_index_in_dim)/dynamic_update_slice | solution.py:698
  319.9 20.9 %dynamic_update_slice.271 = bf16[8,912,256]{2,0,1:T(8,128)(2,1)} dynamic-update-slice(bf16[8,912,256]{2,0,1:T(8,128)(2,1)} %dynamic_update_slice.270, bf16[1,912,256]{2,0,1:T(2,128)(2,1)S(1)} %copy-done.19, s32[]{:T(128)S(6)} %select_n.373, s32[]{:T(128)} %constant.490.clone.1, s32[]{:T(128)} %constant.490.clone.1) | dynamic-update-slice | bytes 933892 | tf_op jit(solution)/shard_map/jit(dynamic_update_index_in_dim)/dynamic_update_slice | solution.py:698
  394.6 13.0 %attend.1 = f32[3,3,256,128]{3,2,1,0:T(8,128)S(1)} custom-call(s32[3]{0:T(128)S(1)} %get-tuple-element.40.count_ref, s32[3,24]{1,0:T(4,128)S(1)} %select_reduce_fusion.slots_ref, s32[1]{0:T(128)} %bitcast.parity_ref, bf16[3,3,256,64]{3,2,1,0:T(8,128)(2,1)S(1)} %bitcast.325, bf16[24,128,256]{2,1,0:T(8,128)(2,1)S(1)} %bitcast.323), custom_call_target="tpu_custom_call" | custom-call | flops 2013265920 | bytes 8388608 | tf_op jit(solution)/shard_map/attend/pallas_call | solution.py:116
  421.2 166.6 %middle.1 = (f32[96,2048]{1,0:T(8,128)}, f32[96,2048]{1,0:T(8,128)}, f32[1,2048]{1,0:T(1,128)}, bf16[384,384]{1,0:T(8,128)(2,1)}, bf16[384,2048]{1,0:T(8,128)(2,...) custom-call(bf16[384,384]{1,0:T(8,128)(2,1)} %copy.100.attn_ref, bf16[384,2048]{1,0:T(8,128)(2,1)} %states_ref.1, ...), custom_call_target="tpu_custom_call" | custom-call | tf_op jit(solution)/shard_map/middle/pallas_call | solution.py:501
  590.7 26.6 %attend_back.1 = (f32[3,3,256,64]{3,2,1,0:T(8,128)}, f32[24,128,256]{2,1,0:T(8,128)}) custom-call(s32[3]{0:T(128)} %copy-done.3, s32[3,24]{1,0:T(4,128)} %copy-done.2, s32[1]{0:T(128)} %bitcast.parity_ref, bf16[3,3,256,64]{3,2,1,0:T(8,128)(2,1)} %bitcast.326, bf16[3,3,256,64]{3,2,1,0:T(8,128)(2,1)} %bitcast.351, f32[3,3,1,256]{3,2,1,0:T(1,128)} %bitcast.387, ...), custom_call_target="tpu_custom_call" | custom-call | flops 5033164800 | bytes 8388608 | tf_op jit(solution)/shard_map/attend_back/pallas_call | solution.py:187
  655.3 6.5 collective-permute-start.64
  678.0 6.8 collective-permute-done.65
  705.2 6.2 collective-permute-done.74
  714.6 15.7 %collective-permute-done.54 = bf16[96,2048]{1,0:T(8,128)(2,1)S(1)} collective-permute-done((bf16[96,2048]{1,0:T(8,128)(2,1)S(1)}, bf16[96,2048]{1,0:T(8,128)(2,1)S(1)}, u32[]{:S(2)}, u32[]{:S(2)}) %collective-permute-start.54) | collective-permute-done | bytes 393248 | tf_op jit(solution)/shard_map/ppermute | solution.py:582
  742.2 22.8 %collective-permute-done.55 = bf16[96,2048]{1,0:T(8,128)(2,1)S(1)} collective-permute-done((bf16[96,2048]{1,0:T(8,128)(2,1)S(1)}, bf16[96,2048]{1,0:T(8,128)(2,1)S(1)}, u32[]{:S(2)}, u32[]{:S(2)}) %collective-permute-start.55) | collective-permute-done | bytes 393248 | tf_op jit(solution)/shard_map/ppermute | solution.py:582
  769.5 13.8 %collective-permute-done.76 = bf16[256,640]{1,0:T(8,128)(2,1)S(1)} collective-permute-done((bf16[256,640]{1,0:T(8,128)(2,1)S(1)}, bf16[256,640]{1,0:T(8,128)(2,1)S(1)}, u32[]{:S(2)}, u32[]{:S(2)}) %collective-permute-start.76) | collective-permute-done | bytes 327712 | tf_op jit(solution)/shard_map/ppermute | solution.py:582
  795.8 37.0 %psum.15 = f32[4224]{0:T(1024)S(1)} all-reduce(f32[4224]{0:T(1024)S(1)} %concatenate.102), channel_id=1, replica_groups=mesh['dp'=8,'tensor'=4] {'dp','tensor'}, use_global_device_ids=true, to_apply=%region_13.14 | all-reduce | flops 4224 | bytes 33792 | tf_op jit(solution)/shard_map/psum | solution.py:879
  838.1 7.1 collective-permute-done.68
  (531 shorter events, 307.1 us)
Async XLA Ops:
  7.2 846.8 %all-reduce.8.cloned.1.call-start = ((), (), s32[]{:S(2)}) async-start(), calls=%async_computation | async-start | bytes 1572864 | tf_op jit(solution)/shard_map/psum | solution.py:873
  7.2 51.4 %collective-permute-start = (bf16[2,256]{1,0:T(2,128)(2,1)}, bf16[2,256]{1,0:T(2,128)(2,1)S(1)}, u32[]{:S(2)}, u32[]{:S(2)}) collective-permute-start(bf16[2,256]{1,0:T(2,128)(2,1)} %bitcast.395), channel_id=1, source_target_pairs={{0,4},{1,5},{2,6},{3,7},{4,0},{5,1},{6,2},{7,3},{8,12},{9,13},{10,... | collective-permute-start | bytes 3080 | tf_op jit(solution)/shard_map/ppermute | solution.py:582
  10.3 46.2 %collective-permute-start.1 = (bf16[2,256]{1,0:T(2,128)(2,1)}, bf16[2,256]{1,0:T(2,128)(2,1)S(1)}, u32[]{:S(2)}, u32[]{:S(2)}) collective-permute-start(bf16[2,256]{1,0:T(2,128)(2,1)} %bitcast.396), channel_id=1, source_target_pairs={{0,8},{1,9},{2,10},{3,11},{4,12},{5,13},{6,14},{7,15},{8,0},{9,1},... | collective-permute-start | bytes 3080 | tf_op jit(solution)/shard_map/ppermute | solution.py:582
  11.8 44.2 %collective-permute-start.3 = (bf16[2,256]{1,0:T(2,128)(2,1)}, bf16[2,256]{1,0:T(2,128)(2,1)S(1)}, u32[]{:S(2)}, u32[]{:S(2)}) collective-permute-start(bf16[2,256]{1,0:T(2,128)(2,1)} %bitcast.397), channel_id=1, source_target_pairs={{0,16},{1,17},{2,18},{3,19},{4,20},{5,21},{6,22},{7,23},{8,24},{9,... | collective-permute-start | bytes 3080 | tf_op jit(solution)/shard_map/ppermute | solution.py:582
  16.2 87.1 %collective-permute-start.35 = (bf16[96,2048]{1,0:T(8,128)(2,1)}, bf16[96,2048]{1,0:T(8,128)(2,1)}, u32[]{:S(2)}, u32[]{:S(2)}) collective-permute-start(bf16[96,2048]{1,0:T(8,128)(2,1)} %constant_dynamic-slice_fusion.9), channel_id=1, source_target_pairs={{0,2},{1,3},{2,0},{3,1},{4,6},{5,7},{6,4},{7,5},{8,10},{9,11},{10,... | collective-permute-start | bytes 1179656 | tf_op jit(solution)/shard_map/ppermute | solution.py:582
  95.8 42.0 %collective-permute-start.28 = (bf16[912,256]{1,0:T(8,128)(2,1)S(1)}, bf16[912,256]{1,0:T(8,128)(2,1)S(1)}, u32[]{:S(2)}, u32[]{:S(2)}) collective-permute-start(bf16[912,256]{1,0:T(8,128)(2,1)S(1)} %bitcast.353), channel_id=1, source_target_pairs={{0,4},{1,5},{2,6},{3,7},{4,0},{5,1},{6,2},{7,3},{8,12},{9,13},{10,... | collective-permute-start | bytes 1400840 | tf_op jit(solution)/shard_map/ppermute | solution.py:582
  97.6 43.9 %collective-permute-start.29 = (bf16[912,256]{1,0:T(8,128)(2,1)S(1)}, bf16[912,256]{1,0:T(8,128)(2,1)S(1)}, u32[]{:S(2)}, u32[]{:S(2)}) collective-permute-start(bf16[912,256]{1,0:T(8,128)(2,1)S(1)} %copy-done.42), channel_id=1, source_target_pairs={{0,8},{1,9},{2,10},{3,11},{4,12},{5,13},{6,14},{7,15},{8,0},{9,1},... | collective-permute-start | bytes 1400840 | tf_op jit(solution)/shard_map/ppermute | solution.py:582
  137.8 52.6 %collective-permute-start.9 = (bf16[256,640]{1,0:T(8,128)(2,1)}, bf16[256,640]{1,0:T(8,128)(2,1)}, u32[]{:S(2)}, u32[]{:S(2)}) collective-permute-start(bf16[256,640]{1,0:T(8,128)(2,1)} %collective-permute-done.8), channel_id=1, source_target_pairs={{0,4},{1,5},{2,6},{3,7},{4,0},{5,1},{6,2},{7,3},{8,12},{9,13},{10,... | collective-permute-start | bytes 983048 | tf_op jit(solution)/shard_map/ppermute | solution.py:582
  137.8 51.1 %collective-permute-start.27 = (bf16[256,384]{1,0:T(8,128)(2,1)S(1)}, bf16[256,384]{1,0:T(8,128)(2,1)}, u32[]{:S(2)}, u32[]{:S(2)}) collective-permute-start(bf16[256,384]{1,0:T(8,128)(2,1)S(1)} %collective-permute-done.26), channel_id=1, source_target_pairs={{0,4},{1,5},{2,6},{3,7},{4,0},{5,1},{6,2},{7,3},{8,12},{9,13},{10,... | collective-permute-start | bytes 589832 | tf_op jit(solution)/shard_map/ppermute | solution.py:582
  141.5 54.0 %collective-permute-start.11 = (bf16[256,640]{1,0:T(8,128)(2,1)}, bf16[256,640]{1,0:T(8,128)(2,1)}, u32[]{:S(2)}, u32[]{:S(2)}) collective-permute-start(bf16[256,640]{1,0:T(8,128)(2,1)} %collective-permute-done.10), channel_id=1, source_target_pairs={{0,4},{1,5},{2,6},{3,7},{4,0},{5,1},{6,2},{7,3},{8,12},{9,13},{10,... | collective-permute-start | bytes 983048 | tf_op jit(solution)/shard_map/ppermute | solution.py:582
  143.2 57.5 %collective-permute-start.12 = (bf16[256,640]{1,0:T(8,128)(2,1)}, bf16[256,640]{1,0:T(8,128)(2,1)}, u32[]{:S(2)}, u32[]{:S(2)}) collective-permute-start(bf16[256,640]{1,0:T(8,128)(2,1)} %collective-permute-done.10), channel_id=1, source_target_pairs={{0,8},{1,9},{2,10},{3,11},{4,12},{5,13},{6,14},{7,15},{8,0},{9,1},... | collective-permute-start | bytes 983048 | tf_op jit(solution)/shard_map/ppermute | solution.py:582
  144.9 213.3 %collective-permute-start.36 = (bf16[192,2048]{1,0:T(8,128)(2,1)}, bf16[192,2048]{1,0:T(8,128)(2,1)}, u32[]{:S(2)}, u32[]{:S(2)}) collective-permute-start(bf16[192,2048]{1,0:T(8,128)(2,1)} %pad_maximum_fusion.1), channel_id=1, source_target_pairs={{0,1},{1,0},{2,3},{3,2},{4,5},{5,4},{6,7},{7,6},{8,9},{9,8},{10,11... | collective-permute-start | bytes 2359304 | tf_op jit(solution)/shard_map/ppermute | solution.py:582
  211.2 137.6 %collective-permute-start.13 = (bf16[256,640]{1,0:T(8,128)(2,1)}, bf16[256,640]{1,0:T(8,128)(2,1)}, u32[]{:S(2)}, u32[]{:S(2)}) collective-permute-start(bf16[256,640]{1,0:T(8,128)(2,1)} %collective-permute-done.12), channel_id=1, source_target_pairs={{0,4},{1,5},{2,6},{3,7},{4,0},{5,1},{6,2},{7,3},{8,12},{9,13},{10,... | collective-permute-start | bytes 983048 | tf_op jit(solution)/shard_map/ppermute | solution.py:582
  216.6 172.8 %collective-permute-start.39 = (bf16[192,2048]{1,0:T(8,128)(2,1)}, bf16[192,2048]{1,0:T(8,128)(2,1)}, u32[]{:S(2)}, u32[]{:S(2)}) collective-permute-start(bf16[192,2048]{1,0:T(8,128)(2,1)} %pad_maximum_fusion.2), channel_id=1, source_target_pairs={{0,1},{1,0},{2,3},{3,2},{4,5},{5,4},{6,7},{7,6},{8,9},{9,8},{10,11... | collective-permute-start | bytes 2359304 | tf_op jit(solution)/shard_map/ppermute | solution.py:582
  224.4 167.1 %collective-permute-start.42 = (bf16[192,2048]{1,0:T(8,128)(2,1)}, bf16[192,2048]{1,0:T(8,128)(2,1)}, u32[]{:S(2)}, u32[]{:S(2)}) collective-permute-start(bf16[192,2048]{1,0:T(8,128)(2,1)} %pad_maximum_fusion.3), channel_id=1, source_target_pairs={{0,1},{1,0},{2,3},{3,2},{4,5},{5,4},{6,7},{7,6},{8,9},{9,8},{10,11... | collective-permute-start | bytes 2359304 | tf_op jit(solution)/shard_map/ppermute | solution.py:582
  234.4 133.6 %collective-permute-start.44 = (bf16[96,2048]{1,0:T(8,128)(2,1)}, bf16[96,2048]{1,0:T(8,128)(2,1)}, u32[]{:S(2)}, u32[]{:S(2)}) collective-permute-start(bf16[96,2048]{1,0:T(8,128)(2,1)} %collective-permute-done.43), channel_id=1, source_target_pairs={{0,2},{1,3},{2,0},{3,1},{4,6},{5,7},{6,4},{7,5},{8,10},{9,11},{10,... | collective-permute-start | bytes 1179656 | tf_op jit(solution)/shard_map/ppermute | solution.py:582
  374.2 43.6 %collective-permute-start.45 = (bf16[192,2048]{1,0:T(8,128)(2,1)}, bf16[192,2048]{1,0:T(8,128)(2,1)}, u32[]{:S(2)}, u32[]{:S(2)}) collective-permute-start(bf16[192,2048]{1,0:T(8,128)(2,1)} %pad_maximum_fusion.4), channel_id=1, source_target_pairs={{0,1},{1,0},{2,3},{3,2},{4,5},{5,4},{6,7},{7,6},{8,9},{9,8},{10,11... | collective-permute-start | bytes 2359304 | tf_op jit(solution)/shard_map/ppermute | solution.py:582
  632.2 42.5 %collective-permute-start.59 = (bf16[384,256]{0,1:T(8,128)(2,1)}, bf16[384,256]{0,1:T(8,128)(2,1)}, u32[]{:S(2)}, u32[]{:S(2)}) collective-permute-start(bf16[384,256]{0,1:T(8,128)(2,1)} %bitcast.312), channel_id=1, source_target_pairs={{0,4},{1,5},{2,6},{3,7},{4,0},{5,1},{6,2},{7,3},{8,12},{9,13},{10,... | collective-permute-start | bytes 589832 | tf_op jit(solution)/shard_map/ppermute | solution.py:582
  651.1 41.1 %collective-permute-start.77 = (bf16[256,384]{1,0:T(8,128)(2,1)S(1)}, bf16[256,384]{1,0:T(8,128)(2,1)S(1)}, u32[]{:S(2)}, u32[]{:S(2)}) collective-permute-start(bf16[256,384]{1,0:T(8,128)(2,1)S(1)} %get-tuple-element.48), channel_id=1, source_target_pairs={{0,4},{1,5},{2,6},{3,7},{4,0},{5,1},{6,2},{7,3},{8,12},{9,13},{10,... | collective-permute-start | bytes 589832 | tf_op jit(solution)/shard_map/ppermute | solution.py:582
  693.0 46.0 %collective-permute-start.66 = (bf16[192,2048]{1,0:T(8,128)(2,1)S(1)}, bf16[192,2048]{1,0:T(8,128)(2,1)S(1)}, u32[]{:S(2)}, u32[]{:S(2)}) collective-permute-start(bf16[192,2048]{1,0:T(8,128)(2,1)S(1)} %pad_maximum_fusion.10), channel_id=1, source_target_pairs={{0,1},{1,0},{2,3},{3,2},{4,5},{5,4},{6,7},{7,6},{8,9},{9,8},{10,11... | collective-permute-start | bytes 2359304 | tf_op jit(solution)/shard_map/ppermute | solution.py:582
  704.4 61.6 %collective-permute-start.70 = (bf16[256,640]{1,0:T(8,128)(2,1)S(1)}, bf16[256,640]{1,0:T(8,128)(2,1)S(1)}, u32[]{:S(2)}, u32[]{:S(2)}) collective-permute-start(bf16[256,640]{1,0:T(8,128)(2,1)S(1)} %get-tuple-element.42), channel_id=1, source_target_pairs={{0,4},{1,5},{2,6},{3,7},{4,0},{5,1},{6,2},{7,3},{8,12},{9,13},{10,... | collective-permute-start | bytes 983048 | tf_op jit(solution)/shard_map/ppermute | solution.py:582
  711.4 124.4 %collective-permute-start.47 = (bf16[96,2048]{1,0:T(8,128)(2,1)}, bf16[96,2048]{1,0:T(8,128)(2,1)}, u32[]{:S(2)}, u32[]{:S(2)}) collective-permute-start(bf16[96,2048]{1,0:T(8,128)(2,1)} %fusion.25), channel_id=1, source_target_pairs={{0,2},{1,3},{2,0},{3,1},{4,6},{5,7},{6,4},{7,5},{8,10},{9,11},{10,... | collective-permute-start | bytes 1179656 | tf_op jit(solution)/shard_map/ppermute | solution.py:582
  741.5 94.3 %collective-permute-start.50 = (bf16[96,2048]{1,0:T(8,128)(2,1)}, bf16[96,2048]{1,0:T(8,128)(2,1)}, u32[]{:S(2)}, u32[]{:S(2)}) collective-permute-start(bf16[96,2048]{1,0:T(8,128)(2,1)} %fusion.24), channel_id=1, source_target_pairs={{0,8},{1,9},{2,10},{3,11},{4,12},{5,13},{6,14},{7,15},{8,0},{9,1},... | collective-permute-start | bytes 1179656 | tf_op jit(solution)/shard_map/ppermute | solution.py:582
  766.6 69.2 %collective-permute-start.56 = (bf16[96,2048]{1,0:T(8,128)(2,1)}, bf16[96,2048]{1,0:T(8,128)(2,1)}, u32[]{:S(2)}, u32[]{:S(2)}) collective-permute-start(bf16[96,2048]{1,0:T(8,128)(2,1)} %fusion.21), channel_id=1, source_target_pairs={{0,16},{1,17},{2,18},{3,19},{4,20},{5,21},{6,22},{7,23},{8,24},{9,... | collective-permute-start | bytes 1179656 | tf_op jit(solution)/shard_map/ppermute | solution.py:582
  (130 other events, 2958.4 us)
Sparse Core Ops, SparseCore 0:
  788.8 31.9 all-reduce.7

commit v3 on v2

--- a/solution.py
+++ b/solution.py
@@ -540,7 +540,740 @@
     )(attn_out, states, out_grad, gain, w_output, w_hidden, down_grads)
 
 
-def local(
+class Gather:
+    def __init__(self, links, block, own=None):
+        self.links, self.block, self.y = links, block, links.place.y
+        self.own = block(0, self.y) if own is None else own
+        self.lines = []
+
+    def over_lines(self, move):
+        place = self.block(move, self.y)
+        source = self.own if move == 0 else place
+        self.lines.append(self.links.send(source, place, ky=1))
+
+    def start(self):
+        place = self.block(0, self.y)
+        self.far = self.links.send(self.own, place, kz=2)
+        self.near = self.links.send(self.own, place, kz=1)
+        self.over_lines(0)
+
+    def relay(self):
+        self.near.wait_recv()
+        self.over_lines(1)
+        self.far.wait_recv()
+        place = self.block(2, self.y)
+        self.corner = self.links.send(place, place, kz=1)
+        self.over_lines(2)
+
+    def last(self):
+        self.corner.wait_recv()
+        self.over_lines(3)
+
+    def finish(self):
+        for copy in self.lines:
+            copy.wait_recv()
+
+
+def head_mean(value):
+    row = lax.broadcasted_iota(jnp.int32, (128, 128), 0) // HEAD_WIDTH
+    column = lax.broadcasted_iota(jnp.int32, (128, 128), 1) // HEAD_WIDTH
+    average = jnp.where(row == column, 1.0 / HEAD_WIDTH, 0.0).astype(F32)
+    return jnp.dot(
+        value, average, preferred_element_type=F32, precision=lax.Precision.HIGHEST
+    )
+
+
+def halves_swapped(value):
+    first = lax.rem(lax.broadcasted_iota(jnp.int32, value.shape, 1), HEAD_WIDTH) < HEAD_WIDTH // 2
+    return jnp.where(
+        first,
+        pltpu.roll(value, 128 - HEAD_WIDTH // 2, 1),
+        pltpu.roll(value, HEAD_WIDTH // 2, 1),
+    )
+
+
+FRONT_COPIES = 46
+
+
+def front_kernel(
+    lines,
+    heads,
+    states_ref,
+    gains_in,
+    w_attend_in,
+    cosine_ref,
+    sine_ref,
+    head_gain_ref,
+    w_output_in,
+    w_hidden_in,
+    grad_any,
+    lin_ref,
+    attn_in_ref,
+    query_ref,
+    kv_ref,
+    gains_ref,
+    w_attend_ref,
+    w_output_ref,
+    w_hidden_ref,
+    down_ref,
+    local_sems,
+    send_sems,
+    recv_sems,
+):
+    here = Place(lines)
+    links = Links(here, send_sems, recv_sems)
+    token_rows, width = states_ref.shape
+    quarter = token_rows // 4
+    half = 2 * quarter
+    weight_rows = w_attend_in.shape[0]
+    head_width = heads * HEAD_WIDTH
+    mine, my_half = rows_at(here.quarter, quarter), rows_at(here.c, half)
+
+    def rank(move, line):
+        return here.plane(move) * lines + line
+
+    def rows_of(ref):
+        return lambda move, line: ref.at[rows_at(rank(move, line), weight_rows)]
+
+    def columns_of(ref):
+        return lambda move, line: ref.at[:, rows_at(rank(move, line), weight_rows)]
+
+    loads = [
+        pltpu.make_async_copy(w_output_in, rows_of(w_output_ref)(0, here.y), local_sems.at[0]),
+        pltpu.make_async_copy(
+            w_hidden_in.at[here.z], columns_of(w_hidden_ref)(0, here.y), local_sems.at[1]
+        ),
+        pltpu.make_async_copy(grad_any, down_ref.at[here.z], local_sems.at[2]),
+    ]
+    for load in loads:
+        load.start()
+    links.greet([dict(kc=1), dict(kx=1), dict(ky=1), dict(kz=1), dict(kz=2), dict(kz=3)])
+
+    gains = Gather(links, columns_of(gains_ref), gains_in)
+    gains.start()
+    attend = Gather(links, rows_of(w_attend_ref), w_attend_in)
+    attend.start()
+    columns_of(gains_ref)(0, here.y)[...] = gains_in[...]
+    rows_of(w_attend_ref)(0, here.y)[...] = w_attend_in[...]
+    gains.relay()
+    gains.last()
+    gains.finish()
+    states = states_ref[...].astype(F32)
+    inverse = lax.rsqrt(jnp.mean(states * states, axis=-1, keepdims=True) + EPSILON)
+    attn_in_ref[...] = (states * inverse * gains_ref[0:1, :]).astype(BF16)
+
+    attend.relay()
+    output = Gather(links, rows_of(w_output_ref), w_output_in)
+    output.start()
+    planes = [
+        links.send(w_hidden_in.at[here.plane(move)], columns_of(w_hidden_ref)(0, here.y), kz=move)
+        for move in (1, 2, 3)
+    ]
+    attend.last()
+    attend.finish()
+    lin = product(attn_in_ref[...], w_attend_ref[...])
+    lin_ref[...] = lin
+    blocks = token_rows // STRETCH
+    own_rows = rows_at(rank(0, here.y), token_rows)
+
+    def turned(group):
+        columns = slice(group * 128, (group + 1) * 128)
+        value = lin[:, columns]
+        value = value * lax.rsqrt(head_mean(value * value) + EPSILON) * head_gain_ref[:, columns]
+        return (value * cosine_ref[...] + halves_swapped(value) * sine_ref[...]).astype(BF16)
+
+    keys = head_width // 128
+    kv_ref[own_rows, :128] = turned(keys)
+    kv_ref[own_rows, 128:] = lin[:, head_width + 128 :].astype(BF16)
+    keyvalue = Gather(
+        links, lambda move, line: kv_ref.at[rows_at(rank(move, line), token_rows)]
+    )
+    keyvalue.start()
+    for pair in range(PAIRS):
+        rotated_pair = turned(pair)
+        for block in range(blocks):
+            rows = rotated_pair[block * STRETCH : (block + 1) * STRETCH]
+            query_ref[block, pair, :STRETCH] = rows[:, :HEAD_WIDTH]
+            query_ref[block, pair, STRETCH:] = rows[:, HEAD_WIDTH:]
+    keyvalue.relay()
+    keyvalue.last()
+
+    loads[2].wait()
+
+    def block_of(move):
+        return down_ref.at[here.plane(move), mine]
+
+    far = links.send(block_of(0), block_of(0), kz=2)
+    near = links.send(block_of(0), block_of(0), kz=1)
+    loads[0].wait()
+    loads[1].wait()
+    output.relay()
+    hidden_lines = []
+    for move in range(4):
+        if move:
+            planes[move - 1].wait_recv()
+        place = columns_of(w_hidden_ref)(move, here.y)
+        hidden_lines.append(links.send(place, place, ky=1))
+    near.wait_recv()
+    across = [links.send(block_of(1), block_of(1), kx=1)]
+    far.wait_recv()
+    corner = links.send(block_of(2), block_of(2), kz=1)
+    across.append(links.send(block_of(2), block_of(2), kx=1))
+    output.last()
+    corner.wait_recv()
+    across.append(links.send(block_of(3), block_of(3), kx=1))
+    cores = []
+    for move in (1, 2, 3):
+        across[move - 1].wait_recv()
+        both = down_ref.at[here.plane(move), my_half]
+        cores.append(links.send(both, both, kc=1))
+    keyvalue.finish()
+    output.finish()
+    for copy in hidden_lines + cores:
+        copy.wait_recv()
+    links.finish()
+
+
+def front(lines, heads, states, gains, w_attend, cosine, sine, head_gain, w_output, w_hidden, grad):
+    token_rows, width = states.shape
+    ranks = 4 * lines
+    hidden = w_hidden.shape[1]
+    blocks = token_rows // STRETCH
+    vmem = pl.BlockSpec(memory_space=pltpu.VMEM)
+    hbm = pl.BlockSpec(memory_space=pl.ANY)
+    shape = jax.ShapeDtypeStruct
+    return pl.pallas_call(
+        functools.partial(front_kernel, lines, heads),
+        out_shape=(
+            shape((token_rows, w_attend.shape[1]), F32),
+            shape((token_rows, width), BF16),
+            shape((blocks, PAIRS, 2 * STRETCH, HEAD_WIDTH), BF16),
+            shape((ranks * token_rows, 4 * HEAD_WIDTH), BF16),
+            shape((gains.shape[0], width), F32),
+            shape((width, w_attend.shape[1]), BF16),
+            shape((width, w_output.shape[1]), BF16),
+            shape((hidden, width), BF16),
+            shape((4, token_rows, width), BF16),
+        ),
+        in_specs=[vmem] * 6 + [hbm] * 3,
+        out_specs=(vmem,) * 6 + (hbm,) * 3,
+        scratch_shapes=[
+            pltpu.SemaphoreType.DMA((3,)),
+            pltpu.SemaphoreType.DMA((FRONT_COPIES,)),
+            pltpu.SemaphoreType.DMA((FRONT_COPIES,)),
+        ],
+        compiler_params=pltpu.CompilerParams(
+            collective_id=1, has_side_effects=True, vmem_limit_bytes=56 << 20
+        ),
+        name="front",
+    )(states, gains, w_attend, cosine, sine, head_gain, w_output, w_hidden, grad)
+
+
+TAIL_COPIES = 50
+
+
+class Scatter:
+    ORDER = (3, 1, 2, 0)
+
+    def __init__(self, links, y_out, y_in, z_out, z_in, sums):
+        self.links = links
+        self.y_out, self.y_in, self.z_out, self.z_in, self.sums = y_out, y_in, z_out, z_in, sums
+        self.lines, self.planes = {}, {}
+
+    def start(self, move, block):
+        self.y_out[move] = block.astype(BF16)
+        self.lines[move] = self.links.send(self.y_out.at[move], self.y_in.at[move], ky=1)
+
+    def add(self, move, block):
+        self.lines[move].wait_recv()
+        total = block + self.y_in[move].astype(F32)
+        if move in (3, 1):
+            slot = 0 if move == 1 else 1
+            self.z_out[slot] = total.astype(BF16)
+            self.planes[slot] = self.links.send(self.z_out.at[slot], self.z_in.at[slot], kz=1)
+        elif move == 2:
+            self.planes[1].wait_recv()
+            self.z_out[2] = (total + self.z_in[1].astype(F32)).astype(BF16)
+            self.planes[2] = self.links.send(self.z_out.at[2], self.z_in.at[2], kz=2)
+        else:
+            self.sums[...] = total
+
+    def finish(self):
+        self.planes[0].wait_recv()
+        self.planes[2].wait_recv()
+        return self.sums[...] + self.z_in[0].astype(F32) + self.z_in[2].astype(F32)
+
+
+def scatter_scratch(block):
+    return [
+        pltpu.VMEM((4, *block), BF16),
+        pltpu.VMEM((4, *block), BF16),
+        pltpu.VMEM((3, *block), BF16),
+        pltpu.VMEM((3, *block), BF16),
+        pltpu.VMEM(block, F32),
+    ]
+
+
+def tail_kernel(
+    lines,
+    heads,
+    d_kv_ref,
+    d_query_ref,
+    lin_ref,
+    attn_in_ref,
+    output_grad_ref,
+    attn_out_ref,
+    w_attend_ref,
+    back_ref,
+    gains_ref,
+    gain_ffn_ref,
+    states_ref,
+    middle_ref,
+    mixed_ref,
+    cosine_ref,
+    sine_ref,
+    head_gain_ref,
+    w_hidden_any,
+    result_ref,
+    states_grad_ref,
+    g_attend_ref,
+    g_output_ref,
+    g_kv_ref,
+    small_ref,
+    *scratch,
+):
+    here = Place(lines)
+    (
+        w_down_ref,
+        d_lin_ref,
+        partial_ref,
+        core_out,
+        core_in,
+        x_out,
+        x_in,
+        sums_ref,
+        z_out,
+        z_in,
+        small_out,
+        small_in,
+        local_sems,
+        send_sems,
+        recv_sems,
+    ) = scratch[:15]
+    links = Links(here, send_sems, recv_sems)
+    kv_sum = Scatter(links, *scratch[15:20])
+    output_sum = Scatter(links, *scratch[20:25])
+    attend_sum = Scatter(links, *scratch[25:30])
+    token_rows, width = states_ref.shape
+    quarter = token_rows // 4
+    half = 2 * quarter
+    weight_rows = width // (4 * lines)
+    head_width = heads * HEAD_WIDTH
+    blocks = token_rows // STRETCH
+    hidden = mixed_ref.shape[0]
+    mine, other = rows_at(here.quarter, quarter), rows_at(here.c * 2 + 1 - here.x, quarter)
+    my_half, other_half = rows_at(here.c, half), rows_at(1 - here.c, half)
+    x_mine, x_other = rows_at(here.x, quarter), rows_at(1 - here.x, quarter)
+
+    load = pltpu.make_async_copy(
+        w_hidden_any.at[pl.ds(2 * hidden, hidden)], w_down_ref, local_sems.at[0]
+    )
+    load.start()
+    links.greet([dict(kc=1), dict(kx=1), dict(ky=1), dict(kz=1), dict(kz=2)])
+
+    def rank(move, line):
+        return here.plane(move) * lines + line
+
+    def kv_block(move, line):
+        return d_kv_ref[rows_at(rank(move, line), token_rows), :]
+
+    for move in Scatter.ORDER:
+        kv_sum.start(move, kv_block(move, 1 - here.y))
+
+    def columns(move, line):
+        return rows_at(rank(move, line), weight_rows)
+
+    def output_block(move, line):
+        return by_rows(output_grad_ref[:, columns(move, line)], attn_out_ref[...])
+
+    def attend_block(move, line):
+        return by_rows(attn_in_ref[:, columns(move, line)], d_lin_ref[...])
+
+    def group_back(group, grad):
+        at = slice(group * 128, (group + 1) * 128)
+        linear = lin_ref[:, at]
+        inverse = lax.rsqrt(head_mean(linear * linear) + EPSILON)
+        unit = linear * inverse
+        grad = grad * cosine_ref[...] + halves_swapped(grad * sine_ref[...])
+        gain = jnp.sum(grad * unit, axis=0, keepdims=True)
+        scaled = grad * head_gain_ref[:, at]
+        return inverse * (scaled - unit * head_mean(scaled * unit)), gain
+
+    small_ref[...] = jnp.zeros_like(small_ref)
+    small_ref[1:2, :] = gain_ffn_ref[...]
+    for pair in range(PAIRS):
+        grad = jnp.concatenate(
+            [
+                jnp.concatenate(
+                    [d_query_ref[block, pair, :STRETCH], d_query_ref[block, pair, STRETCH:]], axis=1
+                )
+                for block in range(blocks)
+            ],
+            axis=0,
+        )
+        linear_grad, gain = group_back(pair, grad)
+        d_lin_ref[:, pair * 128 : (pair + 1) * 128] = linear_grad.astype(BF16)
+        small_ref[2:3, pair * 128 : (pair + 1) * 128] = gain
+
+    for move in Scatter.ORDER[:2]:
+        kv_sum.add(move, kv_block(move, here.y))
+
+    core_copies, x_copies = {}, {}
+    load.wait()
+
+    def out_start(move, slot):
+        at = pl.ds(pl.multiple_of(here.plane(move) * token_rows, token_rows), token_rows)
+        partial_ref[slot] = by_rows(mixed_ref[:, at], w_down_ref[...])
+        core_out[move] = partial_ref[slot, other_half, :].astype(BF16)
+        core_copies[move] = links.send(core_out.at[move], core_in.at[move], kc=1)
+
+    def add_cores(move, slot):
+        core_copies[move].wait_recv()
+        x_out[move] = (partial_ref[slot, other, :] + core_in[move, x_other, :].astype(F32)).astype(
+            BF16
+        )
+        x_copies[move] = links.send(x_out.at[move], x_in.at[move], kx=1)
+        sums_ref[move] = partial_ref[slot, mine, :] + core_in[move, x_mine, :].astype(F32)
+
+    def add_x(move):
+        x_copies[move].wait_recv()
+        sums_ref[move] += x_in[move].astype(F32)
+
+    out_start(3, 0)
+    out_start(1, 1)
+    for move in Scatter.ORDER[2:]:
+        kv_sum.add(move, kv_block(move, here.y))
+    add_cores(3, 0)
+    out_start(2, 0)
+    add_cores(1, 1)
+    out_start(0, 1)
+    for move in Scatter.ORDER:
+        output_sum.start(move, output_block(move, 1 - here.y))
+
+    d_kv = kv_sum.finish()
+    linear_grad, gain = group_back(PAIRS, d_kv[:, :128])
+    d_lin_ref[:, head_width : head_width + 128] = linear_grad.astype(BF16)
+    d_lin_ref[:, head_width + 128 :] = d_kv[:, 128:].astype(BF16)
+    small_ref[2:3, head_width : head_width + 128] = gain
+
+    for move in Scatter.ORDER:
+        attend_sum.start(move, attend_block(move, 1 - here.y))
+
+    add_cores(2, 0)
+    add_cores(0, 1)
+    partial_ref[0] = by_cols(d_lin_ref[...], w_attend_ref[...])
+    core_out[4] = partial_ref[0, other_half, :].astype(BF16)
+    core_copies[4] = links.send(core_out.at[4], core_in.at[4], kc=1)
+    add_cores(4, 0)
+    for move in Scatter.ORDER[:2]:
+        output_sum.add(move, output_block(move, here.y))
+    for move in Scatter.ORDER[:2]:
+        attend_sum.add(move, attend_block(move, here.y))
+    add_x(4)
+    states = states_ref[mine, :].astype(F32)
+    inverse = lax.rsqrt(jnp.mean(states * states, axis=-1, keepdims=True) + EPSILON)
+    unit = states * inverse
+    grad = sums_ref[4]
+    small_ref[0:1, :] = jnp.sum(grad * unit, axis=0, keepdims=True)
+    scaled = grad * gains_ref[0:1, :]
+    total = back_ref[...] + inverse * (
+        scaled - unit * jnp.mean(scaled * unit, axis=-1, keepdims=True)
+    )
+    states_grad_ref[mine, :] = total.astype(BF16)
+    block = states_grad_ref.at[mine]
+    states_x = links.send(block, block, kx=1)
+
+    def small_step(step, **move):
+        small_out[step] = small_ref[...]
+        return links.send(small_out.at[step], small_in.at[step], **move)
+
+    small = small_step(0, kc=1)
+    output_sum.add(2, output_block(2, here.y))
+    attend_sum.add(2, attend_block(2, here.y))
+    small.wait_recv()
+    small_ref[...] += small_in[0]
+    small = small_step(1, kx=1)
+    states_x.wait_recv()
+    both = states_grad_ref.at[my_half]
+    states_core = links.send(both, both, kc=1)
+    output_sum.add(0, output_block(0, here.y))
+    attend_sum.add(0, attend_block(0, here.y))
+    small.wait_recv()
+    small_ref[...] += small_in[1]
+    small = small_step(2, ky=1)
+
+    add_x(3)
+    add_x(1)
+    z_out[1] = sums_ref[3].astype(BF16)
+    z_out[0] = sums_ref[1].astype(BF16)
+    z_copies = {1: links.send(z_out.at[1], z_in.at[1], kz=1)}
+    z_copies[0] = links.send(z_out.at[0], z_in.at[0], kz=1)
+    add_x(2)
+    add_x(0)
+    small.wait_recv()
+    small_ref[...] += small_in[2]
+    small = small_step(3, kz=1)
+    z_copies[1].wait_recv()
+    z_out[2] = (sums_ref[2] + z_in[1].astype(F32)).astype(BF16)
+    z_copies[2] = links.send(z_out.at[2], z_in.at[2], kz=2)
+    small.wait_recv()
+    small_ref[...] += small_in[3]
+    small = small_step(4, kz=2)
+
+    total = attend_sum.finish()
+    g_attend_ref[...] = total[:, :head_width]
+    part = here.x * 2 + here.c
+    g_kv_ref[part] = total[:, head_width:].astype(BF16)
+    block = g_kv_ref.at[part]
+    kv_core = links.send(block, block, kc=1)
+    kv_x = links.send(block, block, kx=1)
+    g_output_ref[...] = output_sum.finish()
+    z_copies[0].wait_recv()
+    z_copies[2].wait_recv()
+    result_ref[mine, :] = (
+        middle_ref[...] + sums_ref[0] + z_in[0].astype(F32) + z_in[2].astype(F32)
+    ).astype(BF16)
+    block = result_ref.at[mine]
+    result_x = links.send(block, block, kx=1)
+    kv_x.wait_recv()
+    block = g_kv_ref.at[(1 - here.x) * 2 + here.c]
+    kv_both = links.send(block, block, kc=1)
+    small.wait_recv()
+    small_ref[...] += small_in[4]
+    result_x.wait_recv()
+    both = result_ref.at[my_half]
+    result_core = links.send(both, both, kc=1)
+    for copy in (states_core, kv_core, kv_both, result_core):
+        copy.wait_recv()
+    links.finish()
+
+
+def tail(lines, heads, *arguments):
+    (d_kv, d_query, lin, attn_in, output_grad, attn_out, w_attend, *others) = arguments
+    token_rows, width = attn_in.shape
+    quarter = token_rows // 4
+    half = 2 * quarter
+    weight_rows = width // (4 * lines)
+    head_width = heads * HEAD_WIDTH
+    hidden = arguments[12].shape[0]
+    vmem = pl.BlockSpec(memory_space=pltpu.VMEM)
+    hbm = pl.BlockSpec(memory_space=pl.ANY)
+    shape = jax.ShapeDtypeStruct
+    return pl.pallas_call(
+        functools.partial(tail_kernel, lines, heads),
+        out_shape=(
+            shape((token_rows, width), BF16),
+            shape((token_rows, width), BF16),
+            shape((weight_rows, head_width), F32),
+            shape((weight_rows, head_width), F32),
+            shape((4, weight_rows, 4 * HEAD_WIDTH), BF16),
+            shape((8, width), F32),
+        ),
+        in_specs=[vmem] * 16 + [hbm],
+        out_specs=(vmem,) * 6,
+        scratch_shapes=[
+            pltpu.VMEM((hidden, width), BF16),
+            pltpu.VMEM(lin.shape, BF16),
+            pltpu.VMEM((2, token_rows, width), F32),
+            pltpu.VMEM((5, half, width), BF16),
+            pltpu.VMEM((5, half, width), BF16),
+            pltpu.VMEM((5, quarter, width), BF16),
+            pltpu.VMEM((5, quarter, width), BF16),
+            pltpu.VMEM((5, quarter, width), F32),
+            pltpu.VMEM((3, quarter, width), BF16),
+            pltpu.VMEM((3, quarter, width), BF16),
+            pltpu.VMEM((5, 8, width), F32),
+            pltpu.VMEM((5, 8, width), F32),
+            pltpu.SemaphoreType.DMA((1,)),
+            pltpu.SemaphoreType.DMA((TAIL_COPIES,)),
+            pltpu.SemaphoreType.DMA((TAIL_COPIES,)),
+            *scatter_scratch((token_rows, 4 * HEAD_WIDTH)),
+            *scatter_scratch((weight_rows, head_width)),
+            *scatter_scratch((weight_rows, lin.shape[1])),
+        ],
+        compiler_params=pltpu.CompilerParams(
+            collective_id=2, has_side_effects=True, vmem_limit_bytes=62 << 20
+        ),
+        name="tail",
+    )(*arguments)
+
+
+def local_kernels(
+    states,
+    query_weight,
+    keyvalue_matrix,
+    output_weight,
+    gate_weight,
+    up_weight,
+    down_weight,
+    norm_gains,
+    query_gain,
+    key_gain,
+    slot_sequence,
+    slot_offset,
+    out_grad,
+):
+    token_rows, width = states.shape
+    dp_ranks = lax.axis_size("dp")
+    tensor_ranks = lax.axis_size("tensor")
+    lines = dp_ranks // PLANES
+    rank, part = lax.axis_index("dp"), lax.axis_index("tensor")
+    heads_here = QUERY_HEADS // tensor_ranks
+    head_width = heads_here * HEAD_WIDTH
+    sharing_count = QUERY_HEADS // KEYVALUE_HEADS
+    blocks_here = token_rows // STRETCH
+    slot_count = slot_sequence.shape[0]
+    hidden = gate_weight.shape[2]
+    slice_width = hidden // PLANES
+    weight_rows = width // dp_ranks
+
+    sequence_here = lax.dynamic_slice_in_dim(slot_sequence, rank * blocks_here, blocks_here)
+    offset_here = lax.dynamic_slice_in_dim(slot_offset, rank * blocks_here, blocks_here)
+    counts = offset_here // STRETCH + 1
+    places = jnp.arange(slot_count, dtype=jnp.int32)
+    same = (slot_sequence[None, None, :] == sequence_here[:, None, None]) & (
+        slot_offset[None, None, :] == places[None, :, None] * STRETCH
+    )
+    slots = jnp.sum(jnp.where(same, places[None, None, :], 0), axis=2).astype(jnp.int32)
+    parity = jnp.reshape(part % 2, (1,)).astype(jnp.int32)
+    positions = (offset_here[:, None] + jnp.arange(STRETCH, dtype=jnp.int32)[None, :]).reshape(-1)
+    columns = jnp.arange(2 * HEAD_WIDTH, dtype=jnp.int32)
+    exponent = -(columns % (HEAD_WIDTH // 2)).astype(F32) * 2.0 / HEAD_WIDTH
+    phase = positions.astype(F32)[:, None] * (10000.0**exponent)[None, :]
+    cosine = jnp.cos(phase)
+    sine = jnp.sin(phase) * jnp.where(columns % HEAD_WIDTH < HEAD_WIDTH // 2, -1.0, 1.0)[None, :]
+    head_gain = jnp.concatenate([jnp.tile(query_gain[0], heads_here), jnp.tile(key_gain[0], 2)])
+
+    first_key = (part * heads_here) // sharing_count * HEAD_WIDTH
+    value_start = KEYVALUE_HEADS * HEAD_WIDTH
+    w_attend = jnp.concatenate(
+        [
+            query_weight[0],
+            lax.dynamic_slice_in_dim(keyvalue_matrix[0], first_key, 2 * HEAD_WIDTH, 1),
+            lax.dynamic_slice_in_dim(
+                keyvalue_matrix[0], value_start + first_key, 2 * HEAD_WIDTH, 1
+            ),
+        ],
+        axis=1,
+    )
+    gains = jnp.pad(norm_gains[0].T.astype(F32), ((0, 6), (0, 0)))
+
+    def turned(weight):
+        return weight[0].reshape(weight_rows, PLANES, slice_width).transpose(1, 2, 0)
+
+    packed = jnp.concatenate(
+        [turned(gate_weight), turned(up_weight), turned(down_weight)], axis=1
+    )
+    lin, attn_in, queries, keyvalues, gains, w_attend, w_output, w_hidden, down_grads = front(
+        lines,
+        heads_here,
+        states,
+        gains,
+        w_attend,
+        cosine,
+        sine,
+        head_gain[None],
+        output_weight[0],
+        packed,
+        out_grad,
+    )
+    keyvalues = keyvalues.reshape(slot_count, STRETCH, 4 * HEAD_WIDTH)
+    attended = attend(counts, slots, parity, queries, keyvalues)
+
+    def from_pairs(value):
+        return (
+            value.reshape(blocks_here, PAIRS, 2, STRETCH, HEAD_WIDTH)
+            .transpose(0, 3, 1, 2, 4)
+            .reshape(token_rows, head_width)
+        )
+
+    def to_pairs(value):
+        return (
+            value.reshape(blocks_here, STRETCH, PAIRS, 2, HEAD_WIDTH)
+            .transpose(0, 2, 3, 1, 4)
+            .reshape(blocks_here, PAIRS, 2 * STRETCH, HEAD_WIDTH)
+        )
+
+    attn_out = from_pairs(attended[..., :HEAD_WIDTH].astype(BF16))
+    middle_rows, back, gain_ffn, d_heads, output_grad, mixed, collected = middle(
+        lines, slice_width, attn_out, states, out_grad, gains[1:2], w_output, w_hidden, down_grads
+    )
+    d_pairs = to_pairs(d_heads)
+    delta = jnp.sum(d_pairs.astype(F32) * attended[..., :HEAD_WIDTH], axis=-1)
+    d_query, d_keyvalue = attend_back(
+        counts,
+        slots,
+        parity,
+        queries,
+        d_pairs,
+        attended[..., HEAD_WIDTH][:, :, None, :],
+        delta[:, :, None, :],
+        keyvalues,
+    )
+    result, states_grad, g_attend, g_output, g_kv, small = tail(
+        lines,
+        heads_here,
+        d_keyvalue.reshape(dp_ranks * token_rows, 4 * HEAD_WIDTH),
+        d_query,
+        lin,
+        attn_in,
+        output_grad,
+        attn_out,
+        w_attend,
+        back,
+        gains,
+        gain_ffn,
+        states,
+        middle_rows,
+        mixed,
+        cosine,
+        sine,
+        head_gain[None],
+        w_hidden,
+    )
+
+    def hidden_grad(index):
+        piece = collected[:, index * slice_width : (index + 1) * slice_width]
+        return piece.transpose(2, 0, 1).astype(F32).reshape(1, weight_rows, hidden)
+
+    d_keyvalue_matrix = jnp.zeros((weight_rows, 2 * value_start), F32)
+    for other in range(tensor_ranks):
+        start = (other * heads_here) // sharing_count * HEAD_WIDTH
+        block = g_kv[other].astype(F32)
+        for offset, piece in (
+            (start, block[:, : 2 * HEAD_WIDTH]),
+            (value_start + start, block[:, 2 * HEAD_WIDTH :]),
+        ):
+            after = 2 * value_start - offset - 2 * HEAD_WIDTH
+            d_keyvalue_matrix += jnp.pad(piece, ((0, 0), (offset, after)))
+    head_gains = small[2, : head_width + 2 * HEAD_WIDTH].reshape(-1, HEAD_WIDTH)
+    d_gains = lax.dynamic_slice_in_dim(small[:2], rank * weight_rows, weight_rows, 1).T
+    return (
+        result,
+        states_grad.astype(F32),
+        g_attend[None],
+        d_keyvalue_matrix[None],
+        g_output[None],
+        hidden_grad(0),
+        hidden_grad(1),
+        hidden_grad(2),
+        d_gains[None],
+        jnp.sum(head_gains[:heads_here], axis=0)[None],
+        jnp.sum(head_gains[heads_here:], axis=0)[None],
+    )
+
+
+def local_permutes(
     states,
     query_weight,
     keyvalue_matrix,
@@ -570,7 +1303,6 @@
     hidden = gate_weight.shape[2]
     slice_width = hidden // PLANES
     weight_rows = width // dp_ranks
-    kernels = lines == 2 and weight_rows % 128 == 0 and tensor_ranks == 4
 
     def send(value, kz=0, ky=0, kx=0, kc=0):
         move_rank, move_part = kz * lines + ky, kx * 2 + kc
@@ -625,21 +1357,20 @@
         both = jnp.concatenate([block, send(block, kx=1)], axis=0)
         return jnp.concatenate([both, send(both, kc=1)], axis=0)
 
-    def first_row(move):
-        other = part ^ move
-        return (other % 2 * 2 + other // 2) * quarter
-
     def in_order(blocks):
         whole = jnp.zeros_like(blocks)
         for index, move in enumerate((0, 2, 1, 3)):
             whole = lax.dynamic_update_slice_in_dim(
-                whole, blocks[index * quarter : (index + 1) * quarter], first_row(move), 0
+                whole,
+                blocks[index * quarter : (index + 1) * quarter],
+                (part ^ move) * quarter,
+                0,
             )
         return whole
 
     def quarters(value):
         return [
-            lax.dynamic_slice_in_dim(value, first_row(move), quarter, 0)
+            lax.dynamic_slice_in_dim(value, (part ^ move) * quarter, quarter, 0)
             for move in range(tensor_ranks)
         ]
 
@@ -665,50 +1396,38 @@
     w_attend = gather_dp(jnp.concatenate([query_weight[0], *kv_columns], axis=1)).reshape(width, -1)
     w_output = gather_dp(output_weight[0]).reshape(width, head_width)
 
-    def turned(weight):
-        pieces = weight[0].reshape(weight_rows, PLANES, slice_width)
-        return pieces.transpose(1, 2, 0)
-
     def sliced(weight):
         return weight[0].reshape(weight_rows, PLANES, slice_width).transpose(1, 0, 2)
 
     pad_first = -2 * slice_width % 128
     pad_second = -slice_width % 128
-    if kernels:
-        packed = jnp.concatenate(
-            [turned(gate_weight), turned(up_weight), turned(down_weight)], axis=1
-        )
-    else:
-        packed = jnp.concatenate(
-            [
-                sliced(gate_weight),
-                sliced(up_weight),
-                jnp.zeros((PLANES, weight_rows, pad_first), BF16),
-                sliced(down_weight),
-                jnp.zeros((PLANES, weight_rows, pad_second), BF16),
-            ],
-            axis=2,
-        )
-    w_hidden = jnp.zeros((dp_ranks, *packed.shape[1:]), BF16)
+    packed = jnp.concatenate(
+        [
+            sliced(gate_weight),
+            sliced(up_weight),
+            jnp.zeros((PLANES, weight_rows, pad_first), BF16),
+            sliced(down_weight),
+            jnp.zeros((PLANES, weight_rows, pad_second), BF16),
+        ],
+        axis=2,
+    )
+    w_hidden = jnp.zeros((dp_ranks, weight_rows, packed.shape[2]), BF16)
     for kz in range(PLANES):
         piece = lax.dynamic_index_in_dim(packed, plane ^ kz, 0, keepdims=False)
         piece = send(piece, kz=kz) if kz else piece
         for ky in range(lines):
             got = send(piece, ky=ky) if ky else piece
             w_hidden = lax.dynamic_update_index_in_dim(w_hidden, got, rank ^ (kz * lines + ky), 0)
-    if kernels:
-        w_hidden = w_hidden.transpose(1, 0, 2).reshape(3 * slice_width, width)
-    else:
-        w_hidden = w_hidden.reshape(width, -1)
-        down_start = 2 * slice_width + pad_first
-        w_gate_up = w_hidden[:, : 2 * slice_width]
-        w_down = w_hidden[:, down_start : down_start + slice_width]
+    w_hidden = w_hidden.reshape(width, -1)
+    down_start = 2 * slice_width + pad_first
+    w_gate_up = w_hidden[:, : 2 * slice_width]
+    w_down = w_hidden[:, down_start : down_start + slice_width]
 
     def gather_group(block):
         return [gather_tensor(piece) for piece in gather_planes(block)]
 
     def quarter_of(value):
-        return lax.dynamic_slice_in_dim(value, first_row(0), quarter, 0)
+        return lax.dynamic_slice_in_dim(value, part * quarter, quarter, 0)
 
     query_g, key_g = query_gain[0], key_gain[0]
     attn_in = rounded(normed(states.astype(F32), gains[0]))
@@ -748,6 +1467,34 @@
     attn_out = rounded(from_pairs(attended[..., :HEAD_WIDTH]).reshape(token_rows, head_width))
     logs = attended[..., HEAD_WIDTH]
 
+    branch = scatter_tensor(quarters(by_cols(attn_out, w_output)))
+    states_quarter = quarter_of(states).astype(F32)
+    middle = states_quarter + branch
+    ffn_in = rounded(normed(middle, gains[1]))
+
+    down_grads = gather_group(quarter_of(out_grad))
+    ffn_ins = gather_group(ffn_in)
+    mixed_chunks, d_chunks, back_parts, out_parts = [], [], [], []
+    for down_grad, ffn_chunk in zip(down_grads, ffn_ins):
+        gate_up = product(ffn_chunk, w_gate_up)
+        gate_pre, up_pre = gate_up[:, :slice_width], gate_up[:, slice_width:]
+        sigmoid_gate = jax.nn.sigmoid(gate_pre)
+        mixed = rounded(gate_pre * sigmoid_gate * up_pre)
+        d_mixed = product(down_grad, w_down)
+        d_gate = d_mixed * up_pre * sigmoid_gate * (1.0 + gate_pre * (1.0 - sigmoid_gate))
+        d_up = d_mixed * gate_pre * sigmoid_gate
+        d_gate_up = jnp.concatenate([rounded(d_gate), rounded(d_up)], axis=1)
+        mixed_chunks.append(mixed)
+        d_chunks.append(d_gate_up)
+
+        def reduced(value):
+            blocks = value.reshape(4, quarter, width)
+            return scatter_tensor([blocks[0], blocks[2], blocks[1], blocks[3]])
+
+        back_parts.append(reduced(by_cols(d_gate_up, w_gate_up)))
+        out_parts.append(reduced(by_cols(mixed, w_down)))
+    d_ffn_in = scatter_planes(back_parts)
+
     def norm_back(vector, gain_vector, grad):
         inverse = lax.rsqrt(jnp.mean(vector * vector, axis=-1, keepdims=True) + EPSILON)
         unit = vector * inverse
@@ -755,62 +1502,13 @@
         back = inverse * (scaled - unit * jnp.mean(scaled * unit, axis=-1, keepdims=True))
         return back, jnp.sum(grad * unit, axis=0)
 
-
-    def planes_in_order(chunks):
-        whole = jnp.zeros((PLANES, *chunks[0].shape), chunks[0].dtype)
-        for kz, chunk in enumerate(chunks):
-            whole = lax.dynamic_update_index_in_dim(whole, chunk, plane ^ kz, 0)
-        return whole
-
-    states_quarter = quarter_of(states).astype(F32)
-    down_grads = gather_group(quarter_of(out_grad))
-    if kernels:
-        down_all = planes_in_order([in_order(chunk) for chunk in down_grads])
-        middle_rows, grad_middle, d_gain_ffn, d_heads, output_grad, mixed, collected = middle(
-            lines, slice_width, attn_out, states, out_grad, gains[1:], w_output, w_hidden, down_all
-        )
-        d_gain_ffn = d_gain_ffn[0]
-        d_wout = by_rows(output_grad, attn_out)
-        out_parts = []
-        for kz in range(PLANES):
-            chunk = lax.dynamic_slice_in_dim(
-                mixed, (plane ^ kz) * token_rows, token_rows, 1
-            )
-            out_parts.append(scatter_tensor(quarters(by_rows(chunk, w_hidden[2 * slice_width :]))))
-    else:
-        branch = scatter_tensor(quarters(by_cols(attn_out, w_output)))
-        middle_rows = states_quarter + branch
-        ffn_in = rounded(normed(middle_rows, gains[1]))
-
-        ffn_ins = gather_group(ffn_in)
-        mixed_chunks, d_chunks, back_parts, out_parts = [], [], [], []
-        for down_grad, ffn_chunk in zip(down_grads, ffn_ins):
-            gate_up = product(ffn_chunk, w_gate_up)
-            gate_pre, up_pre = gate_up[:, :slice_width], gate_up[:, slice_width:]
-            sigmoid_gate = jax.nn.sigmoid(gate_pre)
-            mixed = rounded(gate_pre * sigmoid_gate * up_pre)
-            d_mixed = product(down_grad, w_down)
-            d_gate = d_mixed * up_pre * sigmoid_gate * (1.0 + gate_pre * (1.0 - sigmoid_gate))
-            d_up = d_mixed * gate_pre * sigmoid_gate
-            d_gate_up = jnp.concatenate([rounded(d_gate), rounded(d_up)], axis=1)
-            mixed_chunks.append(mixed)
-            d_chunks.append(d_gate_up)
-
-            def reduced(value):
-                blocks = value.reshape(4, quarter, width)
-                return scatter_tensor([blocks[0], blocks[2], blocks[1], blocks[3]])
-
-            back_parts.append(reduced(by_cols(d_gate_up, w_gate_up)))
-            out_parts.append(reduced(by_cols(mixed, w_down)))
-        d_ffn_in = scatter_planes(back_parts)
-
-        d_middle, d_gain_ffn = norm_back(middle_rows, gains[1], d_ffn_in)
-        grad_middle = quarter_of(out_grad).astype(F32) + d_middle
-        output_grad = in_order(gather_tensor(rounded(grad_middle)))
-        d_wout = by_rows(output_grad, attn_out)
-        d_heads = rounded(product(output_grad, w_output))
-
-    d_pairs = to_pairs(d_heads.reshape(token_rows, heads_here, HEAD_WIDTH))
+    d_middle, d_gain_ffn = norm_back(middle, gains[1], d_ffn_in)
+    grad_middle = quarter_of(out_grad).astype(F32) + d_middle
+    output_grad = in_order(gather_tensor(rounded(grad_middle)))
+
+    d_wout = by_rows(output_grad, attn_out)
+    d_heads = rounded(product(output_grad, w_output)).reshape(token_rows, heads_here, HEAD_WIDTH)
+    d_pairs = to_pairs(d_heads)
     delta = jnp.sum(d_pairs.astype(F32) * attended[..., :HEAD_WIDTH], axis=-1)
     d_query, d_keyvalue = attend_back(
         counts,
@@ -834,35 +1532,30 @@
 
     d_wattend = scatter_dp(by_rows(attn_in, d_lin).reshape(dp_ranks, weight_rows, -1))
     d_wout = scatter_dp(d_wout.reshape(dp_ranks, weight_rows, -1))
-    if not kernels:
-        ffn_all = jnp.concatenate(ffn_ins, axis=0)
-        down_all = jnp.concatenate(down_grads, axis=0)
-        grads_hidden = jnp.concatenate(
-            [
-                by_rows(ffn_all, jnp.concatenate(d_chunks, axis=0)),
-                by_rows(down_all, jnp.concatenate(mixed_chunks, axis=0)),
-            ],
-            axis=1,
-        ).reshape(dp_ranks, weight_rows, 3 * slice_width)
-        collected = jnp.zeros((PLANES, weight_rows, 3 * slice_width), F32)
-        for kz in range(PLANES):
-            total = lax.dynamic_index_in_dim(grads_hidden, rank ^ (kz * lines), 0, keepdims=False)
-            for ky in range(1, lines):
-                piece = lax.dynamic_index_in_dim(
-                    grads_hidden, rank ^ (kz * lines + ky), 0, keepdims=False
-                )
-                total = total + send(rounded(piece), ky=ky).astype(F32)
-            if kz:
-                total = send(rounded(total), kz=kz).astype(F32)
-            collected = lax.dynamic_update_index_in_dim(collected, total, plane ^ kz, 0)
+    ffn_all = jnp.concatenate(ffn_ins, axis=0)
+    down_all = jnp.concatenate(down_grads, axis=0)
+    grads_hidden = jnp.concatenate(
+        [
+            by_rows(ffn_all, jnp.concatenate(d_chunks, axis=0)),
+            by_rows(down_all, jnp.concatenate(mixed_chunks, axis=0)),
+        ],
+        axis=1,
+    ).reshape(dp_ranks, weight_rows, 3 * slice_width)
+    collected = jnp.zeros((PLANES, weight_rows, 3 * slice_width), F32)
+    for kz in range(PLANES):
+        total = lax.dynamic_index_in_dim(grads_hidden, rank ^ (kz * lines), 0, keepdims=False)
+        for ky in range(1, lines):
+            piece = lax.dynamic_index_in_dim(
+                grads_hidden, rank ^ (kz * lines + ky), 0, keepdims=False
+            )
+            total = total + send(rounded(piece), ky=ky).astype(F32)
+        if kz:
+            total = send(rounded(total), kz=kz).astype(F32)
+        collected = lax.dynamic_update_index_in_dim(collected, total, plane ^ kz, 0)
 
     def unsliced(index):
-        columns = slice(index * slice_width, (index + 1) * slice_width)
-        if kernels:
-            piece = collected[:, columns].transpose(2, 0, 1).astype(F32)
-        else:
-            piece = collected[:, :, columns].transpose(1, 0, 2)
-        return piece.reshape(1, weight_rows, hidden)
+        piece = collected[:, :, index * slice_width : (index + 1) * slice_width]
+        return piece.transpose(1, 0, 2).reshape(1, weight_rows, hidden)
 
     kv_grad = d_wattend[:, head_width:]
     spread = jnp.zeros((weight_rows, 2 * value_start), F32)
@@ -872,7 +1565,7 @@
     )
     d_wkeyvalue = lax.psum(spread, "tensor")
 
-    result_quarter = rounded(middle_rows + scatter_planes(out_parts))
+    result_quarter = rounded(middle + scatter_planes(out_parts))
     result = in_order(gather_tensor(result_quarter))
 
     small = jnp.concatenate([d_gain_attn, d_gain_ffn, d_querygain, d_keygain])
@@ -893,6 +1586,13 @@
         small[2 * width : 2 * width + HEAD_WIDTH][None],
         small[2 * width + HEAD_WIDTH :][None],
     )
+
+
+def local(*arguments):
+    rows = arguments[0].shape[1] // lax.axis_size("dp")
+    if lax.axis_size("dp") == 2 * PLANES and lax.axis_size("tensor") == 4 and rows % 128 == 0:
+        return local_kernels(*arguments)
+    return local_permutes(*arguments)
 
 
 def solution(mesh):

time: 880 us -> 535 us (0.61)
  Pallas kernels: 206 us -> 487 us
  local copies, waits for them, and re-layouts: 290 us -> 18.8 us
  waiting for transfers between devices: 177 us -> 0 us
  starting transfers between devices: 86.3 us -> 0 us
  blocking collectives: 37 us -> 0 us
  other arithmetic: 36.2 us -> 17.8 us
  between operations: 16.3 us -> 1.09 us
  matrix products: 14.6 us -> 0 us
    pallas_call x0 -> x2, Pallas kernels: none -> 287 us  [the longest x1 147 us: front(): pl.pallas_call(functools.partial(front_kernel, lines, heads), out_shape=(...]
    dynamic_update_slice x66 -> x0, local copies, waits for them, and re-layouts: 215 us -> none  [the longest x8 166 us: local(): lax.dynamic_update_index_in_dim(w_hidden, got, rank ^ kz * lines + ky, 0)]
    ppermute x84 -> x0, waiting for transfers between devices: 177 us -> none  [send(): return lax.ppermute(value, ('dp', 'tensor'), pairs)]
    ppermute x84 -> x0, starting transfers between devices: 86.3 us -> none  [send(): return lax.ppermute(value, ('dp', 'tensor'), pairs)]
    psum x1 -> x0, blocking collectives: 37 us -> none  [local(): small = lax.psum(small, ('dp', 'tensor'))]
    broadcast_in_dim x31 -> x2, local copies, waits for them, and re-layouts: 26.6 us -> 1.19 us  [the longest x1 0.61 us: local_kernels(): delta[:, :, None, :]]
    unnamed x150 -> x29, local copies, waits for them, and re-layouts: 22.3 us -> 6.79 us
    dot_general x8 -> x0, matrix products: 14.6 us -> none  [the longest x6 8.12 us: by_rows(): lax.dot_general(left_side, right_side, (((0,), (0,)), ((), ())), preferre...]
  transfers between devices with their start and end apart: 85 -> 0, of which waited for: 28 -> 0; matrix products, arithmetic and copies ran while one was open for 37% -> 0% of each run, Pallas kernels for 2% -> 0%
where the time goes in v3:
time: 535 us; the launch traced here: 525 us
  Pallas kernels  487 us (91%)
  local copies, waits for them, and re-layouts  18.8 us (4%)
  other arithmetic  17.8 us (3%)
    pallas_call x1, Pallas kernels, middle(): pl.pallas_call(functools.partial(middle_kernel, lines, slice_width), out_...  168 us
    pallas_call x1, Pallas kernels, front(): pl.pallas_call(functools.partial(front_kernel, lines, heads), out_shape=(...  147 us
    pallas_call x1, Pallas kernels, tail(): pl.pallas_call(functools.partial(tail_kernel, lines, heads), out_shape=(s...  140 us
    pallas_call x1, Pallas kernels, attend_back(): pl.pallas_call(attend_back_kernel, out_shape=(jax.ShapeDtypeStruct((block...  21.7 us

profile of v3, /device:TPU:0, one launch (start us, length us, event | category | flops | bytes accessed | tf_op | source)
XLA Modules:
  0.0 524.8 jit_solution(4158442981374018782)
XLA Ops:
  0.7 0.8 dynamic_slice.20
  6.0 1.3 pad_convert_fusion.gains_in
  7.3 1.1 dynamic-slice_bitcast_fusion.1
  8.4 1.7 pad_maximum_fusion.1.w_attend_in
  10.1 1.5 fusion
  11.6 2.4 pad_maximum_fusion.w_hidden_in
  14.0 147.3 %front.1 = (f32[384,640]{1,0:T(8,128)}, bf16[384,2048]{1,0:T(8,128)(2,1)}, bf16[3,3,256,64]{3,2,1,0:T(8,128)(2,1)}, bf16[3072,256]{1,0:T(8,128)(2,1)}, f32[8,204...) custom-call(bf16[384,2048]{1,0:T(8,128)(2,1)} %states_ref.5, ...), custom_call_target="tpu_custom_call" | custom-call | tf_op jit(solution)/shard_map/front/pallas_call | solution.py:745
  161.4 1.4 slice.74.gain_ref
  162.8 1.4 copy-done.2
  164.2 1.1 copy-done.3
  165.3 10.2 %attend.1 = f32[3,3,256,128]{3,2,1,0:T(8,128)S(1)} custom-call(s32[3]{0:T(128)S(1)} %get-tuple-element.59.count_ref, s32[3,24]{1,0:T(4,128)S(1)} %select_reduce_fusion.slots_ref, s32[1]{0:T(128)} %bitcast.parity_ref, bf16[3,3,256,64]{3,2,1,0:T(8,128)(2,1)S(1)} %copy-done.3, bf16[24,128,256]{2,1,0:T(8,128)(2,1)S(1)} %bitcast.73), custom_call_target="tpu_custom_call" | custom-call | flops 2013265920 | bytes 8388608 | tf_op jit(solution)/shard_map/attend/pallas_call | solution.py:116
  176.0 0.9 copy.34.attn_ref.attn_out_ref
  176.9 168.0 %middle.1 = (f32[96,2048]{1,0:T(8,128)}, f32[96,2048]{1,0:T(8,128)}, f32[1,2048]{1,0:T(1,128)}, bf16[384,384]{1,0:T(8,128)(2,1)}, bf16[384,2048]{1,0:T(8,128)(2,...) custom-call(bf16[384,384]{1,0:T(8,128)(2,1)} %copy.34.attn_ref.attn_out_ref, bf16[384,2048]{1,0:T(8,128)(2,1)} %states_ref.5, ...), custom_call_target="tpu_custom_call" | custom-call | tf_op jit(solution)/shard_map/middle/pallas_call | solution.py:501
  344.9 1.2 copy.35
  348.1 1.0 copy.39
  349.1 21.7 %attend_back.1 = (f32[3,3,256,64]{3,2,1,0:T(8,128)}, f32[24,128,256]{2,1,0:T(8,128)}) custom-call(s32[3]{0:T(128)} %copy-done.1, s32[3,24]{1,0:T(4,128)} %copy-done, s32[1]{0:T(128)} %bitcast.parity_ref, bf16[3,3,256,64]{3,2,1,0:T(8,128)(2,1)} %get-tuple-element.35.q_ref, bf16[3,3,256,64]{3,2,1,0:T(8,128)(2,1)} %bitcast.75, f32[3,3,1,256]{3,2,1,0:T(1,128)} %bitcast.92, ...), custom_call_target="tpu_custom_call" | custom-call | flops 5033164800 | bytes 8388608 | tf_op jit(solution)/shard_map/attend_back/pallas_call | solution.py:187
  370.8 139.8 %tail.1 = (bf16[384,2048]{1,0:T(8,128)(2,1)}, bf16[384,2048]{1,0:T(8,128)(2,1)}, f32[256,384]{1,0:T(8,128)}, f32[256,384]{1,0:T(8,128)}, bf16[4,256,256]{2,1,0:T(8,128)(2,1)}, /*index=5*/f32[8,2048]{1,0:T(8,128)}) custom-call(f32[3072,256]{1,0:T(8,128)} %bitcast.74, f32[3,3,256,64]{3,2,1,0:T(8,128)} %get-tuple-element.43.d_query_ref, ...), custom_call_target="tpu_custom_call" | custom-call | tf_op jit(solution)/shard_map/tail/pallas_call | solution.py:1072
  512.7 0.8 slice.91
  514.7 1.2 bitcast_convert_fusion.3
  516.0 1.2 add_bitcast_fusion
  517.5 2.0 convert_element_type.94
  519.5 2.0 slice_convert_fusion.1
  521.8 1.1 copy.46
  523.8 0.7 copy.48
  (54 shorter events, 11.7 us)
Async XLA Ops:
  0.6 11.0 %copy-start.8 = (bf16[1,256,1216]{1,2,0:T(8,128)(2,1)S(1)}, bf16[1,256,1216]{1,2,0:T(8,128)(2,1)}, u32[]{:S(2)}) copy-start(bf16[1,256,1216]{1,2,0:T(8,128)(2,1)} %param.19) | copy-start | bytes 1867780
  0.7 10.9 %copy-start.9 = (bf16[1,256,1216]{1,2,0:T(8,128)(2,1)S(1)}, bf16[1,256,1216]{1,2,0:T(8,128)(2,1)}, u32[]{:S(2)}) copy-start(bf16[1,256,1216]{1,2,0:T(8,128)(2,1)} %param.18) | copy-start | bytes 1867780
  3.0 159.8 %copy-start.1 = (s32[3]{0:T(128)}, s32[3]{0:T(128)S(1)}, u32[]{:S(2)}) copy-start(s32[3]{0:T(128)S(1)} %get-tuple-element.59.count_ref) | copy-start | bytes 40
  4.7 158.1 %copy-start = (s32[3,24]{1,0:T(4,128)}, s32[3,24]{1,0:T(4,128)S(1)}, u32[]{:S(2)}) copy-start(s32[3,24]{1,0:T(4,128)S(1)} %select_reduce_fusion.slots_ref) | copy-start | bytes 868
  162.8 1.4 copy-start.2
  164.2 1.1 copy-start.3
  346.5 1.6 copy-start.4
  515.9 1.5 copy-start.7
  517.5 2.0 copy-start.5
  519.5 2.3 copy-start.6
  521.8 1.2 copy-start.11
  521.8 2.0 copy-start.10

commit v4 on v1

--- a/solution.py
+++ b/solution.py
@@ -14,6 +14,7 @@
 EPSILON = 1e-06
 PLANES = 4
 PAIRS = 3
+LONGEST = 12
 LOG2E = 1.4426950408889634
 BF16 = jnp.bfloat16
 F32 = jnp.float32
@@ -200,7 +201,1217 @@
     )(counts, slots, parity, queries, d_out, logs, delta, keyvalues)
 
 
-def local(
+class Place:
+    def __init__(self, lines):
+        rank, part = lax.axis_index("dp"), lax.axis_index("tensor")
+        self.lines = lines
+        self.z, self.y = rank // lines, lax.rem(rank, lines)
+        self.x, self.c = part // 2, lax.rem(part, 2)
+        self.quarter = self.c * 2 + self.x
+
+    def plane(self, move):
+        if move == 0:
+            return self.z
+        if move == 1:
+            return self.z + 1 - 2 * lax.rem(self.z, 2)
+        if move == 2:
+            return self.z + 2 - 4 * (self.z // 2)
+        return 3 - self.z
+
+    def to(self, kz=0, ky=0, kx=0, kc=0):
+        y = 1 - self.y if ky else self.y
+        x = 1 - self.x if kx else self.x
+        c = 1 - self.c if kc else self.c
+        return (self.plane(kz) * self.lines + y, x * 2 + c)
+
+
+class Links:
+    def __init__(self, place, send_sems, recv_sems):
+        self.place, self.send_sems, self.recv_sems = place, send_sems, recv_sems
+        self.number, self.unsent = 0, []
+
+    def greet(self, moves):
+        barrier = pltpu.get_barrier_semaphore()
+        for move in moves:
+            pl.semaphore_signal(
+                barrier, inc=1, device_id=self.place.to(**move), device_id_type=pl.DeviceIdType.MESH
+            )
+        pl.semaphore_wait(barrier, len(moves))
+
+    def send(self, source, target, **move):
+        number, self.number = self.number, self.number + 1
+        copy = pltpu.make_async_remote_copy(
+            src_ref=source,
+            dst_ref=target,
+            send_sem=self.send_sems.at[number],
+            recv_sem=self.recv_sems.at[number],
+            device_id=self.place.to(**move),
+            device_id_type=pl.DeviceIdType.MESH,
+        )
+        copy.start()
+        self.unsent.append(copy)
+        return copy
+
+    def sent(self, copy):
+        copy.wait_send()
+        self.unsent = [other for other in self.unsent if other is not copy]
+
+    def finish(self):
+        for copy in self.unsent:
+            copy.wait_send()
+
+
+def rows_at(index, size):
+    return pl.ds(pl.multiple_of(index * size, size), size)
+
+
+class Gather:
+    def __init__(self, links, block, own=None):
+        self.links, self.block, self.y = links, block, links.place.y
+        self.own = block(0, self.y) if own is None else own
+        self.lines = []
+
+    def over_lines(self, move):
+        place = self.block(move, self.y)
+        source = self.own if move == 0 else place
+        self.lines.append(self.links.send(source, place, ky=1))
+
+    def start(self):
+        place = self.block(0, self.y)
+        self.far = self.links.send(self.own, place, kz=2)
+        self.near = self.links.send(self.own, place, kz=1)
+        self.over_lines(0)
+
+    def relay(self):
+        self.near.wait_recv()
+        self.over_lines(1)
+        self.far.wait_recv()
+        place = self.block(2, self.y)
+        self.corner = self.links.send(place, place, kz=1)
+        self.over_lines(2)
+
+    def last(self):
+        self.corner.wait_recv()
+        self.over_lines(3)
+
+    def finish(self):
+        for copy in self.lines:
+            copy.wait_recv()
+
+
+def head_mean(value):
+    row = lax.broadcasted_iota(jnp.int32, (128, 128), 0) // HEAD_WIDTH
+    column = lax.broadcasted_iota(jnp.int32, (128, 128), 1) // HEAD_WIDTH
+    average = jnp.where(row == column, 1.0 / HEAD_WIDTH, 0.0).astype(F32)
+    return jnp.dot(
+        value, average, preferred_element_type=F32, precision=lax.Precision.HIGHEST
+    )
+
+
+def halves_swapped(value):
+    first = lax.rem(lax.broadcasted_iota(jnp.int32, value.shape, 1), HEAD_WIDTH) < HEAD_WIDTH // 2
+    return jnp.where(
+        first,
+        pltpu.roll(value, 128 - HEAD_WIDTH // 2, 1),
+        pltpu.roll(value, HEAD_WIDTH // 2, 1),
+    )
+
+
+class Scatter:
+    ORDER = (3, 1, 2, 0)
+
+    def __init__(self, links, y_out, y_in, z_out, z_in, sums):
+        self.links = links
+        self.y_out, self.y_in, self.z_out, self.z_in, self.sums = y_out, y_in, z_out, z_in, sums
+        self.lines, self.planes = {}, {}
+
+    def start(self, move, block):
+        self.y_out[move] = block.astype(BF16)
+        self.lines[move] = self.links.send(self.y_out.at[move], self.y_in.at[move], ky=1)
+
+    def add(self, move, block):
+        self.lines[move].wait_recv()
+        total = block + self.y_in[move].astype(F32)
+        if move in (3, 1):
+            slot = 0 if move == 1 else 1
+            self.z_out[slot] = total.astype(BF16)
+            self.planes[slot] = self.links.send(self.z_out.at[slot], self.z_in.at[slot], kz=1)
+        elif move == 2:
+            self.planes[1].wait_recv()
+            self.z_out[2] = (total + self.z_in[1].astype(F32)).astype(BF16)
+            self.planes[2] = self.links.send(self.z_out.at[2], self.z_in.at[2], kz=2)
+        else:
+            self.sums[...] = total
+
+    def finish(self):
+        self.planes[0].wait_recv()
+        self.planes[2].wait_recv()
+        return self.sums[...] + self.z_in[0].astype(F32) + self.z_in[2].astype(F32)
+
+
+def scatter_scratch(block):
+    return [
+        pltpu.VMEM((4, *block), BF16),
+        pltpu.VMEM((4, *block), BF16),
+        pltpu.VMEM((3, *block), BF16),
+        pltpu.VMEM((3, *block), BF16),
+        pltpu.VMEM(block, F32),
+    ]
+
+
+FORWARD_COPIES = 100
+
+
+def forward_kernel(
+    lines,
+    heads,
+    slice_width,
+    longest,
+    sequence_ref,
+    offset_ref,
+    states_ref,
+    gains_in,
+    w_attend_in,
+    cosine_ref,
+    sine_ref,
+    head_gain_ref,
+    w_output_in,
+    w_hidden_in,
+    grad_any,
+    lin_ref,
+    attn_in_ref,
+    query_ref,
+    kv_ref,
+    attended_ref,
+    attn_out_ref,
+    gains_ref,
+    w_attend_ref,
+    middle_ref,
+    back_ref,
+    gain_out_ref,
+    d_heads_ref,
+    output_grad_ref,
+    mixed_ref,
+    collected_ref,
+    table_ref,
+    w_down_any,
+    acc_ref,
+    w_output_ref,
+    w_hidden_ref,
+    down_ref,
+    ffn_ref,
+    d_hidden_ref,
+    partial_ref,
+    core_out,
+    core_in,
+    x_out,
+    x_in,
+    sums_ref,
+    z_out,
+    z_in,
+    y_out,
+    y_in,
+    local_sems,
+    send_sems,
+    recv_sems,
+):
+    here = Place(lines)
+    links = Links(here, send_sems, recv_sems)
+    token_rows, width = states_ref.shape
+    quarter = token_rows // 4
+    half = 2 * quarter
+    weight_rows = w_attend_in.shape[0]
+    hidden = slice_width
+    blocks = token_rows // STRETCH
+    slot_count = offset_ref.shape[0]
+    mine, my_half = rows_at(here.quarter, quarter), rows_at(here.c, half)
+    other_half = rows_at(1 - here.c, half)
+    x_mine, x_other = rows_at(here.x, quarter), rows_at(1 - here.x, quarter)
+    odd = here.c == 1
+
+    def rank(move, line):
+        return here.plane(move) * lines + line
+
+    def rows_of(ref, columns=slice(None)):
+        return lambda move, line: ref.at[rows_at(rank(move, line), weight_rows), columns]
+
+    def columns_of(ref):
+        return lambda move, line: ref.at[:, rows_at(rank(move, line), weight_rows)]
+
+    loads = [
+        pltpu.make_async_copy(grad_any, down_ref.at[here.z], local_sems.at[0]),
+        pltpu.make_async_copy(w_output_in, rows_of(w_output_ref)(0, here.y), local_sems.at[1]),
+        pltpu.make_async_copy(
+            w_hidden_in.at[here.z], columns_of(w_hidden_ref)(0, here.y), local_sems.at[2]
+        ),
+    ]
+    for load in loads:
+        load.start()
+    links.greet([dict(kc=1), dict(kx=1), dict(ky=1), dict(kz=1), dict(kz=2), dict(kz=3)])
+
+    kv_width = 4 * HEAD_WIDTH
+    gains = Gather(links, columns_of(gains_ref), gains_in)
+    gains.start()
+    first, second = slice(0, kv_width), slice(kv_width, w_attend_in.shape[1])
+    kv_weights = Gather(links, rows_of(w_attend_ref, first), w_attend_in.at[:, first])
+    kv_weights.start()
+    query_weights = Gather(links, rows_of(w_attend_ref, second), w_attend_in.at[:, second])
+    query_weights.start()
+    columns_of(gains_ref)(0, here.y)[...] = gains_in[...]
+    rows_of(w_attend_ref)(0, here.y)[...] = w_attend_in[...]
+
+    def fill(index, carry):
+        block, place = index // longest, lax.rem(index, longest)
+        sequence = sequence_ref[rank(0, here.y) * blocks + block]
+        found = jnp.int32(0)
+        for slot in range(slot_count):
+            same = (sequence_ref[slot] == sequence) & (offset_ref[slot] == place * STRETCH)
+            found = jnp.where(same, slot, found)
+        table_ref[index] = found
+        return carry
+
+    lax.fori_loop(0, blocks * longest, fill, 0)
+    gains.relay()
+    gains.last()
+    gains.finish()
+    states = states_ref[...].astype(F32)
+    inverse = lax.rsqrt(jnp.mean(states * states, axis=-1, keepdims=True) + EPSILON)
+    attn_in_ref[...] = (states * inverse * gains_ref[0:1, :]).astype(BF16)
+
+    def turned(value, group):
+        value = (
+            value
+            * lax.rsqrt(head_mean(value * value) + EPSILON)
+            * head_gain_ref[:, group * 128 : (group + 1) * 128]
+        )
+        return (value * cosine_ref[...] + halves_swapped(value) * sine_ref[...]).astype(BF16)
+
+    kv_weights.relay()
+    kv_weights.last()
+    query_weights.relay()
+    kv_weights.finish()
+    lin = product(attn_in_ref[...], w_attend_ref[:, first])
+    lin_ref[:, first] = lin
+    own_blocks = pl.ds(rank(0, here.y) * blocks, blocks)
+    kv_ref[own_blocks, :, :128] = turned(lin[:, :128], 0).reshape(blocks, STRETCH, 128)
+    kv_ref[own_blocks, :, 128:] = lin[:, 128:].astype(BF16).reshape(blocks, STRETCH, 128)
+    keyvalue = Gather(
+        links, lambda move, line: kv_ref.at[pl.ds(rank(move, line) * blocks, blocks)]
+    )
+    keyvalue.start()
+    query_weights.last()
+    query_weights.finish()
+    output = Gather(links, rows_of(w_output_ref), w_output_in)
+    output.start()
+    lin = product(attn_in_ref[...], w_attend_ref[:, second])
+    lin_ref[:, second] = lin
+    for pair in range(PAIRS):
+        rotated_pair = turned(lin[:, pair * 128 : (pair + 1) * 128], pair + 1)
+        for block in range(blocks):
+            rows = rotated_pair[block * STRETCH : (block + 1) * STRETCH]
+            query_ref[block, pair, :STRETCH] = rows[:, :HEAD_WIDTH]
+            query_ref[block, pair, STRETCH:] = rows[:, HEAD_WIDTH:]
+    keyvalue.relay()
+
+    planes = [
+        links.send(w_hidden_in.at[here.plane(move)], columns_of(w_hidden_ref)(0, here.y), kz=move)
+        for move in (1, 2, 3)
+    ]
+    hidden_lines = []
+
+    def hidden_line(move):
+        if move:
+            planes[move - 1].wait_recv()
+        else:
+            loads[2].wait()
+        place = columns_of(w_hidden_ref)(move, here.y)
+        hidden_lines.append(links.send(place, place, ky=1))
+
+    def down_block(move):
+        return down_ref.at[here.plane(move), mine]
+
+    loads[0].wait()
+    down_far = links.send(down_block(0), down_block(0), kz=2)
+    down_near = links.send(down_block(0), down_block(0), kz=1)
+    down_across, down_cores = {}, {}
+
+    def down_x(move):
+        down_across[move] = links.send(down_block(move), down_block(move), kx=1)
+
+    def down_core(move):
+        down_across[move].wait_recv()
+        both = down_ref.at[here.plane(move), my_half]
+        down_cores[move] = links.send(both, both, kc=1)
+
+    keyvalue.last()
+    hidden_line(0)
+    keyvalue.finish()
+
+    ones = jnp.ones((STRETCH, HEAD_WIDTH), BF16)
+
+    def attend_block(block):
+        acc_ref[...] = jnp.zeros_like(acc_ref)
+        offset = offset_ref[rank(0, here.y) * blocks + block]
+        shape = (2 * STRETCH, STRETCH)
+        ahead = lax.broadcasted_iota(jnp.int32, shape, 1) - lax.rem(
+            lax.broadcasted_iota(jnp.int32, shape, 0), STRETCH
+        )
+
+        def step(place, carry):
+            slot = table_ref[block * longest + place]
+            tile = kv_ref[slot]
+            keys = [tile[:, :64], tile[:, 64:128]]
+            values = [
+                jnp.concatenate([tile[:, 128:192], ones], axis=1),
+                jnp.concatenate([tile[:, 192:256], ones], axis=1),
+            ]
+            middle_key = jnp.where(odd, keys[1], keys[0])
+            middle_value = jnp.where(odd, values[1], values[0])
+            visible = ahead <= offset - place * STRETCH
+            for pair, key, value in (
+                (0, keys[0], values[0]),
+                (1, middle_key, middle_value),
+                (2, keys[1], values[1]),
+            ):
+                scores = by_cols(query_ref[block, pair], key)
+                weights = jnp.exp2(scores * (LOG2E * HEAD_WIDTH**-0.5))
+                weights = jnp.where(visible, weights, 0.0)
+                acc_ref[pair] += product(weights.astype(BF16), value)
+            return carry
+
+        lax.fori_loop(0, longest, step, 0)
+        for pair in range(PAIRS):
+            total = acc_ref[pair]
+            denominator = total[:, HEAD_WIDTH:]
+            heads_out = total[:, :HEAD_WIDTH] / denominator
+            attended_ref[block, pair] = jnp.concatenate(
+                [heads_out, jnp.log2(denominator)], axis=1
+            )
+            attn_out_ref[
+                block * STRETCH : (block + 1) * STRETCH, pair * 128 : (pair + 1) * 128
+            ] = jnp.concatenate([heads_out[:STRETCH], heads_out[STRETCH:]], axis=1).astype(BF16)
+
+    attend_block(0)
+    output.relay()
+    hidden_line(1)
+    output.last()
+    attend_block(1)
+    down_near.wait_recv()
+    down_x(1)
+    hidden_line(2)
+    attend_block(2)
+    down_far.wait_recv()
+    down_corner = links.send(down_block(2), down_block(2), kz=1)
+    down_x(2)
+
+    loads[1].wait()
+    output.finish()
+    cut = 4
+    piece = width // cut
+    core_copies = []
+    for part in range(cut):
+        columns = slice(part * piece, (part + 1) * piece)
+        weight = w_output_ref[columns, :]
+        core_out[4, :, columns] = by_cols(attn_out_ref[other_half, :], weight).astype(BF16)
+        core_copies.append(
+            links.send(core_out.at[4, :, columns], core_in.at[4, :, columns], kc=1)
+        )
+        partial_ref[0, :half, columns] = by_cols(attn_out_ref[my_half, :], weight)
+    x_copies = []
+    for part in range(cut):
+        columns = slice(part * piece, (part + 1) * piece)
+        core_copies[part].wait_recv()
+        x_out[4, :, columns] = (
+            partial_ref[0, x_other, columns] + core_in[4, x_other, columns].astype(F32)
+        ).astype(BF16)
+        x_copies.append(links.send(x_out.at[4, :, columns], x_in.at[4, :, columns], kx=1))
+        middle_ref[:, columns] = (
+            states_ref[mine, columns].astype(F32)
+            + partial_ref[0, x_mine, columns]
+            + core_in[4, x_mine, columns].astype(F32)
+        )
+    for part in range(cut):
+        columns = slice(part * piece, (part + 1) * piece)
+        x_copies[part].wait_recv()
+        middle_ref[:, columns] += x_in[4, :, columns].astype(F32)
+    middle = middle_ref[...]
+    inverse = lax.rsqrt(jnp.mean(middle * middle, axis=-1, keepdims=True) + EPSILON)
+    ffn_ref[here.z, mine, :] = (middle * inverse * gains_ref[1:2, :]).astype(BF16)
+
+    def block_of(move):
+        return ffn_ref.at[here.plane(move), mine]
+
+    far = links.send(block_of(0), block_of(0), kz=2)
+    near = links.send(block_of(0), block_of(0), kz=1)
+    across = {0: links.send(block_of(0), block_of(0), kx=1)}
+    down_core(1)
+    hidden_line(3)
+    down_corner.wait_recv()
+    near.wait_recv()
+    across[1] = links.send(block_of(1), block_of(1), kx=1)
+    down_x(3)
+    far.wait_recv()
+    corner = links.send(block_of(2), block_of(2), kz=1)
+    across[2] = links.send(block_of(2), block_of(2), kx=1)
+    cores = {}
+
+    def spread(move):
+        across[move].wait_recv()
+        both = ffn_ref.at[here.plane(move), my_half]
+        cores[move] = links.send(both, both, kc=1)
+
+    spread(0)
+    down_core(2)
+    for copy in hidden_lines:
+        copy.wait_recv()
+
+    core_copies, x_copies = [], []
+
+    def add_cores(move):
+        core_copies[move].wait_recv()
+        total_rows = rows_at(here.c * 2 + 1 - here.x, quarter)
+        x_out[move] = (
+            partial_ref[move % 2, total_rows, :] + core_in[move, x_other, :].astype(F32)
+        ).astype(BF16)
+        x_copies.append(links.send(x_out.at[move], x_in.at[move], kx=1))
+        sums_ref[move] = partial_ref[move % 2, mine, :] + core_in[move, x_mine, :].astype(F32)
+
+    def add_x(move):
+        x_copies[move].wait_recv()
+        sums_ref[move] += x_in[move].astype(F32)
+
+    for move in range(4):
+        if move == 2:
+            corner.wait_recv()
+            across[3] = links.send(block_of(3), block_of(3), kx=1)
+        cores[move].wait_recv()
+        if move:
+            down_cores[move].wait_recv()
+        plane = here.plane(move)
+        chunk = ffn_ref[plane]
+        gate_pre = by_cols(w_hidden_ref[:hidden, :], chunk)
+        up_pre = by_cols(w_hidden_ref[hidden : 2 * hidden, :], chunk)
+        sigmoid_gate = 1.0 / (1.0 + jnp.exp(-gate_pre))
+        silu = gate_pre * sigmoid_gate
+        columns = pl.ds(pl.multiple_of(plane * token_rows, token_rows), token_rows)
+        mixed_ref[:, columns] = (silu * up_pre).astype(BF16)
+        d_mixed = by_cols(w_hidden_ref[2 * hidden :, :], down_ref[plane])
+        d_hidden_ref[:hidden, columns] = (
+            d_mixed * up_pre * sigmoid_gate * (1.0 + gate_pre * (1.0 - sigmoid_gate))
+        ).astype(BF16)
+        d_hidden_ref[hidden:, columns] = (d_mixed * silu).astype(BF16)
+        partial_ref[move % 2] = by_rows(d_hidden_ref[:, columns], w_hidden_ref[: 2 * hidden, :])
+        core_out[move] = partial_ref[move % 2, other_half, :].astype(BF16)
+        core_copies.append(links.send(core_out.at[move], core_in.at[move], kc=1))
+        if move == 0:
+            down_core(3)
+        if move > 0:
+            add_cores(move - 1)
+        if move + 1 < 4:
+            spread(move + 1)
+    add_cores(3)
+
+    def gradient(move, line):
+        columns = rows_at(rank(move, line), weight_rows)
+        first = jnp.zeros((2 * hidden, weight_rows), F32)
+        second = jnp.zeros((hidden, weight_rows), F32)
+        for plane in range(4):
+            tokens = slice(plane * token_rows, (plane + 1) * token_rows)
+            first += product(d_hidden_ref[:, tokens], ffn_ref[plane, :, columns])
+            second += product(mixed_ref[:, tokens], down_ref[plane, :, columns])
+        return first, second
+
+    y_copies = {}
+    for move in (3, 2, 1, 0):
+        first, second = gradient(move, 1 - here.y)
+        y_out[move, : 2 * hidden] = first.astype(BF16)
+        y_out[move, 2 * hidden :] = second.astype(BF16)
+        y_copies[move] = links.send(y_out.at[move], y_in.at[move], ky=1)
+
+    add_x(1)
+    z_out[0] = sums_ref[1].astype(BF16)
+    z_copies = [links.send(z_out.at[0], z_in.at[0], kz=1)]
+    add_x(0)
+    add_x(2)
+    add_x(3)
+    z_out[1] = sums_ref[3].astype(BF16)
+    z_copies.append(links.send(z_out.at[1], z_in.at[1], kz=1))
+    z_copies[1].wait_recv()
+    z_out[2] = (sums_ref[2] + z_in[1].astype(F32)).astype(BF16)
+    z_copies.append(links.send(z_out.at[2], z_in.at[2], kz=2))
+    g_copies = []
+
+    def send_gradient(move):
+        first, second = gradient(move, here.y)
+        y_copies[move].wait_recv()
+        target = y_out.at[move] if move else collected_ref.at[here.z]
+        if move:
+            links.sent(y_copies[move])
+        target[: 2 * hidden] = (first + y_in[move, : 2 * hidden].astype(F32)).astype(BF16)
+        target[2 * hidden :] = (second + y_in[move, 2 * hidden :].astype(F32)).astype(BF16)
+        if move:
+            g_copies.append(links.send(target, collected_ref.at[here.z], kz=move))
+
+    send_gradient(3)
+    z_copies[0].wait_recv()
+    z_copies[2].wait_recv()
+    d_normed = sums_ref[0] + z_in[0].astype(F32) + z_in[2].astype(F32)
+    middle = middle_ref[...]
+    inverse = lax.rsqrt(jnp.mean(middle * middle, axis=-1, keepdims=True) + EPSILON)
+    unit = middle * inverse
+    gain_out_ref[...] = jnp.sum(d_normed * unit, axis=0, keepdims=True)
+    scaled = d_normed * gains_ref[1:2, :]
+    back = inverse * (scaled - unit * jnp.mean(scaled * unit, axis=-1, keepdims=True))
+    grad_middle = down_ref[here.z, mine, :].astype(F32) + back
+    back_ref[...] = grad_middle
+    output_grad_ref[mine, :] = grad_middle.astype(BF16)
+    block = output_grad_ref.at[mine]
+    x_copy = links.send(block, block, kx=1)
+    send_gradient(2)
+    x_copy.wait_recv()
+    both = output_grad_ref.at[my_half]
+    core = links.send(both, both, kc=1)
+    send_gradient(1)
+    send_gradient(0)
+    save = pltpu.make_async_copy(
+        w_hidden_ref.at[pl.ds(2 * hidden, hidden)], w_down_any, local_sems.at[3]
+    )
+    save.start()
+    core.wait_recv()
+    d_heads_ref[...] = product(output_grad_ref[...], w_output_ref[...]).astype(BF16)
+    for copy in g_copies:
+        copy.wait_recv()
+    save.wait()
+    links.finish()
+
+
+def forward(
+    lines,
+    heads,
+    slice_width,
+    longest,
+    sequence,
+    offset,
+    states,
+    gains,
+    w_attend,
+    cosine,
+    sine,
+    head_gain,
+    w_output,
+    w_hidden,
+    grad,
+):
+    token_rows, width = states.shape
+    ranks = 4 * lines
+    quarter = token_rows // 4
+    half = 2 * quarter
+    hidden = slice_width
+    head_width = heads * HEAD_WIDTH
+    weight_rows = width // ranks
+    blocks = token_rows // STRETCH
+    vmem = pl.BlockSpec(memory_space=pltpu.VMEM)
+    smem = pl.BlockSpec(memory_space=pltpu.SMEM)
+    hbm = pl.BlockSpec(memory_space=pl.ANY)
+    shape = jax.ShapeDtypeStruct
+    return pl.pallas_call(
+        functools.partial(forward_kernel, lines, heads, slice_width, longest),
+        out_shape=(
+            shape((token_rows, w_attend.shape[1]), F32),
+            shape((token_rows, width), BF16),
+            shape((blocks, PAIRS, 2 * STRETCH, HEAD_WIDTH), BF16),
+            shape((ranks * blocks, STRETCH, 4 * HEAD_WIDTH), BF16),
+            shape((blocks, PAIRS, 2 * STRETCH, 128), F32),
+            shape((token_rows, head_width), BF16),
+            shape((gains.shape[0], width), F32),
+            shape((width, w_attend.shape[1]), BF16),
+            shape((quarter, width), F32),
+            shape((quarter, width), F32),
+            shape((1, width), F32),
+            shape((token_rows, head_width), BF16),
+            shape((token_rows, width), BF16),
+            shape((hidden, 4 * token_rows), BF16),
+            shape((4, 3 * hidden, weight_rows), BF16),
+            shape((blocks * longest,), jnp.int32),
+            shape((hidden, width), BF16),
+        ),
+        in_specs=[smem] * 2 + [vmem] * 6 + [hbm] * 3,
+        out_specs=(vmem,) * 15 + (smem, hbm),
+        scratch_shapes=[
+            pltpu.VMEM((PAIRS, 2 * STRETCH, 128), F32),
+            pltpu.VMEM((width, head_width), BF16),
+            pltpu.VMEM((3 * hidden, width), BF16),
+            pltpu.VMEM((4, token_rows, width), BF16),
+            pltpu.VMEM((4, token_rows, width), BF16),
+            pltpu.VMEM((2 * hidden, 4 * token_rows), BF16),
+            pltpu.VMEM((2, token_rows, width), F32),
+            pltpu.VMEM((5, half, width), BF16),
+            pltpu.VMEM((5, half, width), BF16),
+            pltpu.VMEM((5, quarter, width), BF16),
+            pltpu.VMEM((5, quarter, width), BF16),
+            pltpu.VMEM((4, quarter, width), F32),
+            pltpu.VMEM((3, quarter, width), BF16),
+            pltpu.VMEM((3, quarter, width), BF16),
+            pltpu.VMEM((4, 3 * hidden, weight_rows), BF16),
+            pltpu.VMEM((4, 3 * hidden, weight_rows), BF16),
+            pltpu.SemaphoreType.DMA((4,)),
+            pltpu.SemaphoreType.DMA((FORWARD_COPIES,)),
+            pltpu.SemaphoreType.DMA((FORWARD_COPIES,)),
+        ],
+        compiler_params=pltpu.CompilerParams(
+            collective_id=0, has_side_effects=True, vmem_limit_bytes=64 << 20
+        ),
+        name="forward",
+    )(
+        sequence,
+        offset,
+        states,
+        gains,
+        w_attend,
+        cosine,
+        sine,
+        head_gain,
+        w_output,
+        w_hidden,
+        grad,
+    )
+
+
+BACKWARD_COPIES = 60
+
+
+def backward_kernel(
+    lines,
+    heads,
+    longest,
+    sequence_ref,
+    offset_ref,
+    table_ref,
+    query_ref,
+    kv_ref,
+    attended_ref,
+    d_heads_ref,
+    lin_ref,
+    attn_in_ref,
+    output_grad_ref,
+    attn_out_ref,
+    w_attend_ref,
+    back_ref,
+    gains_ref,
+    gain_ffn_ref,
+    states_ref,
+    middle_ref,
+    mixed_ref,
+    cosine_ref,
+    sine_ref,
+    head_gain_ref,
+    w_down_any,
+    result_ref,
+    states_grad_ref,
+    g_attend_ref,
+    g_output_ref,
+    g_kv_ref,
+    small_ref,
+    *scratch,
+):
+    here = Place(lines)
+    (
+        w_down_ref,
+        d_query_ref,
+        d_kv_ref,
+        d_lin_ref,
+        partial_ref,
+        core_out,
+        core_in,
+        x_out,
+        x_in,
+        sums_ref,
+        z_out,
+        z_in,
+        small_out,
+        small_in,
+        local_sems,
+        send_sems,
+        recv_sems,
+    ) = scratch[:17]
+    links = Links(here, send_sems, recv_sems)
+    kv_sum = Scatter(links, *scratch[17:22])
+    output_sum = Scatter(links, *scratch[22:27])
+    attend_sum = Scatter(links, *scratch[27:32])
+    token_rows, width = states_ref.shape
+    quarter = token_rows // 4
+    half = 2 * quarter
+    weight_rows = width // (4 * lines)
+    kv_width = 4 * HEAD_WIDTH
+    blocks = token_rows // STRETCH
+    mine, other = rows_at(here.quarter, quarter), rows_at(here.c * 2 + 1 - here.x, quarter)
+    my_half, other_half = rows_at(here.c, half), rows_at(1 - here.c, half)
+    x_mine, x_other = rows_at(here.x, quarter), rows_at(1 - here.x, quarter)
+    odd = here.c == 1
+    scale = HEAD_WIDTH**-0.5
+
+    load = pltpu.make_async_copy(w_down_any, w_down_ref, local_sems.at[0])
+    load.start()
+    links.greet([dict(kc=1), dict(kx=1), dict(ky=1), dict(kz=1), dict(kz=2)])
+
+    def rank(move, line):
+        return here.plane(move) * lines + line
+
+    core_copies, x_copies = {}, {}
+    load.wait()
+
+    def out_start(move, slot):
+        at = pl.ds(pl.multiple_of(here.plane(move) * token_rows, token_rows), token_rows)
+        partial_ref[slot] = by_rows(mixed_ref[:, at], w_down_ref[...])
+        core_out[move] = partial_ref[slot, other_half, :].astype(BF16)
+        core_copies[move] = links.send(core_out.at[move], core_in.at[move], kc=1)
+
+    def add_cores(move, slot):
+        core_copies[move].wait_recv()
+        x_out[move] = (partial_ref[slot, other, :] + core_in[move, x_other, :].astype(F32)).astype(
+            BF16
+        )
+        x_copies[move] = links.send(x_out.at[move], x_in.at[move], kx=1)
+        sums_ref[move] = partial_ref[slot, mine, :] + core_in[move, x_mine, :].astype(F32)
+
+    def add_x(move):
+        x_copies[move].wait_recv()
+        sums_ref[move] += x_in[move].astype(F32)
+
+    def columns(move, line):
+        return rows_at(rank(move, line), weight_rows)
+
+    def output_block(move, line):
+        return by_rows(output_grad_ref[:, columns(move, line)], attn_out_ref[...])
+
+    def attend_grad(move, line):
+        return by_rows(attn_in_ref[:, columns(move, line)], d_lin_ref[...])
+
+    out_start(3, 0)
+    out_start(1, 1)
+    add_cores(3, 0)
+    out_start(2, 0)
+    add_cores(1, 1)
+    out_start(0, 1)
+    for move in Scatter.ORDER:
+        output_sum.start(move, output_block(move, 1 - here.y))
+    add_cores(2, 0)
+    add_cores(0, 1)
+
+    one_row = jnp.ones((8, HEAD_WIDTH), F32)
+    pick = jnp.where(
+        lax.broadcasted_iota(jnp.int32, (8, HEAD_WIDTH), 1) == 0, 1.0, 0.0
+    ).astype(F32)
+
+    def as_row(weights, value):
+        return lax.dot_general(
+            weights,
+            value,
+            (((1,), (1,)), ((), ())),
+            preferred_element_type=F32,
+            precision=lax.Precision.HIGHEST,
+        )[:1]
+
+    def attend_block(block):
+        offset = offset_ref[rank(0, here.y) * blocks + block]
+        rows = slice(block * STRETCH, (block + 1) * STRETCH)
+        shape = (STRETCH, 2 * STRETCH)
+        ahead = lax.broadcasted_iota(jnp.int32, shape, 0) - lax.rem(
+            lax.broadcasted_iota(jnp.int32, shape, 1), STRETCH
+        )
+        d_outs, deltas, logs = [], [], []
+        for pair in range(PAIRS):
+            both = d_heads_ref[rows, pair * 128 : (pair + 1) * 128]
+            d_out = jnp.concatenate([both[:, :HEAD_WIDTH], both[:, HEAD_WIDTH:]], axis=0)
+            kept = attended_ref[block, pair]
+            d_outs.append(d_out)
+            deltas.append(as_row(one_row, d_out.astype(F32) * kept[:, :HEAD_WIDTH]))
+            logs.append(as_row(pick, kept[:, HEAD_WIDTH:]))
+            d_query_ref[block, pair] = jnp.zeros((2 * STRETCH, HEAD_WIDTH), F32)
+
+        def step(place, carry):
+            slot = table_ref[block * longest + place]
+            tile = kv_ref[slot]
+            keys = [tile[:, :64], tile[:, 64:128]]
+            values = [tile[:, 128:192], tile[:, 192:256]]
+            middle_key = jnp.where(odd, keys[1], keys[0])
+            middle_value = jnp.where(odd, values[1], values[0])
+            visible = ahead <= offset - place * STRETCH
+            d_keys, d_values = [], []
+            for pair, key, value in (
+                (0, keys[0], values[0]),
+                (1, middle_key, middle_value),
+                (2, keys[1], values[1]),
+            ):
+                query, d_out = query_ref[block, pair], d_outs[pair]
+                scores = by_cols(key, query)
+                weights = jnp.exp2(scores * (LOG2E * scale) - logs[pair])
+                weights = jnp.where(visible, weights, 0.0)
+                d_weights = by_cols(value, d_out)
+                d_scores = (weights * (d_weights - deltas[pair])).astype(BF16)
+                d_values.append(product(weights.astype(BF16), d_out))
+                d_keys.append(product(d_scores, query))
+                d_query_ref[block, pair] += by_rows(d_scores, key) * scale
+            zero = jnp.zeros((STRETCH, HEAD_WIDTH), F32)
+            parts = [
+                (d_keys[0] + jnp.where(odd, zero, d_keys[1])) * scale,
+                (d_keys[2] + jnp.where(odd, d_keys[1], zero)) * scale,
+                d_values[0] + jnp.where(odd, zero, d_values[1]),
+                d_values[2] + jnp.where(odd, d_values[1], zero),
+            ]
+            d_kv_ref[block * longest + place] = jnp.concatenate(parts, axis=1)
+            return carry
+
+        lax.fori_loop(0, longest, step, 0)
+
+    attend_block(0)
+    add_x(3)
+    z_out[1] = sums_ref[3].astype(BF16)
+    z_copies = {1: links.send(z_out.at[1], z_in.at[1], kz=1)}
+    add_x(1)
+    z_out[0] = sums_ref[1].astype(BF16)
+    z_copies[0] = links.send(z_out.at[0], z_in.at[0], kz=1)
+    for move in Scatter.ORDER[:2]:
+        output_sum.add(move, output_block(move, here.y))
+    attend_block(1)
+    add_x(2)
+    z_copies[1].wait_recv()
+    z_out[2] = (sums_ref[2] + z_in[1].astype(F32)).astype(BF16)
+    z_copies[2] = links.send(z_out.at[2], z_in.at[2], kz=2)
+    add_x(0)
+    for move in Scatter.ORDER[2:]:
+        output_sum.add(move, output_block(move, here.y))
+    attend_block(2)
+
+    def kv_block(move, line):
+        pieces = []
+        for index in range(blocks):
+            slot = rank(move, line) * blocks + index
+            sequence = sequence_ref[slot]
+            place = offset_ref[slot] // STRETCH
+            total = jnp.zeros((STRETCH, kv_width), F32)
+            for block in range(blocks):
+                same = sequence_ref[rank(0, here.y) * blocks + block] == sequence
+                total += jnp.where(same, d_kv_ref[block * longest + place], 0.0)
+            pieces.append(total)
+        return jnp.concatenate(pieces, axis=0)
+
+    for move in Scatter.ORDER:
+        kv_sum.start(move, kv_block(move, 1 - here.y))
+
+    def group_back(group, at, grad):
+        linear = lin_ref[:, at]
+        inverse = lax.rsqrt(head_mean(linear * linear) + EPSILON)
+        unit = linear * inverse
+        grad = grad * cosine_ref[...] + halves_swapped(grad * sine_ref[...])
+        gain = jnp.sum(grad * unit, axis=0, keepdims=True)
+        scaled = grad * head_gain_ref[:, group * 128 : (group + 1) * 128]
+        return inverse * (scaled - unit * head_mean(scaled * unit)), gain
+
+    small_ref[...] = jnp.zeros_like(small_ref)
+    small_ref[1:2, :] = gain_ffn_ref[...]
+    for pair in range(PAIRS):
+        grad = jnp.concatenate(
+            [
+                jnp.concatenate(
+                    [d_query_ref[block, pair, :STRETCH], d_query_ref[block, pair, STRETCH:]], axis=1
+                )
+                for block in range(blocks)
+            ],
+            axis=0,
+        )
+        at = slice(kv_width + pair * 128, kv_width + (pair + 1) * 128)
+        linear_grad, gain = group_back(pair + 1, at, grad)
+        d_lin_ref[:, at] = linear_grad.astype(BF16)
+        small_ref[2:3, (pair + 1) * 128 : (pair + 2) * 128] = gain
+    for move in Scatter.ORDER:
+        kv_sum.add(move, kv_block(move, here.y))
+    d_kv = kv_sum.finish()
+    linear_grad, gain = group_back(0, slice(0, 128), d_kv[:, :128])
+    d_lin_ref[:, :128] = linear_grad.astype(BF16)
+    d_lin_ref[:, 128:kv_width] = d_kv[:, 128:].astype(BF16)
+    small_ref[2:3, :128] = gain
+
+    for move in Scatter.ORDER:
+        attend_sum.start(move, attend_grad(move, 1 - here.y))
+
+    partial_ref[0] = by_cols(d_lin_ref[...], w_attend_ref[...])
+    core_out[4] = partial_ref[0, other_half, :].astype(BF16)
+    core_copies[4] = links.send(core_out.at[4], core_in.at[4], kc=1)
+    add_cores(4, 0)
+    attend_sum.add(3, attend_grad(3, here.y))
+    attend_sum.add(1, attend_grad(1, here.y))
+    add_x(4)
+    states = states_ref[mine, :].astype(F32)
+    inverse = lax.rsqrt(jnp.mean(states * states, axis=-1, keepdims=True) + EPSILON)
+    unit = states * inverse
+    grad = sums_ref[4]
+    small_ref[0:1, :] = jnp.sum(grad * unit, axis=0, keepdims=True)
+    scaled = grad * gains_ref[0:1, :]
+    total = back_ref[...] + inverse * (
+        scaled - unit * jnp.mean(scaled * unit, axis=-1, keepdims=True)
+    )
+    states_grad_ref[mine, :] = total.astype(BF16)
+    block = states_grad_ref.at[mine]
+    states_x = links.send(block, block, kx=1)
+
+    def small_step(step, **move):
+        small_out[step] = small_ref[...]
+        return links.send(small_out.at[step], small_in.at[step], **move)
+
+    small = small_step(0, kc=1)
+    attend_sum.add(2, attend_grad(2, here.y))
+    z_copies[0].wait_recv()
+    z_copies[2].wait_recv()
+    result_ref[mine, :] = (
+        middle_ref[...] + sums_ref[0] + z_in[0].astype(F32) + z_in[2].astype(F32)
+    ).astype(BF16)
+    block = result_ref.at[mine]
+    result_x = links.send(block, block, kx=1)
+    small.wait_recv()
+    small_ref[...] += small_in[0]
+    small = small_step(1, kx=1)
+    states_x.wait_recv()
+    both = states_grad_ref.at[my_half]
+    states_core = links.send(both, both, kc=1)
+    small.wait_recv()
+    small_ref[...] += small_in[1]
+    small = small_step(2, ky=1)
+    attend_sum.add(0, attend_grad(0, here.y))
+    small.wait_recv()
+    small_ref[...] += small_in[2]
+    small = small_step(3, kz=1)
+    g_output_ref[...] = output_sum.finish()
+    result_x.wait_recv()
+    both = result_ref.at[my_half]
+    result_core = links.send(both, both, kc=1)
+    small.wait_recv()
+    small_ref[...] += small_in[3]
+    small = small_step(4, kz=2)
+
+    total = attend_sum.finish()
+    part = here.x * 2 + here.c
+    g_kv_ref[part] = total[:, :kv_width].astype(BF16)
+    block = g_kv_ref.at[part]
+    kv_x = links.send(block, block, kx=1)
+    kv_core = links.send(block, block, kc=1)
+    g_attend_ref[...] = total[:, kv_width:]
+    kv_x.wait_recv()
+    block = g_kv_ref.at[(1 - here.x) * 2 + here.c]
+    kv_both = links.send(block, block, kc=1)
+    small.wait_recv()
+    small_ref[...] += small_in[4]
+    for copy in (states_core, kv_core, kv_both, result_core):
+        copy.wait_recv()
+    links.finish()
+
+
+def backward(lines, heads, longest, *arguments):
+    kv, attn_in, lin, mixed = arguments[4], arguments[8], arguments[7], arguments[17]
+    token_rows, width = attn_in.shape
+    quarter = token_rows // 4
+    half = 2 * quarter
+    weight_rows = width // (4 * lines)
+    head_width = heads * HEAD_WIDTH
+    blocks = token_rows // STRETCH
+    vmem = pl.BlockSpec(memory_space=pltpu.VMEM)
+    smem = pl.BlockSpec(memory_space=pltpu.SMEM)
+    hbm = pl.BlockSpec(memory_space=pl.ANY)
+    shape = jax.ShapeDtypeStruct
+    return pl.pallas_call(
+        functools.partial(backward_kernel, lines, heads, longest),
+        out_shape=(
+            shape((token_rows, width), BF16),
+            shape((token_rows, width), BF16),
+            shape((weight_rows, head_width), F32),
+            shape((weight_rows, head_width), F32),
+            shape((4, weight_rows, 4 * HEAD_WIDTH), BF16),
+            shape((8, width), F32),
+        ),
+        in_specs=[smem] * 3 + [vmem] * 18 + [hbm],
+        out_specs=(vmem,) * 6,
+        scratch_shapes=[
+            pltpu.VMEM((mixed.shape[0], width), BF16),
+            pltpu.VMEM((blocks, PAIRS, 2 * STRETCH, HEAD_WIDTH), F32),
+            pltpu.VMEM((blocks * longest, STRETCH, 4 * HEAD_WIDTH), F32),
+            pltpu.VMEM(lin.shape, BF16),
+            pltpu.VMEM((2, token_rows, width), F32),
+            pltpu.VMEM((5, half, width), BF16),
+            pltpu.VMEM((5, half, width), BF16),
+            pltpu.VMEM((5, quarter, width), BF16),
+            pltpu.VMEM((5, quarter, width), BF16),
+            pltpu.VMEM((5, quarter, width), F32),
+            pltpu.VMEM((3, quarter, width), BF16),
+            pltpu.VMEM((3, quarter, width), BF16),
+            pltpu.VMEM((5, 8, width), F32),
+            pltpu.VMEM((5, 8, width), F32),
+            pltpu.SemaphoreType.DMA((1,)),
+            pltpu.SemaphoreType.DMA((BACKWARD_COPIES,)),
+            pltpu.SemaphoreType.DMA((BACKWARD_COPIES,)),
+            *scatter_scratch((token_rows, 4 * HEAD_WIDTH)),
+            *scatter_scratch((weight_rows, head_width)),
+            *scatter_scratch((weight_rows, lin.shape[1])),
+        ],
+        compiler_params=pltpu.CompilerParams(
+            collective_id=1, has_side_effects=True, vmem_limit_bytes=64 << 20
+        ),
+        name="backward",
+    )(*arguments)
+
+
+def local_kernels(
+    states,
+    query_weight,
+    keyvalue_matrix,
+    output_weight,
+    gate_weight,
+    up_weight,
+    down_weight,
+    norm_gains,
+    query_gain,
+    key_gain,
+    slot_sequence,
+    slot_offset,
+    out_grad,
+):
+    token_rows, width = states.shape
+    dp_ranks = lax.axis_size("dp")
+    tensor_ranks = lax.axis_size("tensor")
+    lines = dp_ranks // PLANES
+    rank, part = lax.axis_index("dp"), lax.axis_index("tensor")
+    heads_here = QUERY_HEADS // tensor_ranks
+    head_width = heads_here * HEAD_WIDTH
+    sharing_count = QUERY_HEADS // KEYVALUE_HEADS
+    blocks_here = token_rows // STRETCH
+    slot_count = slot_sequence.shape[0]
+    hidden = gate_weight.shape[2]
+    slice_width = hidden // PLANES
+    weight_rows = width // dp_ranks
+
+    offset_here = lax.dynamic_slice_in_dim(slot_offset, rank * blocks_here, blocks_here)
+    positions = (offset_here[:, None] + jnp.arange(STRETCH, dtype=jnp.int32)[None, :]).reshape(-1)
+    columns = jnp.arange(2 * HEAD_WIDTH, dtype=jnp.int32)
+    exponent = -(columns % (HEAD_WIDTH // 2)).astype(F32) * 2.0 / HEAD_WIDTH
+    phase = positions.astype(F32)[:, None] * (10000.0**exponent)[None, :]
+    cosine = jnp.cos(phase)
+    sine = jnp.sin(phase) * jnp.where(columns % HEAD_WIDTH < HEAD_WIDTH // 2, -1.0, 1.0)[None, :]
+    head_gain = jnp.concatenate([jnp.tile(key_gain[0], 2), jnp.tile(query_gain[0], heads_here)])
+
+    first_key = (part * heads_here) // sharing_count * HEAD_WIDTH
+    value_start = KEYVALUE_HEADS * HEAD_WIDTH
+    w_attend = jnp.concatenate(
+        [
+            lax.dynamic_slice_in_dim(keyvalue_matrix[0], first_key, 2 * HEAD_WIDTH, 1),
+            lax.dynamic_slice_in_dim(
+                keyvalue_matrix[0], value_start + first_key, 2 * HEAD_WIDTH, 1
+            ),
+            query_weight[0],
+        ],
+        axis=1,
+    )
+    gains = jnp.pad(norm_gains[0].T.astype(F32), ((0, 6), (0, 0)))
+
+    def turned(weight):
+        return weight[0].reshape(weight_rows, PLANES, slice_width).transpose(1, 2, 0)
+
+    packed = jnp.concatenate(
+        [turned(gate_weight), turned(up_weight), turned(down_weight)], axis=1
+    )
+    (
+        lin,
+        attn_in,
+        queries,
+        keyvalues,
+        attended,
+        attn_out,
+        gains,
+        w_attend,
+        middle_rows,
+        back,
+        gain_ffn,
+        d_heads,
+        output_grad,
+        mixed,
+        collected,
+        table,
+        w_down,
+    ) = forward(
+        lines,
+        heads_here,
+        slice_width,
+        LONGEST,
+        slot_sequence,
+        slot_offset,
+        states,
+        gains,
+        w_attend,
+        cosine,
+        sine,
+        head_gain[None],
+        output_weight[0],
+        packed,
+        out_grad,
+    )
+    result, states_grad, g_attend, g_output, g_kv, small = backward(
+        lines,
+        heads_here,
+        LONGEST,
+        slot_sequence,
+        slot_offset,
+        table,
+        queries,
+        keyvalues,
+        attended,
+        d_heads,
+        lin,
+        attn_in,
+        output_grad,
+        attn_out,
+        w_attend,
+        back,
+        gains,
+        gain_ffn,
+        states,
+        middle_rows,
+        mixed,
+        cosine,
+        sine,
+        head_gain[None],
+        w_down,
+    )
+
+    def hidden_grad(index):
+        piece = collected[:, index * slice_width : (index + 1) * slice_width]
+        return piece.transpose(2, 0, 1).astype(F32).reshape(1, weight_rows, hidden)
+
+    d_keyvalue_matrix = jnp.zeros((weight_rows, 2 * value_start), F32)
+    for other in range(tensor_ranks):
+        start = (other * heads_here) // sharing_count * HEAD_WIDTH
+        block = g_kv[other].astype(F32)
+        for offset, piece in (
+            (start, block[:, : 2 * HEAD_WIDTH]),
+            (value_start + start, block[:, 2 * HEAD_WIDTH :]),
+        ):
+            after = 2 * value_start - offset - 2 * HEAD_WIDTH
+            d_keyvalue_matrix += jnp.pad(piece, ((0, 0), (offset, after)))
+    head_gains = small[2, : head_width + 2 * HEAD_WIDTH].reshape(-1, HEAD_WIDTH)
+    d_gains = lax.dynamic_slice_in_dim(small[:2], rank * weight_rows, weight_rows, 1).T
+    return (
+        result,
+        states_grad.astype(F32),
+        g_attend[None],
+        d_keyvalue_matrix[None],
+        g_output[None],
+        hidden_grad(0),
+        hidden_grad(1),
+        hidden_grad(2),
+        d_gains[None],
+        jnp.sum(head_gains[2:], axis=0)[None],
+        jnp.sum(head_gains[:2], axis=0)[None],
+    )
+
+
+def local_permutes(
     states,
     query_weight,
     keyvalue_matrix,
@@ -513,6 +1724,14 @@
         small[2 * width : 2 * width + HEAD_WIDTH][None],
         small[2 * width + HEAD_WIDTH :][None],
     )
+
+
+def local(*arguments):
+    rows = arguments[0].shape[1] // lax.axis_size("dp")
+    slots = arguments[10].shape[0]
+    if lax.axis_size("dp") == 8 and lax.axis_size("tensor") == 4 and rows == 256 and slots == 24:
+        return local_kernels(*arguments)
+    return local_permutes(*arguments)
 
 
 def solution(mesh):

time: 869 us -> 482 us (0.55)
  Pallas kernels: 39.6 us -> 449 us
  waiting for transfers between devices: 333 us -> 0 us
  local copies, waits for them, and re-layouts: 154 us -> 9.76 us
  starting transfers between devices: 132 us -> 0 us
  matrix products: 85.1 us -> 0 us
  other arithmetic: 58.1 us -> 15 us
  blocking collectives: 37.1 us -> 0 us
  between operations: 16.9 us -> 1.21 us
    pallas_call x2, Pallas kernels: 39.6 us -> 449 us  [the longest x1 298 us: forward(): pl.pallas_call(functools.partial(forward_kernel, lines, heads, slice_widt...]
    ppermute x117 -> x0, waiting for transfers between devices: 332 us -> none  [send(): return lax.ppermute(value, ('dp', 'tensor'), pairs)]
    ppermute x117 -> x0, starting transfers between devices: 132 us -> none  [send(): return lax.ppermute(value, ('dp', 'tensor'), pairs)]
    dot_general x24 -> x0, matrix products: 85.1 us -> none  [the longest x10 31.1 us: by_cols(): lax.dot_general(left_side, right_side, (((1,), (1,)), ((), ())), preferre...]
    unnamed x266 -> x17, local copies, waits for them, and re-layouts: 46.6 us -> 3.3 us
    psum x1 -> x0, blocking collectives: 37.1 us -> none  [local(): small = lax.psum(small, ('dp', 'tensor'))]
    dynamic_slice x15 -> x2, local copies, waits for them, and re-layouts: 38.2 us -> 1.9 us  [the longest x1 1.07 us: local_kernels(): lax.dynamic_slice_in_dim(keyvalue_matrix[0], first_key, 2 * HEAD_WIDTH, 1)]
    dynamic_update_slice x49 -> x0, local copies, waits for them, and re-layouts: 32.1 us -> none  [the longest x8 12.9 us: local(): lax.dynamic_update_index_in_dim(w_hidden, got, rank ^ kz * lines + ky, 0)]
  transfers between devices with their start and end apart: 118 -> 0, of which waited for: 53 -> 0; matrix products, arithmetic and copies ran while one was open for 34% -> 0% of each run, Pallas kernels for 5% -> 0%
where the time goes in v4:
time: 482 us; the launch traced here: 475 us
  Pallas kernels  449 us (93%)
  other arithmetic  15 us (3%)
  local copies, waits for them, and re-layouts  9.76 us (2%)
    pallas_call x1, Pallas kernels, forward(): pl.pallas_call(functools.partial(forward_kernel, lines, heads, slice_widt...  298 us
    pallas_call x1, Pallas kernels, backward(): pl.pallas_call(functools.partial(backward_kernel, lines, heads, longest),...  151 us

profile of v4, /device:TPU:0, one launch (start us, length us, event | category | flops | bytes accessed | tf_op | source)
XLA Modules:
  0.0 475.1 jit_solution(3286227151040542066)
XLA Ops:
  0.7 0.8 dynamic_slice.20
  1.5 0.7 tile.21
  2.3 0.7 tile.24
  3.1 0.6 pad_maximum_fusion.2
  3.7 1.3 pad_convert_fusion.gains_in
  4.9 1.1 dynamic-slice_bitcast_fusion.1
  6.0 1.7 pad_maximum_fusion.1.w_attend_in
  7.7 1.5 fusion
  9.2 2.4 pad_maximum_fusion.w_hidden_in
  11.7 297.8 %forward.1 = (f32[384,640]{1,0:T(8,128)}, bf16[384,2048]{1,0:T(8,128)(2,1)}, bf16[3,3,256,64]{3,2,1,0:T(8,128)(2,1)}, bf16[24,128,256]{2,1,0:T(8,128)(2,1)}, f32...) custom-call(s32[24]{0:T(128)} %sequence_ref.3, ...), custom_call_target="tpu_custom_call" | custom-call | tf_op jit(solution)/shard_map/forward/pallas_call | solution.py:817
  309.5 151.3 %backward.1 = (bf16[384,2048]{1,0:T(8,128)(2,1)}, bf16[384,2048]{1,0:T(8,128)(2,1)}, f32[256,384]{1,0:T(8,128)}, f32[256,384]{1,0:T(8,128)}, bf16[4,256,256]{2,1,0:T(8,128)(2,1)}, /*index=5*/f32[8,2048]{1,0:T(8,128)}) custom-call(s32[24]{0:T(128)} %sequence_ref.3, s32[24]{0:T(128)} %offset_ref.3, s32[36]{0:T(128)} %get-tuple-element.34.table_ref, ...), custom_call_target="tpu_custom_call" | custom-call | tf_op jit(solution)/shard_map/backward/pallas_call | solution.py:1221
  460.8 0.7 slice_reduce_fusion.1
  461.6 0.5 reduce_sum.19
  462.1 0.7 slice_reduce_fusion
  462.8 0.8 slice.78
  463.7 0.6 dynamic-slice_bitcast_fusion.2
  464.3 0.5 reduce_sum.18
  464.9 1.2 bitcast_convert_fusion.3
  466.2 1.2 add_bitcast_fusion
  467.6 2.0 convert_element_type.86
  469.7 2.0 slice_convert_fusion
  472.0 1.1 copy.27
  473.2 0.7 copy.28
  473.9 0.7 copy.29
  (24 shorter events, 1.1 us)
Async XLA Ops:
  0.6 8.6 %copy-start.3 = (bf16[1,256,1216]{1,2,0:T(8,128)(2,1)S(1)}, bf16[1,256,1216]{1,2,0:T(8,128)(2,1)}, u32[]{:S(2)}) copy-start(bf16[1,256,1216]{1,2,0:T(8,128)(2,1)} %param.19) | copy-start | bytes 1867780
  0.7 8.6 %copy-start.4 = (bf16[1,256,1216]{1,2,0:T(8,128)(2,1)S(1)}, bf16[1,256,1216]{1,2,0:T(8,128)(2,1)}, u32[]{:S(2)}) copy-start(bf16[1,256,1216]{1,2,0:T(8,128)(2,1)} %param.18) | copy-start | bytes 1867780
  466.1 1.5 copy-start.2
  467.6 2.0 copy-start
  469.7 2.3 copy-start.1
  472.0 1.2 copy-start.6
  472.0 2.0 copy-start.5
